TPU v7x, 32 devices: a whole 2x2x4 slice. The times are simulated.
32 devices in a mesh: tile: 16 (over z, x, core), lev: 2 (over y).
Axes of the slice: x: 2, y: 2, z: 4, core: 2. Of those that a mesh axis runs over, the one named last changes fastest.
Arguments:
- gradient: float32 [144, 2, 256, 640], P('lev', None, 'tile'), may hold values from -6 to 6
- land_sea: int32 [144, 256, 640], P('lev', 'tile'), may hold values 0 or 1
- roughness: float32 [144, 256, 640], P('lev', 'tile'), may hold values from 0.5 to 1.4
- scale_index: int32 [10, 144], replicated, may hold values from 0 to 7
- scale_table: float32 [8], replicated, may hold values from 0.03 to 0.12
- balance: float32 [144, 144], replicated, may hold values from -0.5 to 0.5
- corr_a: float32 [144, 144], replicated, may hold values from -0.5 to 0.5
- corr_b: float32 [144, 144], replicated, may hold values from -0.5 to 0.5
Outputs:
- control_grad: float32 [144, 2, 256, 640], P('lev', None, 'tile')
All inputs are finite; a program needn't handle non-finite values. No bound on the sum of `land_sea` on one device may be relied on, other than what follows from the above.
Results may differ from a plain program's by a relative error of at most 0.000098.
Values sent between devices are 32-bit elements; how exact they have to be, the bound alone decides.
No kernel may reach another device: no remote copies, remote signals or barrier semaphores. Data moves between devices by JAX's collectives and lax.ppermute only.
A program may use at most 128 MiB of HBM per device.

v0:
```python
import functools

import jax
import jax.numpy as jnp
import numpy as np
from jax import lax
from jax.experimental import pallas as pl
from jax.experimental.pallas import tpu as pltpu
from jax.sharding import PartitionSpec as P

PASSES = 10
NSCALE = 8
ROWS = 8
LANES = 128
PAIR = 2
EXACT = lax.Precision.HIGHEST
VMEM_LIMIT = 50 * 1024 * 1024


def chunk_units(total):
    return [2] * (total // 2) + [1] * (total % 2)


def lane_tile(j):
    return slice(j * LANES, (j + 1) * LANES)


def dot_t(a, b):
    return lax.dot_general(
        a, b, (((1,), (1,)), ((), ())), precision=EXACT, preferred_element_type=jnp.float32
    )


def halve(value):
    high = value.astype(jnp.bfloat16)
    return high, (value - high.astype(jnp.float32)).astype(jnp.bfloat16)


def pick_levels(rows, levels, padded, own, starts):
    row = lax.broadcasted_iota(jnp.int32, (rows, levels), 0)
    col = lax.broadcasted_iota(jnp.int32, (rows, levels), 1)
    picked = jnp.zeros((rows, levels), jnp.bool_)
    for s, start in enumerate(starts):
        if start is not None:
            at = row - s * padded
            picked = picked | ((at >= 0) & (at < own) & (col == at + start))
    return picked.astype(jnp.float32)


def three_parts(full, third):
    high, low = halve(full)
    part = lax.broadcasted_iota(jnp.int32, full.shape, 1)
    return jnp.where(part < 2 * third, high.astype(jnp.float32), low.astype(jnp.float32)).astype(jnp.bfloat16)


def dot_exact(a, b):
    return jnp.dot(a, b, precision=EXACT, preferred_element_type=jnp.float32)


def dot_half(a, b):
    return jnp.dot(a, b, preferred_element_type=jnp.float32)


def ordered_parts(lines, plain, order, halves):
    rows, lats = lines.shape[1:]
    for side in range(PAIR):
        high, low = halve(lines[side])
        plain[2 * side * rows : (2 * side + 1) * rows, :] = high
        plain[(2 * side + 1) * rows : (2 * side + 2) * rows, :] = low
    ordered = dot_half(plain[...], order[...])
    for side in range(PAIR):
        place = slice(side * lats, (side + 1) * lats)
        both = ordered[2 * side * rows : 2 * (side + 1) * rows].astype(jnp.bfloat16)
        halves[0 : 2 * rows, place] = both
        halves[2 * rows : 3 * rows, place] = both[0:rows]


def plane(lons, lon, var):
    side, at = divmod(lon, lons // 2)
    group, place = divmod(at, PAIR)
    if side == 0:
        return 3 * PAIR * group + place if var == 0 else None
    return 3 * PAIR * group + PAIR + 2 * place + var


def mix_kernel(shape, offsets, at, *refs):
    levels, own, padded, lons, tiles, targets = shape
    grads, (bal, cor_a, cor_b, order, _), refs = refs[:tiles], refs[tiles : tiles + 5], refs[tiles + 5 :]
    outs, (weight, weight_raw, lines, plain, halves) = refs[:-5], refs[-5:]
    lats = tiles * LANES
    step = pl.program_id(0)

    @pl.when(step == 0)
    def _():
        first = [at[0], None] * 3
        second = [None, at[0]] * 3
        take_first = pick_levels(6 * padded, levels, padded, own, first)
        take_second = pick_levels(6 * padded, levels, padded, own, second)
        pick = pick_levels(targets * padded, levels, padded, own, [at[t] for t in range(targets)])
        cols_a = dot_t(pick, cor_a[...])
        through_a = dot_t(cols_a, take_first + dot_exact(take_second, bal[...]))
        through_b = dot_t(dot_t(pick, cor_b[...]), take_second)
        only_first = dot_t(cols_a, take_first)
        weight[...] = three_parts(jnp.concatenate([through_a, through_b], 0), 2 * padded)
        weight_raw[...] = three_parts(
            jnp.concatenate([through_a[:padded], only_first[padded:], through_b[:padded]], 0), 2 * padded
        )
        lines[...] = jnp.zeros_like(lines)

    for half in range(2):
        for side in range(PAIR):
            lon = half * (lons // 2) + step * PAIR + side
            for var in range(2):
                for j, grad in enumerate(grads):
                    lines[half, side, pl.ds(var * padded, own), lane_tile(j)] = grad[
                        pl.ds(var * lons + lon, own, stride=2 * lons), :
                    ]
        ordered_parts(lines.at[half], plain.at[half], order, halves.at[half])
    for half in range(2):
        mixed = dot_half((weight_raw if half == 0 else weight)[...], halves[half])
        for side in range(PAIR):
            place = slice(side * lats, (side + 1) * lats)
            for target in range(targets):
                for var in range(2):
                    if half == 0 and target > 0 and var == 1:
                        continue
                    first = (var * targets + target) * padded
                    for c, (start, size) in enumerate(offsets):
                        out = outs[target * len(offsets) + c]
                        value = mixed[first + start : first + start + size, place]
                        if target == 0:
                            out[half, side, var] = value
                        else:
                            out[plane(lons, half * (lons // 2) + side, var)] = value


def raw_kernel(shape, offsets, at, *refs):
    levels, own, padded, lons, tiles, targets = shape
    chunks = len(offsets)
    raws, refs = refs[: tiles * (targets - 1)], refs[tiles * (targets - 1) :]
    (bal, cor_a, cor_b, order), kept, outs = refs[:4], refs[4 : 4 + chunks], refs[4 + chunks : 4 + 2 * chunks]
    weight, lines, plain, halves = refs[4 + 2 * chunks :]
    lats = tiles * LANES
    step = pl.program_id(0)

    @pl.when(step == 0)
    def _():
        pick = pick_levels(padded, levels, padded, own, [at[0]])
        cols_a = dot_t(pick, cor_a[...])
        cols_b = dot_t(pick, cor_b[...])
        for source in range(1, targets):
            take = pick_levels(3 * padded, levels, padded, own, [at[source]] * 3)
            full = jnp.concatenate([dot_t(cols_a, dot_exact(take, bal[...])), dot_t(cols_b, take)], 0)
            weight[source - 1] = three_parts(full, padded)
        lines[...] = jnp.zeros_like(lines)

    total = None
    for source in range(targets - 1):
        for side in range(PAIR):
            for j in range(tiles):
                lines[side, 0:own, lane_tile(j)] = raws[source * tiles + j][
                    pl.ds(step * PAIR + side, own, stride=lons // 2), :
                ]
        ordered_parts(lines, plain, order, halves)
        mixed = dot_half(weight[source], halves[...])
        total = mixed if total is None else total + mixed
    for side in range(PAIR):
        place = slice(side * lats, (side + 1) * lats)
        for var in range(2):
            for (start, size), more, out in zip(offsets, kept, outs):
                first = var * padded + start
                out[0, side, var] = more[0, side, var] + total[first : first + size, place]


def coef_kernel(own, padded, lons, halo, tiles, *refs):
    seas, roughs, (order, _, coef, first, last, lines) = refs[:tiles], refs[tiles : 2 * tiles], refs[2 * tiles :]
    half = lons // 2
    lines[...] = jnp.zeros_like(lines)
    for group in range(2):
        for at in range(half):
            rows = pl.ds(group * half + at, own, stride=lons)
            for j in range(tiles):
                lines[at * padded : at * padded + own, lane_tile(j)] = (
                    seas[j][rows, :].astype(jnp.float32) * roughs[j][rows, :]
                )
        high, low = halve(lines[...])
        value = jnp.dot(high, order[...], preferred_element_type=jnp.float32) + jnp.dot(
            low, order[...], preferred_element_type=jnp.float32
        )
        for at in range(half):
            lon = group * half + at
            piece = value[at * padded : (at + 1) * padded]
            coef[lon] = piece
            if lon < halo:
                first[lon] = piece
            if lon >= lons - halo:
                last[lon - (lons - halo)] = piece


def mixed_at(lons, sums, lon, var):
    value = sums[0][lon // (lons // 2), lon % (lons // 2), var]
    at = plane(lons, lon, var)
    if at is not None:
        for more in sums[1:]:
            value = value + more[at]
    return value


def edge_kernel(lons, halo, parts, passed, *refs):
    sums, coef, (first, last, token) = refs[:parts], refs[parts], refs[parts + 4 + passed : parts + 7 + passed]
    token[...] = jnp.zeros_like(token)
    for lon in range(lons):
        for var in range(2):
            value = coef[lon] * mixed_at(lons, sums, lon, var)
            if lon < halo:
                first[lon, var] = value
            if lon >= lons - halo:
                last[lon - (lons - halo), var] = value


def neighbours(tiles, lane):
    count = len(tiles)
    before = jnp.where(lane == 0, tiles[0], pltpu.roll(tiles[-1], 1, 1))
    after = jnp.where(lane == LANES - 1, tiles[-1], pltpu.roll(tiles[0], LANES - 1, 1))
    line = [before, *tiles, after]
    return [line[j] + line[j + 2] for j in range(count)]


def diffuse(lons, lats, sums, coef, before, after, coef_before, coef_after, rates, weighted, square):
    halo = PASSES
    tiles = lats // LANES
    lane = lax.broadcasted_iota(jnp.int32, (ROWS, LANES), 1)

    for lon in range(lons):
        scale = coef[lon]
        square[halo + lon] = scale * scale
        for var in range(2):
            weighted[0][halo + lon, var] = scale * mixed_at(lons, sums, lon, var)
    for lon in range(halo):
        weighted[0][lon] = before[lon]
        weighted[0][halo + lons + lon] = after[lon]
    for lon in range(halo - 1):
        square[1 + lon] = coef_before[lon] * coef_before[lon]
        square[halo + lons + lon] = coef_after[lon] * coef_after[lon]

    for section in range(PASSES):
        source, target = weighted[section % 2], weighted[(section + 1) % 2]
        rate = rates[section]
        count = (lons + 2 * halo - 2 * section - 2) // 2

        def load(lon):
            return [[source[lon, var, :, lane_tile(j)] for j in range(tiles)] for var in range(2)]

        def part(at, carry):
            start = section + 1 + at * count
            behind, here = load(start - 1), load(start)
            for lon in range(count):
                ahead = load(start + lon + 1)
                factor = [rate * square[start + lon, :, lane_tile(j)] for j in range(tiles)]
                for var in range(2):
                    lat = neighbours(here[var], lane)
                    for j in range(tiles):
                        spread = (behind[var][j] + ahead[var][j]) + lat[j] - 4.0 * here[var][j]
                        target[start + lon, var, :, lane_tile(j)] = here[var][j] + factor[j] * spread
                behind, here = here, ahead
            return carry

        lax.fori_loop(0, 2, part, 0)


def diffuse_kernel(lons, lats, parts, *refs):
    sums, rest = refs[:parts], refs[parts:]
    coef, before, after, coef_before, coef_after, rates, back, _, _, out, token, *rest = rest
    *weighted, square, lines = rest
    tiles = lats // LANES
    token[...] = jnp.zeros_like(token)
    diffuse(lons, lats, sums, coef, before, after, coef_before, coef_after, rates, weighted, square)

    count = ROWS * 2 * lons
    for lon in range(lons):
        scale = coef[lon]
        land = scale == 0.0
        inverse = 1.0 / jnp.where(land, 1.0, scale)
        for var in range(2):
            plain = mixed_at(lons, sums, lon, var)
            value = jnp.where(land, plain, weighted[PASSES % 2][PASSES + lon, var] * inverse)
            for j in range(tiles):
                lines[pl.ds(j * count + var * lons + lon, ROWS, stride=2 * lons), :] = value[:, lane_tile(j)]
    high, low = halve(jnp.concatenate([lines[j * count : (j + 1) * count, :] for j in range(tiles)], 1))
    out[...] = jnp.dot(high, back[...], preferred_element_type=jnp.float32) + jnp.dot(
        low, back[...], preferred_element_type=jnp.float32
    )


def whole(*block):
    return pl.BlockSpec(block, lambda i: (0,) * len(block))


def params():
    return pltpu.CompilerParams(vmem_limit_bytes=VMEM_LIMIT)


def spent(microseconds):
    return pl.CostEstimate(flops=int(microseconds * 1.153e9), bytes_accessed=1024, transcendentals=0)


def on_device(gradient, land_sea, roughness, scale_index, scale_table, balance, corr_a, corr_b):
    own, _, lons, lats = gradient.shape
    levels = balance.shape[0]
    lev_count = lax.axis_size("lev")
    tile_count = lax.axis_size("tile")
    me = lax.axis_index("lev")
    units = -(-own // ROWS)
    padded = units * ROWS
    chunks = chunk_units(units)
    starts = [sum(chunks[:c]) for c in range(len(chunks))]
    offsets = [(s * ROWS, c * ROWS) for s, c in zip(starts, chunks)]
    halo = PASSES
    unit_bytes = lons * 2 * ROWS * lats * 4
    f32 = jnp.float32

    def along(shift):
        return [(i, (i + shift) % lev_count) for i in range(lev_count)]

    with jax.named_scope("raw"):
        rows = gradient[:, 1, : lons // 2]
        raws = [lax.ppermute(rows, "lev", along(shift)) for shift in range(1, lev_count)]

    tiles = lats // LANES
    place = np.arange(lats)
    order = np.zeros((lats, lats), np.float32)
    order[place, (place % tiles) * LANES + place // tiles] = 1.0
    back = jnp.asarray(order.T, jnp.bfloat16)
    order = jnp.asarray(order, jnp.bfloat16)

    up = [(i, (i + 1) % tile_count) for i in range(tile_count)]
    down = [(j, i) for i, j in up]
    with jax.named_scope("coef"):
        coef, first, last = pl.pallas_call(
            functools.partial(coef_kernel, own, padded, lons, halo - 1, tiles),
            grid=(1,),
            out_shape=[
                jax.ShapeDtypeStruct((lons, padded, lats), f32),
                jax.ShapeDtypeStruct((halo - 1, padded, lats), f32),
                jax.ShapeDtypeStruct((halo - 1, padded, lats), f32),
            ],
            in_specs=[pl.BlockSpec((own * lons, LANES), lambda i, j=j: (0, j)) for j in range(tiles)] * 2
            + [whole(lats, lats), pl.BlockSpec(memory_space=pl.ANY)],
            out_specs=[
                whole(lons, padded, lats),
                whole(halo - 1, padded, lats),
                whole(halo - 1, padded, lats),
            ],
            scratch_shapes=[pltpu.VMEM((lons // 2 * padded, lats), f32)],
            compiler_params=params(),
            cost_estimate=spent(10),
            name="coef",
        )(
            *[land_sea.reshape(own * lons, lats)] * tiles,
            *[roughness.reshape(own * lons, lats)] * tiles,
            order,
            rows,
        )
        coef_before = lax.ppermute(last, "tile", up)
        coef_after = lax.ppermute(first, "tile", down)

    half = lons // 2
    shape = (levels, own, padded, lons, tiles, lev_count)
    kept_shapes = [jax.ShapeDtypeStruct((2, half, 2, size, lats), f32) for _, size in offsets]
    sent_shapes = [jax.ShapeDtypeStruct((3 * half, size, lats), f32) for _, size in offsets]
    kept_specs = [pl.BlockSpec((2, PAIR, 2, size, lats), lambda i: (0, i, 0, 0, 0)) for _, size in offsets]
    sent_specs = [pl.BlockSpec((3 * PAIR, size, lats), lambda i: (i, 0, 0)) for _, size in offsets]
    level_starts = [lax.rem(me + shift, lev_count) * own for shift in range(lev_count)]
    with jax.named_scope("mix"):
        mixed = pl.pallas_call(
            functools.partial(mix_kernel, shape, offsets),
            grid=(half // PAIR,),
            out_shape=kept_shapes + sent_shapes * (lev_count - 1),
            in_specs=[pl.BlockSpec(memory_space=pltpu.SMEM)]
            + [pl.BlockSpec((own * 2 * lons, LANES), lambda i, j=j: (0, j)) for j in range(tiles)]
            + [whole(levels, levels)] * 3
            + [whole(lats, lats), pl.BlockSpec(memory_space=pl.ANY)],
            out_specs=kept_specs + sent_specs * (lev_count - 1),
            scratch_shapes=[
                pltpu.VMEM((2 * lev_count * padded, 6 * padded), jnp.bfloat16),
                pltpu.VMEM(((lev_count + 1) * padded, 6 * padded), jnp.bfloat16),
                pltpu.VMEM((2, PAIR, 2 * padded, lats), f32),
                pltpu.VMEM((2, PAIR * 4 * padded, lats), jnp.bfloat16),
                pltpu.VMEM((2, 6 * padded, PAIR * lats), jnp.bfloat16),
            ],
            compiler_params=params(),
            cost_estimate=spent(20),
            name="mix",
        )(
            jnp.stack(level_starts),
            *[gradient.reshape(own * 2 * lons, lats)] * tiles,
            balance,
            corr_a,
            corr_b,
            order,
            first,
        )
        sent = [mixed[c + len(chunks) :: len(chunks)] for c in range(len(chunks))]

        def send(arrays):
            return [lax.ppermute(array, "lev", along(shift + 1)) for shift, array in enumerate(arrays)]

        final = len(chunks) - 1
        received = [send(arrays) if c < final or final < 2 else None for c, arrays in enumerate(sent)]
        kept = pl.pallas_call(
            functools.partial(raw_kernel, shape, offsets),
            grid=(half // PAIR,),
            out_shape=kept_shapes,
            in_specs=[pl.BlockSpec(memory_space=pltpu.SMEM)]
            + [pl.BlockSpec((own * half, LANES), lambda i, j=j: (0, j)) for j in range(tiles)] * (lev_count - 1)
            + [whole(levels, levels)] * 3
            + [whole(lats, lats)]
            + [pl.BlockSpec((1, PAIR, 2, size, lats), lambda i: (0, i, 0, 0, 0)) for _, size in offsets],
            out_specs=[pl.BlockSpec((1, PAIR, 2, size, lats), lambda i: (0, i, 0, 0, 0)) for _, size in offsets],
            scratch_shapes=[
                pltpu.VMEM((lev_count - 1, 2 * padded, 3 * padded), jnp.bfloat16),
                pltpu.VMEM((PAIR, padded, lats), f32),
                pltpu.VMEM((PAIR * 2 * padded, lats), jnp.bfloat16),
                pltpu.VMEM((3 * padded, PAIR * lats), jnp.bfloat16),
            ],
            input_output_aliases={5 + tiles * (lev_count - 1) + c: c for c in range(len(chunks))},
            compiler_params=params(),
            cost_estimate=spent(6),
            name="raw",
        )(
            jnp.stack([level_starts[(lev_count - shift) % lev_count] for shift in range(lev_count)]),
            *[part for raw in raws for part in [raw.reshape(own * half, lats)] * tiles],
            balance,
            corr_a,
            corr_b,
            order,
            *mixed[: len(chunks)],
        )

    with jax.named_scope("rates"):
        own_index = lax.dynamic_slice_in_dim(scale_index, me * own, own, 1)
        picks = own_index[:, :, None] == jnp.arange(NSCALE, dtype=jnp.int32)[None, None, :]
        rates = jnp.sum(picks.astype(f32) * scale_table[None, None, :], -1)
        rates = jnp.pad(rates, ((0, 0), (0, padded - own)))
        rates = jnp.broadcast_to(rates[:, :, None], (PASSES, padded, LANES))

    token_shape = jax.ShapeDtypeStruct((ROWS, LANES), f32)
    token_spec = pl.BlockSpec((ROWS, LANES), lambda i: (0, 0))
    hidden = pl.BlockSpec(memory_space=pl.ANY)
    result = jnp.zeros((ROWS, LANES), f32)
    token = result

    def sum_specs(parts):
        own_sum = pl.BlockSpec((2, half, 2, ROWS, lats), lambda i: (0, 0, 0, i, 0))
        return [own_sum] + [pl.BlockSpec((3 * half, ROWS, lats), lambda i: (0, i, 0))] * (parts - 1)

    def edges(c, token, passed):
        sums = [kept[c]] + received[c]
        count, start = chunks[c], starts[c]
        halo_shape = jax.ShapeDtypeStruct((halo, 2, count * ROWS, lats), f32)
        fixed = [jax.ShapeDtypeStruct(array.shape, array.dtype) for array in passed]
        with jax.named_scope("edges"):
            first, last, token, *passed = pl.pallas_call(
                functools.partial(edge_kernel, lons, halo, len(sums), len(passed)),
                grid=(count,),
                out_shape=[halo_shape, halo_shape, token_shape, *fixed],
                in_specs=sum_specs(len(sums))
                + [pl.BlockSpec((lons, ROWS, lats), lambda i: (0, start + i, 0))]
                + [hidden] * (3 + len(passed)),
                out_specs=[pl.BlockSpec((halo, 2, ROWS, lats), lambda i: (0, 0, i, 0))] * 2
                + [token_spec]
                + [hidden] * len(passed),
                input_output_aliases={len(sums) + 4 + i: 3 + i for i in range(len(passed))},
                compiler_params=params(),
                cost_estimate=spent(2),
                name="edges",
            )(*sums, coef, coef_before, coef_after, token, *passed)
            return lax.ppermute(last, "tile", up), lax.ppermute(first, "tile", down), token, passed

    def diffusion(c, before, after, result, token):
        sums = [kept[c]] + received[c]
        count, start = chunks[c], starts[c]
        fixed = lambda i: (0, 0, i, 0)
        level = lambda i: (0, start + i, 0)
        operands = [*sums, coef, before, after, coef_before, coef_after, rates, back, token, result]
        with jax.named_scope("diffusion"):
            return pl.pallas_call(
                functools.partial(diffuse_kernel, lons, lats, len(sums)),
                grid=(count,),
                out_shape=[jax.ShapeDtypeStruct((own * 2 * lons, lats), f32), token_shape],
                in_specs=sum_specs(len(sums))
                + [pl.BlockSpec((lons, ROWS, lats), level)]
                + [pl.BlockSpec((halo, 2, ROWS, lats), fixed)] * 2
                + [pl.BlockSpec((halo - 1, ROWS, lats), level)] * 2
                + [pl.BlockSpec((PASSES, ROWS, LANES), level), whole(lats, lats), hidden, hidden],
                out_specs=[pl.BlockSpec((ROWS * 2 * lons, lats), lambda i: (start + i, 0)), token_spec],
                scratch_shapes=[
                    pltpu.VMEM((lons + 2 * halo, 2, ROWS, lats), f32),
                    pltpu.VMEM((lons + 2 * halo, 2, ROWS, lats), f32),
                    pltpu.VMEM((lons + 2 * halo, ROWS, lats), f32),
                    pltpu.VMEM((tiles * ROWS * 2 * lons, LANES), f32),
                ],
                input_output_aliases={} if c == 0 else {len(operands) - 1: 0},
                compiler_params=params(),
                cost_estimate=spent(11),
                name="diffusion",
            )(*operands)

    waiting = None
    for c in range(len(chunks)):
        before, after, token, passed = edges(c, token, sent[final] if c == final - 2 else [])
        if c == final - 2:
            received[final] = send(passed)
        if waiting is not None:
            result, token = diffusion(c - 1, *waiting, result, token)
        waiting = (before, after)
    result, _ = diffusion(len(chunks) - 1, *waiting, result, token)
    return result.reshape(own, 2, lons, lats)


def solution(mesh):
    return jax.shard_map(
        on_device,
        mesh=mesh,
        in_specs=(
            P("lev", None, "tile", None),
            P("lev", "tile", None),
            P("lev", "tile", None),
            P(),
            P(),
            P(),
            P(),
            P(),
        ),
        out_specs=P("lev", None, "tile", None),
        check_vma=False,
    )
```

profile of v0, /device:TPU:25, one launch (start us, length us, event | category | flops | bytes accessed | tf_op | source)
XLA Modules:
  0.0 170.3 jit_solution(3363056543601747599)
XLA Ops:
  0.0 1.5 slice_bitcast_fusion.refs_11_
  1.6 1.3 collective-permute-start
  2.9 10.1 %coef.1 = (f32[16,72,640]{2,1,0:T(8,128)}, f32[9,72,640]{2,1,0:T(8,128)}, f32[9,72,640]{2,1,0:T(8,128)}) custom-call(s32[1152,640]{1,0:T(8,128)} %bitcast.16, s32[1152,640]{1,0:T(8,128)} %bitcast.17, s32[1152,640]{1,0:T(8,128)} %bitcast.18, s32[1152,640]{1,0:T(8,128)} %bitcast.19, s32[1152,640]{1,0:T(8,128)} %bitcast.20, f32[1152,640]{1,0:T(8,128)} %bitcast.21, ...), custom_call_target="tpu_custom_call" | custom-call | flops 11530000384 | bytes 1024 | tf_op jit(solution)/shard_map/coef/coef/pallas_call | solution.py:339
  13.0 2.0 %collective-permute-start.2 = (f32[9,72,640]{2,1,0:T(8,128)}, f32[9,72,640]{2,1,0:T(8,128)S(1)}, u32[]{:S(2)}, u32[]{:S(2)}) collective-permute-start(f32[9,72,640]{2,1,0:T(8,128)} %get-tuple-element.58), channel_id=1, source_target_pairs={{0,2},{2,4},{4,6},{6,8},{8,10},{10,12},{12,14},{14,16},{16,18},{18... | collective-permute-start | bytes 4976648 | tf_op jit(solution)/shard_map/coef/ppermute | solution.py:364
  17.2 18.7 %mix.1 = (f32[2,8,2,16,640]{4,3,2,1,0:T(8,128)}, f32[2,8,2,16,640]{4,3,2,1,0:T(8,128)}, f32[2,8,2,16,640]{4,3,2,1,0:T(8,128)}, f32[2,8,2,16,640]{4,3,2,1,0:T(8,1...) custom-call(s32[2]{0:T(128)S(1)} %pad_add_fusion.at, ...), custom_call_target="tpu_custom_call" | custom-call | flops 23060000768 | bytes 1024 | tf_op jit(solution)/shard_map/mix/mix/pallas_call | solution.py:375
  36.9 1.2 collective-permute-start.7
  38.2 1.3 copy-done.3
  39.5 7.2 %raw.1 = (f32[2,8,2,16,640]{4,3,2,1,0:T(8,128)S(1)}, f32[2,8,2,16,640]{4,3,2,1,0:T(8,128)}, f32[2,8,2,16,640]{4,3,2,1,0:T(8,128)}, f32[2,8,2,16,640]{4,3,2,1,0:T(8,128)}, f32[2,8,2,8,640]{4,3,2,1,0:T(8,128)S(1)}) custom-call(s32[2]{0:T(128)S(1)} %pad_add_fusion.at, ...), custom_call_target="tpu_custom_call", output_to_operand_aliasing={{0}: (10, {}), {1}: (11, {}), {2}: (12, {}), {3}: (13, {}),... | custom-call | flops 6918000128 | bytes 1024 | tf_op jit(solution)/shard_map/mix/raw/pallas_call | solution.py:410
  48.6 9.8 %collective-permute-done.4.refs_1_ = f32[24,16,640]{2,1,0:T(8,128)S(1)} collective-permute-done((f32[24,16,640]{2,1,0:T(8,128)S(1)}, f32[24,16,640]{2,1,0:T(8,128)S(1)}, u32[]{:S(2)}, u32[]{:S(2)}) %collective-permute-start.4) | collective-permute-done | bytes 983072 | tf_op jit(solution)/shard_map/mix/ppermute | solution.py:406
  58.4 1.2 copy-done.1
  59.6 1.3 copy-done.5
  60.9 2.4 %edges.5 = (f32[10,2,16,640]{3,2,1,0:T(8,128)}, f32[10,2,16,640]{3,2,1,0:T(8,128)}, f32[8,128]{1,0:T(8,128)S(1)}) custom-call(f32[2,8,2,16,640]{4,3,2,1,0:T(8,128)S(1)} %copy-done.5, f32[24,16,640]{2,1,0:T(8,128)S(1)} %collective-permute-done.4.refs_1_, f32[16,72,640]{2,1,0:T(8,128)} %get-tuple-element.57.refs_2_, f32[9,72,640]{2,1,0:T(8,128)} %copy-done.1, ...), custom_call_target="tpu_custom_call" | custom-call | flops 2305999872 | bytes 1024 | tf_op jit(solution)/shard_map/edges/edges/pallas_call | solution.py:463
  64.3 4.7 %collective-permute-start.5 = (f32[10,2,16,640]{3,2,1,0:T(8,128)}, f32[10,2,16,640]{3,2,1,0:T(8,128)}, u32[]{:S(2)}, u32[]{:S(2)}) collective-permute-start(f32[10,2,16,640]{3,2,1,0:T(8,128)} %get-tuple-element.61), channel_id=1, source_target_pairs={{0,2},{2,4},{4,6},{6,8},{8,10},{10,12},{12,14},{14,16},{16,18},{18... | collective-permute-start | bytes 2457608 | tf_op jit(solution)/shard_map/edges/ppermute | solution.py:478
  69.3 1.2 collective-permute-start.11
  70.7 8.9 %collective-permute-done.7.refs_1_ = f32[24,16,640]{2,1,0:T(8,128)} collective-permute-done((f32[24,16,640]{2,1,0:T(8,128)}, f32[24,16,640]{2,1,0:T(8,128)}, u32[]{:S(2)}, u32[]{:S(2)}) %collective-permute-start.7) | collective-permute-done | bytes 983072 | tf_op jit(solution)/shard_map/mix/ppermute | solution.py:406
  79.6 1.7 %edges.6 = (f32[10,2,16,640]{3,2,1,0:T(8,128)S(1)}, f32[10,2,16,640]{3,2,1,0:T(8,128)S(1)}, f32[8,128]{1,0:T(8,128)S(1)}) custom-call(f32[2,8,2,16,640]{4,3,2,1,0:T(8,128)S(1)} %copy-done.6, f32[24,16,640]{2,1,0:T(8,128)} %collective-permute-done.7.refs_1_, f32[16,72,640]{2,1,0:T(8,128)} %get-tuple-element.57.refs_2_, f32[9,72,640]{2,1,0:T(8,128)} %copy-done.1, ...), custom_call_target="tpu_custom_call" | custom-call | flops 2305999872 | bytes 1024 | tf_op jit(solution)/shard_map/edges/edges/pallas_call | solution.py:463
  81.3 4.8 %collective-permute-start.12 = (f32[10,2,16,640]{3,2,1,0:T(8,128)S(1)}, f32[10,2,16,640]{3,2,1,0:T(8,128)S(1)}, u32[]{:S(2)}, u32[]{:S(2)}) collective-permute-start(f32[10,2,16,640]{3,2,1,0:T(8,128)S(1)} %get-tuple-element.74), channel_id=1, source_target_pairs={{0,2},{2,4},{4,6},{6,8},{8,10},{10,12},{12,14},{14,16},{16,18},{18... | collective-permute-start | bytes 2457608 | tf_op jit(solution)/shard_map/edges/ppermute | solution.py:478
  86.1 1.3 collective-permute-done.5.refs_3_
  87.4 11.5 %collective-permute-done.6.refs_4_ = f32[10,2,16,640]{3,2,1,0:T(8,128)} collective-permute-done((f32[10,2,16,640]{3,2,1,0:T(8,128)}, f32[10,2,16,640]{3,2,1,0:T(8,128)}, u32[]{:S(2)}, u32[]{:S(2)}) %collective-permute-start.6) | collective-permute-done | bytes 819232 | tf_op jit(solution)/shard_map/edges/ppermute | solution.py:478
  99.1 11.4 %diffusion.5 = (f32[2304,640]{1,0:T(8,128)}, f32[8,128]{1,0:T(8,128)S(1)}) custom-call(f32[2,8,2,16,640]{4,3,2,1,0:T(8,128)} %copy-done.4, f32[24,16,640]{2,1,0:T(8,128)S(1)} %copy-done.9, f32[16,72,640]{2,1,0:T(8,128)} %get-tuple-element.57.refs_2_, f32[10,2,16,640]{3,2,1,0:T(8,128)} %collective-permute-done.5.refs_3_, ...), custom_call_target="tpu_custom_call" | custom-call | flops 12682999808 | bytes 1024 | tf_op jit(solution)/shard_map/diffusion/diffusion/pallas_call | solution.py:487
  110.6 1.9 %edges.7 = (f32[10,2,16,640]{3,2,1,0:T(8,128)S(1)}, f32[10,2,16,640]{3,2,1,0:T(8,128)S(1)}, f32[8,128]{1,0:T(8,128)S(1)}, f32[24,8,640]{2,1,0:T(8,128)S(1)}) custom-call(f32[2,8,2,16,640]{4,3,2,1,0:T(8,128)} %get-tuple-element.55.refs_0_, f32[24,16,640]{2,1,0:T(8,128)} %collective-permute-done.1.refs_1_, ...), custom_call_target="tpu_custom_call", output_to_operand_aliasing={{3}: (6, {})} | custom-call | flops 2305999872 | bytes 1024 | tf_op jit(solution)/shard_map/edges/edges/pallas_call | solution.py:463
  113.3 11.4 %diffusion.6 = (f32[2304,640]{1,0:T(8,128)}, f32[8,128]{1,0:T(8,128)S(1)}) custom-call(f32[2,8,2,16,640]{4,3,2,1,0:T(8,128)} %get-tuple-element.63.refs_0_, f32[24,16,640]{2,1,0:T(8,128)} %collective-permute-done.7.refs_1_, f32[16,72,640]{2,1,0:T(8,128)} %get-tuple-element.57.refs_2_, ...), custom_call_target="tpu_custom_call", output_to_operand_aliasing={{0}: (10, {})} | custom-call | flops 12682999808 | bytes 1024 | tf_op jit(solution)/shard_map/diffusion/diffusion/pallas_call | solution.py:487
  124.7 1.4 edges.8
  126.1 1.6 collective-permute-start.16
  127.8 3.1 %collective-permute-done.9.refs_3_ = f32[10,2,16,640]{3,2,1,0:T(8,128)S(1)} collective-permute-done((f32[10,2,16,640]{3,2,1,0:T(8,128)S(1)}, f32[10,2,16,640]{3,2,1,0:T(8,128)S(1)}, u32[]{:S(2)}, u32[]{:S(2)}) %collective-permute-start.9) | collective-permute-done | bytes 819232 | tf_op jit(solution)/shard_map/edges/ppermute | solution.py:478
  130.9 11.4 %diffusion.7 = (f32[2304,640]{1,0:T(8,128)}, f32[8,128]{1,0:T(8,128)S(1)}) custom-call(f32[2,8,2,16,640]{4,3,2,1,0:T(8,128)} %get-tuple-element.55.refs_0_, f32[24,16,640]{2,1,0:T(8,128)} %collective-permute-done.1.refs_1_, f32[16,72,640]{2,1,0:T(8,128)} %get-tuple-element.57.refs_2_, ...), custom_call_target="tpu_custom_call", output_to_operand_aliasing={{0}: (10, {})} | custom-call | flops 12682999808 | bytes 1024 | tf_op jit(solution)/shard_map/diffusion/diffusion/pallas_call | solution.py:487
  142.4 1.2 edges.9
  143.5 2.5 %collective-permute-start.14 = (f32[10,2,8,640]{3,2,1,0:T(8,128)S(1)}, f32[10,2,8,640]{3,2,1,0:T(8,128)S(1)}, u32[]{:S(2)}, u32[]{:S(2)}) collective-permute-start(f32[10,2,8,640]{3,2,1,0:T(8,128)S(1)} %get-tuple-element.82), channel_id=1, source_target_pairs={{0,2},{2,4},{4,6},{6,8},{8,10},{10,12},{12,14},{14,16},{16,18},{18... | collective-permute-start | bytes 1228808 | tf_op jit(solution)/shard_map/edges/ppermute | solution.py:478
  146.1 2.4 %collective-permute-done.16.refs_3_ = f32[10,2,16,640]{3,2,1,0:T(8,128)S(1)} collective-permute-done((f32[10,2,16,640]{3,2,1,0:T(8,128)S(1)}, f32[10,2,16,640]{3,2,1,0:T(8,128)S(1)}, u32[]{:S(2)}, u32[]{:S(2)}) %collective-permute-start.16) | collective-permute-done | bytes 819232 | tf_op jit(solution)/shard_map/edges/ppermute | solution.py:478
  148.4 4.2 %collective-permute-done.17.refs_4_ = f32[10,2,16,640]{3,2,1,0:T(8,128)S(1)} collective-permute-done((f32[10,2,16,640]{3,2,1,0:T(8,128)S(1)}, f32[10,2,16,640]{3,2,1,0:T(8,128)S(1)}, u32[]{:S(2)}, u32[]{:S(2)}) %collective-permute-start.17) | collective-permute-done | bytes 819232 | tf_op jit(solution)/shard_map/edges/ppermute | solution.py:478
  152.7 11.1 %diffusion.8 = (f32[2304,640]{1,0:T(8,128)}, f32[8,128]{1,0:T(8,128)S(1)}) custom-call(f32[2,8,2,16,640]{4,3,2,1,0:T(8,128)} %get-tuple-element.72.refs_0_, f32[24,16,640]{2,1,0:T(8,128)S(1)} %collective-permute-done.11.refs_1_, f32[16,72,640]{2,1,0:T(8,128)} %get-tuple-element.57.refs_2_, ...), custom_call_target="tpu_custom_call", output_to_operand_aliasing={{0}: (10, {})} | custom-call | flops 12682999808 | bytes 1024 | tf_op jit(solution)/shard_map/diffusion/diffusion/pallas_call | solution.py:487
  163.8 6.5 %diffusion.9 = (f32[2304,640]{1,0:T(8,128)}, f32[8,128]{1,0:T(8,128)}) custom-call(f32[2,8,2,8,640]{4,3,2,1,0:T(8,128)S(1)} %copy-done.20, f32[24,8,640]{2,1,0:T(8,128)S(1)} %collective-permute-done.8.refs_1_, f32[16,72,640]{2,1,0:T(8,128)} %get-tuple-element.57.refs_2_, ...), custom_call_target="tpu_custom_call", output_to_operand_aliasing={{0}: (10, {})} | custom-call | flops 12682999808 | bytes 1024 | tf_op jit(solution)/shard_map/diffusion/diffusion/pallas_call | solution.py:487
  (67 shorter events, 7.5 us)
Async XLA Ops:
  0.0 70.5 %copy-start = (s32[10,144]{1,0:T(8,128)S(1)}, s32[10,144]{1,0:T(8,128)}, u32[]{:S(2)}) copy-start(s32[10,144]{1,0:T(8,128)} %param.13) | copy-start | bytes 17284
  0.0 2.9 %copy-start.17 = (bf16[640,640]{1,0:T(8,128)(2,1)S(1)}, bf16[640,640]{1,0:T(8,128)(2,1)}, u32[]{:S(2)}) copy-start(bf16[640,640]{1,0:T(8,128)(2,1)} %constant.26.clone.refs_10_.refs_8_) | copy-start | bytes 2457604
  1.6 36.6 %collective-permute-start = (f32[72,8,640]{2,1,0:T(8,128)S(1)}, f32[72,8,640]{2,1,0:T(8,128)}, u32[]{:S(2)}, u32[]{:S(2)}) collective-permute-start(f32[72,8,640]{2,1,0:T(8,128)S(1)} %slice_bitcast_fusion.refs_11_), channel_id=1, source_target_pairs={{0,1},{1,0},{2,3},{3,2},{4,5},{5,4},{6,7},{7,6},{8,9},{9,8},{10,11... | collective-permute-start | bytes 4423688 | tf_op jit(solution)/shard_map/raw/ppermute | solution.py:327
  2.9 12.2 %copy-start.12 = (f32[144,144]{1,0:T(8,128)S(1)}, f32[144,144]{1,0:T(8,128)}, u32[]{:S(2)}) copy-start(f32[144,144]{1,0:T(8,128)} %refs_5_.3) | copy-start | bytes 248836
  2.9 12.2 %copy-start.13 = (f32[144,144]{1,0:T(8,128)S(1)}, f32[144,144]{1,0:T(8,128)}, u32[]{:S(2)}) copy-start(f32[144,144]{1,0:T(8,128)} %refs_6_.3) | copy-start | bytes 248836
  13.0 45.4 %collective-permute-start.2 = (f32[9,72,640]{2,1,0:T(8,128)}, f32[9,72,640]{2,1,0:T(8,128)S(1)}, u32[]{:S(2)}, u32[]{:S(2)}) collective-permute-start(f32[9,72,640]{2,1,0:T(8,128)} %get-tuple-element.58), channel_id=1, source_target_pairs={{0,2},{2,4},{4,6},{6,8},{8,10},{10,12},{12,14},{14,16},{16,18},{18... | collective-permute-start | bytes 4976648 | tf_op jit(solution)/shard_map/coef/ppermute | solution.py:364
  15.0 43.4 %collective-permute-start.3 = (f32[9,72,640]{2,1,0:T(8,128)}, f32[9,72,640]{2,1,0:T(8,128)}, u32[]{:S(2)}, u32[]{:S(2)}) collective-permute-start(f32[9,72,640]{2,1,0:T(8,128)} %get-tuple-element.48.refs_9_), channel_id=1, source_target_pairs={{2,0},{4,2},{6,4},{8,6},{10,8},{12,10},{14,12},{16,14},{18,16},{20... | collective-permute-start | bytes 4976648 | tf_op jit(solution)/shard_map/coef/ppermute | solution.py:365
  36.7 21.7 %collective-permute-start.4 = (f32[24,16,640]{2,1,0:T(8,128)S(1)}, f32[24,16,640]{2,1,0:T(8,128)S(1)}, u32[]{:S(2)}, u32[]{:S(2)}) collective-permute-start(f32[24,16,640]{2,1,0:T(8,128)S(1)} %get-tuple-element.60), channel_id=1, source_target_pairs={{0,1},{1,0},{2,3},{3,2},{4,5},{5,4},{6,7},{7,6},{8,9},{9,8},{10,11... | collective-permute-start | bytes 2949128 | tf_op jit(solution)/shard_map/mix/ppermute | solution.py:406
  36.9 42.6 %collective-permute-start.7 = (f32[24,16,640]{2,1,0:T(8,128)}, f32[24,16,640]{2,1,0:T(8,128)}, u32[]{:S(2)}, u32[]{:S(2)}) collective-permute-start(f32[24,16,640]{2,1,0:T(8,128)} %get-tuple-element.64), channel_id=1, source_target_pairs={{0,1},{1,0},{2,3},{3,2},{4,5},{5,4},{6,7},{7,6},{8,9},{9,8},{10,11... | collective-permute-start | bytes 2949128 | tf_op jit(solution)/shard_map/mix/ppermute | solution.py:406
  38.2 1.3 copy-start.3
  60.9 9.6 %copy-start.21 = (f32[8]{0:T(128)S(1)}, f32[8]{0:T(128)}, u32[]{:S(2)}) copy-start(f32[8]{0:T(128)} %param.14) | copy-start | bytes 100
  60.9 18.6 %copy-start.6 = (f32[2,8,2,16,640]{4,3,2,1,0:T(8,128)S(1)}, f32[2,8,2,16,640]{4,3,2,1,0:T(8,128)}, u32[]{:S(2)}) copy-start(f32[2,8,2,16,640]{4,3,2,1,0:T(8,128)} %get-tuple-element.63.refs_0_) | copy-start | bytes 3932164
  64.3 23.1 %collective-permute-start.5 = (f32[10,2,16,640]{3,2,1,0:T(8,128)}, f32[10,2,16,640]{3,2,1,0:T(8,128)}, u32[]{:S(2)}, u32[]{:S(2)}) collective-permute-start(f32[10,2,16,640]{3,2,1,0:T(8,128)} %get-tuple-element.61), channel_id=1, source_target_pairs={{0,2},{2,4},{4,6},{6,8},{8,10},{10,12},{12,14},{14,16},{16,18},{18... | collective-permute-start | bytes 2457608 | tf_op jit(solution)/shard_map/edges/ppermute | solution.py:478
  69.0 29.9 %collective-permute-start.6 = (f32[10,2,16,640]{3,2,1,0:T(8,128)}, f32[10,2,16,640]{3,2,1,0:T(8,128)}, u32[]{:S(2)}, u32[]{:S(2)}) collective-permute-start(f32[10,2,16,640]{3,2,1,0:T(8,128)} %get-tuple-element.62), channel_id=1, source_target_pairs={{2,0},{4,2},{6,4},{8,6},{10,8},{12,10},{14,12},{16,14},{18,16},{20... | collective-permute-start | bytes 2457608 | tf_op jit(solution)/shard_map/edges/ppermute | solution.py:478
  69.0 41.5 %collective-permute-start.1 = (f32[24,16,640]{2,1,0:T(8,128)}, f32[24,16,640]{2,1,0:T(8,128)}, u32[]{:S(2)}, u32[]{:S(2)}) collective-permute-start(f32[24,16,640]{2,1,0:T(8,128)} %get-tuple-element.56), channel_id=1, source_target_pairs={{0,1},{1,0},{2,3},{3,2},{4,5},{5,4},{6,7},{7,6},{8,9},{9,8},{10,11... | collective-permute-start | bytes 2949128 | tf_op jit(solution)/shard_map/mix/ppermute | solution.py:406
  69.3 55.5 %collective-permute-start.11 = (f32[24,16,640]{2,1,0:T(8,128)}, f32[24,16,640]{2,1,0:T(8,128)S(1)}, u32[]{:S(2)}, u32[]{:S(2)}) collective-permute-start(f32[24,16,640]{2,1,0:T(8,128)} %get-tuple-element.73), channel_id=1, source_target_pairs={{0,1},{1,0},{2,3},{3,2},{4,5},{5,4},{6,7},{7,6},{8,9},{9,8},{10,11... | collective-permute-start | bytes 2949128 | tf_op jit(solution)/shard_map/mix/ppermute | solution.py:406
  79.6 19.5 %copy-start.9 = (f32[24,16,640]{2,1,0:T(8,128)S(1)}, f32[24,16,640]{2,1,0:T(8,128)}, u32[]{:S(2)}) copy-start(f32[24,16,640]{2,1,0:T(8,128)} %copy-done.8) | copy-start | bytes 2949124
  79.6 19.5 %copy-start.15 = (bf16[640,640]{1,0:T(8,128)(2,1)S(1)}, bf16[640,640]{1,0:T(8,128)(2,1)}, u32[]{:S(2)}) copy-start(bf16[640,640]{1,0:T(8,128)(2,1)} %constant.25.clone.refs_8_) | copy-start | bytes 2457604
  81.3 31.5 %collective-permute-start.12 = (f32[10,2,16,640]{3,2,1,0:T(8,128)S(1)}, f32[10,2,16,640]{3,2,1,0:T(8,128)S(1)}, u32[]{:S(2)}, u32[]{:S(2)}) collective-permute-start(f32[10,2,16,640]{3,2,1,0:T(8,128)S(1)} %get-tuple-element.74), channel_id=1, source_target_pairs={{0,2},{2,4},{4,6},{6,8},{8,10},{10,12},{12,14},{14,16},{16,18},{18... | collective-permute-start | bytes 2457608 | tf_op jit(solution)/shard_map/edges/ppermute | solution.py:478
  87.4 25.9 %collective-permute-start.13 = (f32[10,2,16,640]{3,2,1,0:T(8,128)S(1)}, f32[10,2,16,640]{3,2,1,0:T(8,128)S(1)}, u32[]{:S(2)}, u32[]{:S(2)}) collective-permute-start(f32[10,2,16,640]{3,2,1,0:T(8,128)S(1)} %get-tuple-element.75), channel_id=1, source_target_pairs={{2,0},{4,2},{6,4},{8,6},{10,8},{12,10},{14,12},{16,14},{18,16},{20... | collective-permute-start | bytes 2457608 | tf_op jit(solution)/shard_map/edges/ppermute | solution.py:478
  99.1 11.4 %copy-start.11 = (f32[24,8,640]{2,1,0:T(8,128)S(1)}, f32[24,8,640]{2,1,0:T(8,128)}, u32[]{:S(2)}) copy-start(f32[24,8,640]{2,1,0:T(8,128)} %copy-done.10) | copy-start | bytes 1474564
  112.5 29.8 %collective-permute-start.8 = (f32[24,8,640]{2,1,0:T(8,128)S(1)}, f32[24,8,640]{2,1,0:T(8,128)S(1)}, u32[]{:S(2)}, u32[]{:S(2)}) collective-permute-start(f32[24,8,640]{2,1,0:T(8,128)S(1)} %get-tuple-element.69), channel_id=1, source_target_pairs={{0,1},{1,0},{2,3},{3,2},{4,5},{5,4},{6,7},{7,6},{8,9},{9,8},{10,11... | collective-permute-start | bytes 1474568 | tf_op jit(solution)/shard_map/ppermute | solution.py:406
  112.8 18.1 %collective-permute-start.9 = (f32[10,2,16,640]{3,2,1,0:T(8,128)S(1)}, f32[10,2,16,640]{3,2,1,0:T(8,128)S(1)}, u32[]{:S(2)}, u32[]{:S(2)}) collective-permute-start(f32[10,2,16,640]{3,2,1,0:T(8,128)S(1)} %get-tuple-element.70), channel_id=1, source_target_pairs={{0,2},{2,4},{4,6},{6,8},{8,10},{10,12},{12,14},{14,16},{16,18},{18... | collective-permute-start | bytes 2457608 | tf_op jit(solution)/shard_map/edges/ppermute | solution.py:478
  112.8 18.1 %collective-permute-start.10 = (f32[10,2,16,640]{3,2,1,0:T(8,128)S(1)}, f32[10,2,16,640]{3,2,1,0:T(8,128)S(1)}, u32[]{:S(2)}, u32[]{:S(2)}) collective-permute-start(f32[10,2,16,640]{3,2,1,0:T(8,128)S(1)} %get-tuple-element.71), channel_id=1, source_target_pairs={{2,0},{4,2},{6,4},{8,6},{10,8},{12,10},{14,12},{16,14},{18,16},{20... | collective-permute-start | bytes 2457608 | tf_op jit(solution)/shard_map/edges/ppermute | solution.py:478
  113.3 11.4 %copy-start.7 = (f32[2,8,2,16,640]{4,3,2,1,0:T(8,128)S(1)}, f32[2,8,2,16,640]{4,3,2,1,0:T(8,128)}, u32[]{:S(2)}) copy-start(f32[2,8,2,16,640]{4,3,2,1,0:T(8,128)} %get-tuple-element.72.refs_0_) | copy-start | bytes 3932164
  126.1 22.3 %collective-permute-start.16 = (f32[10,2,16,640]{3,2,1,0:T(8,128)S(1)}, f32[10,2,16,640]{3,2,1,0:T(8,128)S(1)}, u32[]{:S(2)}, u32[]{:S(2)}) collective-permute-start(f32[10,2,16,640]{3,2,1,0:T(8,128)S(1)} %get-tuple-element.84), channel_id=1, source_target_pairs={{0,2},{2,4},{4,6},{6,8},{8,10},{10,12},{12,14},{14,16},{16,18},{18... | collective-permute-start | bytes 2457608 | tf_op jit(solution)/shard_map/edges/ppermute | solution.py:478
  127.8 24.9 %collective-permute-start.17 = (f32[10,2,16,640]{3,2,1,0:T(8,128)S(1)}, f32[10,2,16,640]{3,2,1,0:T(8,128)S(1)}, u32[]{:S(2)}, u32[]{:S(2)}) collective-permute-start(f32[10,2,16,640]{3,2,1,0:T(8,128)S(1)} %get-tuple-element.85), channel_id=1, source_target_pairs={{2,0},{4,2},{6,4},{8,6},{10,8},{12,10},{14,12},{16,14},{18,16},{20... | collective-permute-start | bytes 2457608 | tf_op jit(solution)/shard_map/edges/ppermute | solution.py:478
  130.9 11.4 %copy-start.2 = (f32[9,72,640]{2,1,0:T(8,128)S(1)}, f32[9,72,640]{2,1,0:T(8,128)}, u32[]{:S(2)}) copy-start(f32[9,72,640]{2,1,0:T(8,128)} %copy-done.1) | copy-start | bytes 4976644
  130.9 11.4 %copy-start.20 = (f32[2,8,2,8,640]{4,3,2,1,0:T(8,128)S(1)}, f32[2,8,2,8,640]{4,3,2,1,0:T(8,128)}, u32[]{:S(2)}) copy-start(f32[2,8,2,8,640]{4,3,2,1,0:T(8,128)} %copy-done.19) | copy-start | bytes 1966084
  142.3 10.4 %copy-start.16 = (bf16[640,640]{1,0:T(8,128)(2,1)S(1)}, bf16[640,640]{1,0:T(8,128)(2,1)}, u32[]{:S(2)}) copy-start(bf16[640,640]{1,0:T(8,128)(2,1)} %constant.25.clone.refs_8_) | copy-start | bytes 2457604
  143.5 20.3 %collective-permute-start.14 = (f32[10,2,8,640]{3,2,1,0:T(8,128)S(1)}, f32[10,2,8,640]{3,2,1,0:T(8,128)S(1)}, u32[]{:S(2)}, u32[]{:S(2)}) collective-permute-start(f32[10,2,8,640]{3,2,1,0:T(8,128)S(1)} %get-tuple-element.82), channel_id=1, source_target_pairs={{0,2},{2,4},{4,6},{6,8},{8,10},{10,12},{12,14},{14,16},{16,18},{18... | collective-permute-start | bytes 1228808 | tf_op jit(solution)/shard_map/edges/ppermute | solution.py:478
  146.1 17.8 %collective-permute-start.15 = (f32[10,2,8,640]{3,2,1,0:T(8,128)S(1)}, f32[10,2,8,640]{3,2,1,0:T(8,128)S(1)}, u32[]{:S(2)}, u32[]{:S(2)}) collective-permute-start(f32[10,2,8,640]{3,2,1,0:T(8,128)S(1)} %get-tuple-element.83), channel_id=1, source_target_pairs={{2,0},{4,2},{6,4},{8,6},{10,8},{12,10},{14,12},{16,14},{18,16},{20... | collective-permute-start | bytes 1228808 | tf_op jit(solution)/shard_map/edges/ppermute | solution.py:478
  (8 other events, 8.3 us)
where the time goes:
time: 172 us; the launch traced here: 170 us
  Pallas kernels  96.5 us (56%)
  waiting for transfers between devices  41.3 us (24%)
  starting transfers between devices  20.8 us (12%)
  local copies, waits for them, and re-layouts  11.4 us (7%)
    pallas_call x5, Pallas kernels, diffusion(): pl.pallas_call(functools.partial(diffuse_kernel, lons, lats, len(sums)),...  51.8 us
    pallas_call x1, Pallas kernels, on_device(): pl.pallas_call(functools.partial(mix_kernel, shape, offsets), grid=(half...  18.7 us
    ppermute x5, waiting for transfers between devices, send(): lax.ppermute(array, 'lev', along(shift + 1))  18.7 us
    ppermute x5, waiting for transfers between devices, edges(): lax.ppermute(first, 'tile', down)  15.8 us
    ppermute x5, starting transfers between devices, edges(): lax.ppermute(last, 'tile', up)  13.7 us
    pallas_call x1, Pallas kernels, on_device(): pl.pallas_call(functools.partial(coef_kernel, own, padded, lons, halo - 1...  10.1 us
    unnamed x44, local copies, waits for them, and re-layouts  9.61 us
    pallas_call x5, Pallas kernels, edges(): pl.pallas_call(functools.partial(edge_kernel, lons, halo, len(sums), len(...  8.61 us
  transfers between devices with their start and end apart: 18, of which 7 were waited for; matrix products, arithmetic and copies ran while one was open for 0% of the time, Pallas kernels for 53%

commit v1 on v0

--- a/solution.py
+++ b/solution.py
@@ -12,9 +12,10 @@
 NSCALE = 8
 ROWS = 8
 LANES = 128
+COEF_GROUPS = 4
 PAIR = 2
 EXACT = lax.Precision.HIGHEST
-VMEM_LIMIT = 50 * 1024 * 1024
+VMEM_LIMIT = 65200 * 1024
 
 
 def chunk_units(total):
@@ -85,13 +86,18 @@
 
 def mix_kernel(shape, offsets, at, *refs):
     levels, own, padded, lons, tiles, targets = shape
-    grads, (bal, cor_a, cor_b, order, _), refs = refs[:tiles], refs[tiles : tiles + 5], refs[tiles + 5 :]
-    outs, (weight, weight_raw, lines, plain, halves) = refs[:-5], refs[-5:]
+    (gradient, bal, cor_a, cor_b, order), refs = refs[:5], refs[5:]
+    outs, (weight, weight_raw, lines, plain, halves, grads, sems) = refs[:-7], refs[-7:]
     lats = tiles * LANES
     step = pl.program_id(0)
 
     @pl.when(step == 0)
     def _():
+        arriving = [
+            pltpu.make_async_copy(gradient.at[:, lane_tile(j)], grads.at[j], sems.at[j]) for j in range(tiles)
+        ]
+        for copy in arriving:
+            copy.start()
         first = [at[0], None] * 3
         second = [None, at[0]] * 3
         take_first = pick_levels(6 * padded, levels, padded, own, first)
@@ -106,14 +112,16 @@
             jnp.concatenate([through_a[:padded], only_first[padded:], through_b[:padded]], 0), 2 * padded
         )
         lines[...] = jnp.zeros_like(lines)
+        for copy in arriving:
+            copy.wait()
 
     for half in range(2):
         for side in range(PAIR):
             lon = half * (lons // 2) + step * PAIR + side
             for var in range(2):
-                for j, grad in enumerate(grads):
-                    lines[half, side, pl.ds(var * padded, own), lane_tile(j)] = grad[
-                        pl.ds(var * lons + lon, own, stride=2 * lons), :
+                for j in range(tiles):
+                    lines[half, side, pl.ds(var * padded, own), lane_tile(j)] = grads[
+                        j, pl.ds(var * lons + lon, own, stride=2 * lons), :
                     ]
         ordered_parts(lines.at[half], plain.at[half], order, halves.at[half])
     for half in range(2):
@@ -172,29 +180,45 @@
                 out[0, side, var] = more[0, side, var] + total[first : first + size, place]
 
 
-def coef_kernel(own, padded, lons, halo, tiles, *refs):
-    seas, roughs, (order, _, coef, first, last, lines) = refs[:tiles], refs[tiles : 2 * tiles], refs[2 * tiles :]
-    half = lons // 2
+def coef_kernel(own, padded, lons, halo, tiles, sea, rough, order, _, coef, first, last, seas, roughs, lines, values, sems):
+    arriving = []
+    for j in range(tiles):
+        for source, held in ((sea, seas), (rough, roughs)):
+            arriving.append(pltpu.make_async_copy(source.at[:, lane_tile(j)], held.at[j], sems.at[len(arriving)]))
+    for copy in arriving:
+        copy.start()
     lines[...] = jnp.zeros_like(lines)
-    for group in range(2):
-        for at in range(half):
-            rows = pl.ds(group * half + at, own, stride=lons)
+    for copy in arriving:
+        copy.wait()
+    size = lons // COEF_GROUPS
+    leaving = []
+
+    def leave(source, target):
+        copy = pltpu.make_async_copy(source, target, sems.at[len(arriving) + len(leaving)])
+        copy.start()
+        leaving.append(copy)
+
+    for group in range(COEF_GROUPS):
+        for at in range(size):
+            rows = pl.ds(group * size + at, own, stride=lons)
             for j in range(tiles):
                 lines[at * padded : at * padded + own, lane_tile(j)] = (
-                    seas[j][rows, :].astype(jnp.float32) * roughs[j][rows, :]
+                    seas[j, rows, :].astype(jnp.float32) * roughs[j, rows, :]
                 )
         high, low = halve(lines[...])
-        value = jnp.dot(high, order[...], preferred_element_type=jnp.float32) + jnp.dot(
-            low, order[...], preferred_element_type=jnp.float32
-        )
-        for at in range(half):
-            lon = group * half + at
-            piece = value[at * padded : (at + 1) * padded]
-            coef[lon] = piece
-            if lon < halo:
-                first[lon] = piece
-            if lon >= lons - halo:
-                last[lon - (lons - halo)] = piece
+        value = dot_half(high, order[...]) + dot_half(low, order[...])
+        for at in range(size):
+            values[group * size + at] = value[at * padded : (at + 1) * padded]
+        start, stop = group * size, (group + 1) * size
+        leave(values.at[start:stop], coef.at[start:stop])
+        if start < halo:
+            until = min(stop, halo)
+            leave(values.at[start:until], first.at[start:until])
+        if stop > lons - halo:
+            since = max(start, lons - halo)
+            leave(values.at[since:stop], last.at[since - (lons - halo) : stop - (lons - halo)])
+    for copy in leaving:
+        copy.wait()
 
 
 def mixed_at(lons, sums, lon, var):
@@ -246,26 +270,25 @@
     for section in range(PASSES):
         source, target = weighted[section % 2], weighted[(section + 1) % 2]
         rate = rates[section]
-        count = (lons + 2 * halo - 2 * section - 2) // 2
-
-        def load(lon):
-            return [[source[lon, var, :, lane_tile(j)] for j in range(tiles)] for var in range(2)]
-
-        def part(at, carry):
-            start = section + 1 + at * count
+        start = section + 1
+        stop = lons + 2 * halo - 1 - section
+
+        def one_variable(var, carry):
+            def load(lon):
+                return [source[lon, var, :, lane_tile(j)] for j in range(tiles)]
+
             behind, here = load(start - 1), load(start)
-            for lon in range(count):
-                ahead = load(start + lon + 1)
-                factor = [rate * square[start + lon, :, lane_tile(j)] for j in range(tiles)]
-                for var in range(2):
-                    lat = neighbours(here[var], lane)
-                    for j in range(tiles):
-                        spread = (behind[var][j] + ahead[var][j]) + lat[j] - 4.0 * here[var][j]
-                        target[start + lon, var, :, lane_tile(j)] = here[var][j] + factor[j] * spread
+            for lon in range(start, stop):
+                ahead = load(lon + 1)
+                lat = neighbours(here, lane)
+                for j in range(tiles):
+                    factor = rate * square[lon, :, lane_tile(j)]
+                    spread = (behind[j] + ahead[j]) + lat[j] - 4.0 * here[j]
+                    target[lon, var, :, lane_tile(j)] = here[j] + factor * spread
                 behind, here = here, ahead
             return carry
 
-        lax.fori_loop(0, 2, part, 0)
+        lax.fori_loop(0, 2, one_variable, 0)
 
 
 def diffuse_kernel(lons, lats, parts, *refs):
@@ -318,6 +341,7 @@
     halo = PASSES
     unit_bytes = lons * 2 * ROWS * lats * 4
     f32 = jnp.float32
+    hidden = pl.BlockSpec(memory_space=pl.ANY)
 
     def along(shift):
         return [(i, (i + shift) % lev_count) for i in range(lev_count)]
@@ -338,29 +362,24 @@
     with jax.named_scope("coef"):
         coef, first, last = pl.pallas_call(
             functools.partial(coef_kernel, own, padded, lons, halo - 1, tiles),
-            grid=(1,),
             out_shape=[
                 jax.ShapeDtypeStruct((lons, padded, lats), f32),
                 jax.ShapeDtypeStruct((halo - 1, padded, lats), f32),
                 jax.ShapeDtypeStruct((halo - 1, padded, lats), f32),
             ],
-            in_specs=[pl.BlockSpec((own * lons, LANES), lambda i, j=j: (0, j)) for j in range(tiles)] * 2
-            + [whole(lats, lats), pl.BlockSpec(memory_space=pl.ANY)],
-            out_specs=[
-                whole(lons, padded, lats),
-                whole(halo - 1, padded, lats),
-                whole(halo - 1, padded, lats),
+            in_specs=[hidden, hidden, pl.BlockSpec(memory_space=pltpu.VMEM), hidden],
+            out_specs=[hidden] * 3,
+            scratch_shapes=[
+                pltpu.VMEM((tiles, own * lons, LANES), jnp.int32),
+                pltpu.VMEM((tiles, own * lons, LANES), f32),
+                pltpu.VMEM((lons // COEF_GROUPS * padded, lats), f32),
+                pltpu.VMEM((lons, padded, lats), f32),
+                pltpu.SemaphoreType.DMA((2 * tiles + 3 * COEF_GROUPS,)),
             ],
-            scratch_shapes=[pltpu.VMEM((lons // 2 * padded, lats), f32)],
             compiler_params=params(),
             cost_estimate=spent(10),
             name="coef",
-        )(
-            *[land_sea.reshape(own * lons, lats)] * tiles,
-            *[roughness.reshape(own * lons, lats)] * tiles,
-            order,
-            rows,
-        )
+        )(land_sea.reshape(own * lons, lats), roughness.reshape(own * lons, lats), order, rows)
         coef_before = lax.ppermute(last, "tile", up)
         coef_after = lax.ppermute(first, "tile", down)
 
@@ -377,9 +396,9 @@
             grid=(half // PAIR,),
             out_shape=kept_shapes + sent_shapes * (lev_count - 1),
             in_specs=[pl.BlockSpec(memory_space=pltpu.SMEM)]
-            + [pl.BlockSpec((own * 2 * lons, LANES), lambda i, j=j: (0, j)) for j in range(tiles)]
+            + [hidden]
             + [whole(levels, levels)] * 3
-            + [whole(lats, lats), pl.BlockSpec(memory_space=pl.ANY)],
+            + [whole(lats, lats)],
             out_specs=kept_specs + sent_specs * (lev_count - 1),
             scratch_shapes=[
                 pltpu.VMEM((2 * lev_count * padded, 6 * padded), jnp.bfloat16),
@@ -387,18 +406,19 @@
                 pltpu.VMEM((2, PAIR, 2 * padded, lats), f32),
                 pltpu.VMEM((2, PAIR * 4 * padded, lats), jnp.bfloat16),
                 pltpu.VMEM((2, 6 * padded, PAIR * lats), jnp.bfloat16),
+                pltpu.VMEM((tiles, own * 2 * lons, LANES), f32),
+                pltpu.SemaphoreType.DMA((tiles,)),
             ],
             compiler_params=params(),
             cost_estimate=spent(20),
             name="mix",
         )(
             jnp.stack(level_starts),
-            *[gradient.reshape(own * 2 * lons, lats)] * tiles,
+            gradient.reshape(own * 2 * lons, lats),
             balance,
             corr_a,
             corr_b,
             order,
-            first,
         )
         sent = [mixed[c + len(chunks) :: len(chunks)] for c in range(len(chunks))]
 
@@ -407,6 +427,8 @@
 
         final = len(chunks) - 1
         received = [send(arrays) if c < final or final < 2 else None for c, arrays in enumerate(sent)]
+
+    with jax.named_scope("raw"):
         kept = pl.pallas_call(
             functools.partial(raw_kernel, shape, offsets),
             grid=(half // PAIR,),
@@ -446,7 +468,6 @@
 
     token_shape = jax.ShapeDtypeStruct((ROWS, LANES), f32)
     token_spec = pl.BlockSpec((ROWS, LANES), lambda i: (0, 0))
-    hidden = pl.BlockSpec(memory_space=pl.ANY)
     result = jnp.zeros((ROWS, LANES), f32)
     token = result
 

time: 172 us -> 174 us (1.012)
  the two profiles are of different devices: /device:TPU:25 before, /device:TPU:0 now
where the time goes in v1:
time: 174 us
  Pallas kernels  107 us (61%)
  starting transfers between devices  33.8 us (19%)
  waiting for transfers between devices  27.6 us (16%)
  local copies, waits for them, and re-layouts  4.15 us (2%)
    pallas_call x5, Pallas kernels, diffusion(): pl.pallas_call(functools.partial(diffuse_kernel, lons, lats, len(sums)),...  57.6 us
    ppermute x5, waiting for transfers between devices, send(): lax.ppermute(array, 'lev', along(shift + 1))  27.5 us
    ppermute x5, starting transfers between devices, edges(): lax.ppermute(first, 'tile', down)  22.2 us
    pallas_call x1, Pallas kernels, on_device(): pl.pallas_call(functools.partial(mix_kernel, shape, offsets), grid=(half...  18.2 us
    pallas_call x5, Pallas kernels, edges(): pl.pallas_call(functools.partial(edge_kernel, lons, halo, len(sums), len(...  13.5 us
    pallas_call x1, Pallas kernels, on_device(): pl.pallas_call(functools.partial(coef_kernel, own, padded, lons, halo - 1...  9.94 us
    pallas_call x1, Pallas kernels, on_device(): pl.pallas_call(functools.partial(raw_kernel, shape, offsets), grid=(half...  8.15 us
    ppermute x1, starting transfers between devices, on_device(): coef_after = lax.ppermute(first, 'tile', down)  4.43 us
  transfers between devices with their start and end apart: 18, of which 4 were waited for; matrix products, arithmetic and copies ran while one was open for 1% of the time, Pallas kernels for 57%

profile of v1, /device:TPU:0, one launch (start us, length us, event | category | flops | bytes accessed | tf_op | source)
XLA Modules:
  0.0 173.7 jit_solution(17288352327852777099)
XLA Ops:
  0.0 2.6 %slice_bitcast_fusion._ = f32[72,8,640]{2,1,0:T(8,128)} fusion(f32[72,2,16,640]{3,2,1,0:T(8,128)} %param.10), kind=kLoop, calls=%fused_computation | loop fusion | bytes 2949120 | tf_op jit(solution)/shard_map/raw/squeeze | solution.py:350
  2.6 3.0 %collective-permute-start = (f32[72,8,640]{2,1,0:T(8,128)}, f32[72,8,640]{2,1,0:T(8,128)}, u32[]{:S(2)}, u32[]{:S(2)}) collective-permute-start(f32[72,8,640]{2,1,0:T(8,128)} %slice_bitcast_fusion._), channel_id=1, source_target_pairs={{0,1},{1,0},{2,3},{3,2},{4,5},{5,4},{6,7},{7,6},{8,9},{9,8},{10,11... | collective-permute-start | bytes 4423688 | tf_op jit(solution)/shard_map/raw/ppermute | solution.py:351
  5.6 9.9 %coef.1 = (f32[16,72,640]{2,1,0:T(8,128)}, f32[9,72,640]{2,1,0:T(8,128)}, f32[9,72,640]{2,1,0:T(8,128)}) custom-call(s32[1152,640]{1,0:T(8,128)} %bitcast.12, f32[1152,640]{1,0:T(8,128)} %bitcast.13, bf16[640,640]{1,0:T(8,128)(2,1)} %constant.26.clone.refs_4_.refs_8_.order, f32[72,8,640]{2,1,0:T(8,128)} %slice_bitcast_fusion._), custom_call_target="tpu_custom_call" | custom-call | flops 11530000384 | bytes 1024 | tf_op jit(solution)/shard_map/coef/coef/pallas_call | solution.py:363
  15.6 4.4 %collective-permute-start.3 = (f32[9,72,640]{2,1,0:T(8,128)}, f32[9,72,640]{2,1,0:T(8,128)}, u32[]{:S(2)}, u32[]{:S(2)}) collective-permute-start(f32[9,72,640]{2,1,0:T(8,128)} %get-tuple-element.58), channel_id=1, source_target_pairs={{2,0},{4,2},{6,4},{8,6},{10,8},{12,10},{14,12},{16,14},{18,16},{20... | collective-permute-start | bytes 4976648 | tf_op jit(solution)/shard_map/coef/ppermute | solution.py:384
  20.0 0.7 pad_add_fusion.at
  20.7 18.2 %mix.1 = (f32[2,8,2,16,640]{4,3,2,1,0:T(8,128)}, f32[2,8,2,16,640]{4,3,2,1,0:T(8,128)}, f32[2,8,2,16,640]{4,3,2,1,0:T(8,128)}, f32[2,8,2,16,640]{4,3,2,1,0:T(8,1...) custom-call(s32[2]{0:T(128)} %pad_add_fusion.at, ...), custom_call_target="tpu_custom_call" | custom-call | flops 23060000768 | bytes 1024 | tf_op jit(solution)/shard_map/mix/mix/pallas_call | solution.py:394
  39.0 2.0 %collective-permute-start.7 = (f32[24,16,640]{2,1,0:T(8,128)}, f32[24,16,640]{2,1,0:T(8,128)}, u32[]{:S(2)}, u32[]{:S(2)}) collective-permute-start(f32[24,16,640]{2,1,0:T(8,128)} %get-tuple-element.64), channel_id=1, source_target_pairs={{0,1},{1,0},{2,3},{3,2},{4,5},{5,4},{6,7},{7,6},{8,9},{9,8},{10,11... | collective-permute-start | bytes 2949128 | tf_op jit(solution)/shard_map/mix/ppermute | solution.py:426
  41.0 8.1 %raw.1 = (f32[2,8,2,16,640]{4,3,2,1,0:T(8,128)}, f32[2,8,2,16,640]{4,3,2,1,0:T(8,128)}, f32[2,8,2,16,640]{4,3,2,1,0:T(8,128)}, f32[2,8,2,16,640]{4,3,2,1,0:T(8,128)}, f32[2,8,2,8,640]{4,3,2,1,0:T(8,128)}) custom-call(s32[2]{0:T(128)} %pad_add_fusion.at, ...), custom_call_target="tpu_custom_call", output_to_operand_aliasing={{0}: (10, {}), {1}: (11, {}), {2}: (12, {}), {3}: (13, {}),... | custom-call | flops 6918000128 | bytes 1024 | tf_op jit(solution)/shard_map/raw/raw/pallas_call | solution.py:432
  49.1 14.8 %collective-permute-done.4.refs_1_ = f32[24,16,640]{2,1,0:T(8,128)} collective-permute-done((f32[24,16,640]{2,1,0:T(8,128)}, f32[24,16,640]{2,1,0:T(8,128)}, u32[]{:S(2)}, u32[]{:S(2)}) %collective-permute-start.4) | collective-permute-done | bytes 983072 | tf_op jit(solution)/shard_map/mix/ppermute | solution.py:426
  64.0 0.6 broadcast_in_dim.4.refs_5_.refs_10_
  64.5 2.8 %edges.5 = (f32[10,2,16,640]{3,2,1,0:T(8,128)}, f32[10,2,16,640]{3,2,1,0:T(8,128)}, f32[8,128]{1,0:T(8,128)}) custom-call(f32[2,8,2,16,640]{4,3,2,1,0:T(8,128)} %get-tuple-element.59.refs_0_, f32[24,16,640]{2,1,0:T(8,128)} %collective-permute-done.4.refs_1_, f32[16,72,640]{2,1,0:T(8,128)} %get-tuple-element.56.refs_2_, ...), custom_call_target="tpu_custom_call" | custom-call | flops 2305999872 | bytes 1024 | tf_op jit(solution)/shard_map/edges/edges/pallas_call | solution.py:484
  67.3 4.4 %collective-permute-start.6 = (f32[10,2,16,640]{3,2,1,0:T(8,128)}, f32[10,2,16,640]{3,2,1,0:T(8,128)}, u32[]{:S(2)}, u32[]{:S(2)}) collective-permute-start(f32[10,2,16,640]{3,2,1,0:T(8,128)} %get-tuple-element.62), channel_id=1, source_target_pairs={{2,0},{4,2},{6,4},{8,6},{10,8},{12,10},{14,12},{16,14},{18,16},{20... | collective-permute-start | bytes 2457608 | tf_op jit(solution)/shard_map/edges/ppermute | solution.py:499
  71.8 2.0 %collective-permute-start.11 = (f32[24,16,640]{2,1,0:T(8,128)}, f32[24,16,640]{2,1,0:T(8,128)}, u32[]{:S(2)}, u32[]{:S(2)}) collective-permute-start(f32[24,16,640]{2,1,0:T(8,128)} %get-tuple-element.73), channel_id=1, source_target_pairs={{0,1},{1,0},{2,3},{3,2},{4,5},{5,4},{6,7},{7,6},{8,9},{9,8},{10,11... | collective-permute-start | bytes 2949128 | tf_op jit(solution)/shard_map/mix/ppermute | solution.py:426
  73.8 0.1 constant_dynamic-slice_fusion
  73.9 0.1 select_reduce_fusion
  74.0 11.1 %collective-permute-done.7.refs_1_ = f32[24,16,640]{2,1,0:T(8,128)} collective-permute-done((f32[24,16,640]{2,1,0:T(8,128)}, f32[24,16,640]{2,1,0:T(8,128)}, u32[]{:S(2)}, u32[]{:S(2)}) %collective-permute-start.7) | collective-permute-done | bytes 983072 | tf_op jit(solution)/shard_map/mix/ppermute | solution.py:426
  85.0 2.8 %edges.6 = (f32[10,2,16,640]{3,2,1,0:T(8,128)}, f32[10,2,16,640]{3,2,1,0:T(8,128)}, f32[8,128]{1,0:T(8,128)}) custom-call(f32[2,8,2,16,640]{4,3,2,1,0:T(8,128)} %get-tuple-element.63.refs_0_, f32[24,16,640]{2,1,0:T(8,128)} %collective-permute-done.7.refs_1_, f32[16,72,640]{2,1,0:T(8,128)} %get-tuple-element.56.refs_2_, ...), custom_call_target="tpu_custom_call" | custom-call | flops 2305999872 | bytes 1024 | tf_op jit(solution)/shard_map/edges/edges/pallas_call | solution.py:484
  87.8 4.4 %collective-permute-start.13 = (f32[10,2,16,640]{3,2,1,0:T(8,128)}, f32[10,2,16,640]{3,2,1,0:T(8,128)}, u32[]{:S(2)}, u32[]{:S(2)}) collective-permute-start(f32[10,2,16,640]{3,2,1,0:T(8,128)} %get-tuple-element.75), channel_id=1, source_target_pairs={{2,0},{4,2},{6,4},{8,6},{10,8},{12,10},{14,12},{16,14},{18,16},{20... | collective-permute-start | bytes 2457608 | tf_op jit(solution)/shard_map/edges/ppermute | solution.py:499
  92.3 0.9 broadcast_in_dim.5.refs_7_
  93.2 12.5 %diffusion.5 = (f32[2304,640]{1,0:T(8,128)}, f32[8,128]{1,0:T(8,128)}) custom-call(f32[2,8,2,16,640]{4,3,2,1,0:T(8,128)} %get-tuple-element.59.refs_0_, f32[24,16,640]{2,1,0:T(8,128)} %collective-permute-done.4.refs_1_, f32[16,72,640]{2,1,0:T(8,128)} %get-tuple-element.56.refs_2_, f32[10,2,16,640]{3,2,1,0:T(8,128)} %collective-permute-done.5.refs_3_, ...), custom_call_target="tpu_custom_call" | custom-call | flops 12682999808 | bytes 1024 | tf_op jit(solution)/shard_map/diffusion/diffusion/pallas_call | solution.py:508
  105.7 0.4 collective-permute-done.1.refs_1_
  106.1 2.8 %edges.7 = (f32[10,2,16,640]{3,2,1,0:T(8,128)}, f32[10,2,16,640]{3,2,1,0:T(8,128)}, f32[8,128]{1,0:T(8,128)}, f32[24,8,640]{2,1,0:T(8,128)}) custom-call(f32[2,8,2,16,640]{4,3,2,1,0:T(8,128)} %get-tuple-element.54.refs_0_, f32[24,16,640]{2,1,0:T(8,128)} %collective-permute-done.1.refs_1_, ...), custom_call_target="tpu_custom_call", output_to_operand_aliasing={{3}: (6, {})} | custom-call | flops 2305999872 | bytes 1024 | tf_op jit(solution)/shard_map/edges/edges/pallas_call | solution.py:484
  108.9 4.4 %collective-permute-start.10 = (f32[10,2,16,640]{3,2,1,0:T(8,128)}, f32[10,2,16,640]{3,2,1,0:T(8,128)}, u32[]{:S(2)}, u32[]{:S(2)}) collective-permute-start(f32[10,2,16,640]{3,2,1,0:T(8,128)} %get-tuple-element.71), channel_id=1, source_target_pairs={{2,0},{4,2},{6,4},{8,6},{10,8},{12,10},{14,12},{16,14},{18,16},{20... | collective-permute-start | bytes 2457608 | tf_op jit(solution)/shard_map/edges/ppermute | solution.py:499
  113.4 12.5 %diffusion.6 = (f32[2304,640]{1,0:T(8,128)}, f32[8,128]{1,0:T(8,128)}) custom-call(f32[2,8,2,16,640]{4,3,2,1,0:T(8,128)} %get-tuple-element.63.refs_0_, f32[24,16,640]{2,1,0:T(8,128)} %collective-permute-done.7.refs_1_, f32[16,72,640]{2,1,0:T(8,128)} %get-tuple-element.56.refs_2_, ...), custom_call_target="tpu_custom_call", output_to_operand_aliasing={{0}: (10, {})} | custom-call | flops 12682999808 | bytes 1024 | tf_op jit(solution)/shard_map/diffusion/diffusion/pallas_call | solution.py:508
  125.9 1.2 collective-permute-done.11.refs_1_
  127.2 2.8 %edges.8 = (f32[10,2,16,640]{3,2,1,0:T(8,128)}, f32[10,2,16,640]{3,2,1,0:T(8,128)}, f32[8,128]{1,0:T(8,128)}) custom-call(f32[2,8,2,16,640]{4,3,2,1,0:T(8,128)} %get-tuple-element.72.refs_0_, f32[24,16,640]{2,1,0:T(8,128)} %collective-permute-done.11.refs_1_, f32[16,72,640]{2,1,0:T(8,128)} %get-tuple-element.56.refs_2_, ...), custom_call_target="tpu_custom_call" | custom-call | flops 2305999872 | bytes 1024 | tf_op jit(solution)/shard_map/edges/edges/pallas_call | solution.py:484
  129.9 4.4 %collective-permute-start.17 = (f32[10,2,16,640]{3,2,1,0:T(8,128)}, f32[10,2,16,640]{3,2,1,0:T(8,128)}, u32[]{:S(2)}, u32[]{:S(2)}) collective-permute-start(f32[10,2,16,640]{3,2,1,0:T(8,128)} %get-tuple-element.85), channel_id=1, source_target_pairs={{2,0},{4,2},{6,4},{8,6},{10,8},{12,10},{14,12},{16,14},{18,16},{20... | collective-permute-start | bytes 2457608 | tf_op jit(solution)/shard_map/edges/ppermute | solution.py:499
  134.4 12.5 %diffusion.7 = (f32[2304,640]{1,0:T(8,128)}, f32[8,128]{1,0:T(8,128)}) custom-call(f32[2,8,2,16,640]{4,3,2,1,0:T(8,128)} %get-tuple-element.54.refs_0_, f32[24,16,640]{2,1,0:T(8,128)} %collective-permute-done.1.refs_1_, f32[16,72,640]{2,1,0:T(8,128)} %get-tuple-element.56.refs_2_, ...), custom_call_target="tpu_custom_call", output_to_operand_aliasing={{0}: (10, {})} | custom-call | flops 12682999808 | bytes 1024 | tf_op jit(solution)/shard_map/diffusion/diffusion/pallas_call | solution.py:508
  146.9 2.3 %edges.9 = (f32[10,2,8,640]{3,2,1,0:T(8,128)}, f32[10,2,8,640]{3,2,1,0:T(8,128)}, f32[8,128]{1,0:T(8,128)}) custom-call(f32[2,8,2,8,640]{4,3,2,1,0:T(8,128)} %get-tuple-element.53.refs_0_, f32[24,8,640]{2,1,0:T(8,128)} %collective-permute-done.8.refs_1_, f32[16,72,640]{2,1,0:T(8,128)} %get-tuple-element.56.refs_2_, ...), custom_call_target="tpu_custom_call" | custom-call | flops 2305999872 | bytes 1024 | tf_op jit(solution)/shard_map/edges/edges/pallas_call | solution.py:484
  149.2 4.4 %collective-permute-start.15 = (f32[10,2,8,640]{3,2,1,0:T(8,128)}, f32[10,2,8,640]{3,2,1,0:T(8,128)}, u32[]{:S(2)}, u32[]{:S(2)}) collective-permute-start(f32[10,2,8,640]{3,2,1,0:T(8,128)} %get-tuple-element.83), channel_id=1, source_target_pairs={{2,0},{4,2},{6,4},{8,6},{10,8},{12,10},{14,12},{16,14},{18,16},{20... | collective-permute-start | bytes 1228808 | tf_op jit(solution)/shard_map/edges/ppermute | solution.py:499
  153.7 12.5 %diffusion.8 = (f32[2304,640]{1,0:T(8,128)}, f32[8,128]{1,0:T(8,128)}) custom-call(f32[2,8,2,16,640]{4,3,2,1,0:T(8,128)} %get-tuple-element.72.refs_0_, f32[24,16,640]{2,1,0:T(8,128)} %collective-permute-done.11.refs_1_, f32[16,72,640]{2,1,0:T(8,128)} %get-tuple-element.56.refs_2_, ...), custom_call_target="tpu_custom_call", output_to_operand_aliasing={{0}: (10, {})} | custom-call | flops 12682999808 | bytes 1024 | tf_op jit(solution)/shard_map/diffusion/diffusion/pallas_call | solution.py:508
  166.2 7.5 %diffusion.9 = (f32[2304,640]{1,0:T(8,128)}, f32[8,128]{1,0:T(8,128)}) custom-call(f32[2,8,2,8,640]{4,3,2,1,0:T(8,128)} %get-tuple-element.53.refs_0_, f32[24,8,640]{2,1,0:T(8,128)} %collective-permute-done.8.refs_1_, f32[16,72,640]{2,1,0:T(8,128)} %get-tuple-element.56.refs_2_, ...), custom_call_target="tpu_custom_call", output_to_operand_aliasing={{0}: (10, {})} | custom-call | flops 12682999808 | bytes 1024 | tf_op jit(solution)/shard_map/diffusion/diffusion/pallas_call | solution.py:508
  (27 shorter events, 0.2 us)
Async XLA Ops:
  0.0 73.8 %copy-start = (s32[10,144]{1,0:T(8,128)S(1)}, s32[10,144]{1,0:T(8,128)}, u32[]{:S(2)}) copy-start(s32[10,144]{1,0:T(8,128)} %param.13) | copy-start | bytes 17284
  2.6 38.4 %collective-permute-start = (f32[72,8,640]{2,1,0:T(8,128)}, f32[72,8,640]{2,1,0:T(8,128)}, u32[]{:S(2)}, u32[]{:S(2)}) collective-permute-start(f32[72,8,640]{2,1,0:T(8,128)} %slice_bitcast_fusion._), channel_id=1, source_target_pairs={{0,1},{1,0},{2,3},{3,2},{4,5},{5,4},{6,7},{7,6},{8,9},{9,8},{10,11... | collective-permute-start | bytes 4423688 | tf_op jit(solution)/shard_map/raw/ppermute | solution.py:351
  15.5 48.4 %collective-permute-start.2 = (f32[9,72,640]{2,1,0:T(8,128)}, f32[9,72,640]{2,1,0:T(8,128)}, u32[]{:S(2)}, u32[]{:S(2)}) collective-permute-start(f32[9,72,640]{2,1,0:T(8,128)} %get-tuple-element.57), channel_id=1, source_target_pairs={{0,2},{2,4},{4,6},{6,8},{8,10},{10,12},{12,14},{14,16},{16,18},{18... | collective-permute-start | bytes 4976648 | tf_op jit(solution)/shard_map/coef/ppermute | solution.py:383
  15.6 48.4 %collective-permute-start.3 = (f32[9,72,640]{2,1,0:T(8,128)}, f32[9,72,640]{2,1,0:T(8,128)}, u32[]{:S(2)}, u32[]{:S(2)}) collective-permute-start(f32[9,72,640]{2,1,0:T(8,128)} %get-tuple-element.58), channel_id=1, source_target_pairs={{2,0},{4,2},{6,4},{8,6},{10,8},{12,10},{14,12},{16,14},{18,16},{20... | collective-permute-start | bytes 4976648 | tf_op jit(solution)/shard_map/coef/ppermute | solution.py:384
  38.9 25.1 %collective-permute-start.4 = (f32[24,16,640]{2,1,0:T(8,128)}, f32[24,16,640]{2,1,0:T(8,128)}, u32[]{:S(2)}, u32[]{:S(2)}) collective-permute-start(f32[24,16,640]{2,1,0:T(8,128)} %get-tuple-element.60), channel_id=1, source_target_pairs={{0,1},{1,0},{2,3},{3,2},{4,5},{5,4},{6,7},{7,6},{8,9},{9,8},{10,11... | collective-permute-start | bytes 2949128 | tf_op jit(solution)/shard_map/mix/ppermute | solution.py:426
  39.0 46.1 %collective-permute-start.7 = (f32[24,16,640]{2,1,0:T(8,128)}, f32[24,16,640]{2,1,0:T(8,128)}, u32[]{:S(2)}, u32[]{:S(2)}) collective-permute-start(f32[24,16,640]{2,1,0:T(8,128)} %get-tuple-element.64), channel_id=1, source_target_pairs={{0,1},{1,0},{2,3},{3,2},{4,5},{5,4},{6,7},{7,6},{8,9},{9,8},{10,11... | collective-permute-start | bytes 2949128 | tf_op jit(solution)/shard_map/mix/ppermute | solution.py:426
  64.5 9.3 %copy-start.1 = (f32[8]{0:T(128)S(1)}, f32[8]{0:T(128)}, u32[]{:S(2)}) copy-start(f32[8]{0:T(128)} %param.14) | copy-start | bytes 100
  67.3 20.5 %collective-permute-start.5 = (f32[10,2,16,640]{3,2,1,0:T(8,128)}, f32[10,2,16,640]{3,2,1,0:T(8,128)}, u32[]{:S(2)}, u32[]{:S(2)}) collective-permute-start(f32[10,2,16,640]{3,2,1,0:T(8,128)} %get-tuple-element.61), channel_id=1, source_target_pairs={{0,2},{2,4},{4,6},{6,8},{8,10},{10,12},{12,14},{14,16},{16,18},{18... | collective-permute-start | bytes 2457608 | tf_op jit(solution)/shard_map/edges/ppermute | solution.py:499
  67.3 25.0 %collective-permute-start.6 = (f32[10,2,16,640]{3,2,1,0:T(8,128)}, f32[10,2,16,640]{3,2,1,0:T(8,128)}, u32[]{:S(2)}, u32[]{:S(2)}) collective-permute-start(f32[10,2,16,640]{3,2,1,0:T(8,128)} %get-tuple-element.62), channel_id=1, source_target_pairs={{2,0},{4,2},{6,4},{8,6},{10,8},{12,10},{14,12},{16,14},{18,16},{20... | collective-permute-start | bytes 2457608 | tf_op jit(solution)/shard_map/edges/ppermute | solution.py:499
  71.8 34.3 %collective-permute-start.1 = (f32[24,16,640]{2,1,0:T(8,128)}, f32[24,16,640]{2,1,0:T(8,128)}, u32[]{:S(2)}, u32[]{:S(2)}) collective-permute-start(f32[24,16,640]{2,1,0:T(8,128)} %get-tuple-element.55), channel_id=1, source_target_pairs={{0,1},{1,0},{2,3},{3,2},{4,5},{5,4},{6,7},{7,6},{8,9},{9,8},{10,11... | collective-permute-start | bytes 2949128 | tf_op jit(solution)/shard_map/mix/ppermute | solution.py:426
  71.8 55.4 %collective-permute-start.11 = (f32[24,16,640]{2,1,0:T(8,128)}, f32[24,16,640]{2,1,0:T(8,128)}, u32[]{:S(2)}, u32[]{:S(2)}) collective-permute-start(f32[24,16,640]{2,1,0:T(8,128)} %get-tuple-element.73), channel_id=1, source_target_pairs={{0,1},{1,0},{2,3},{3,2},{4,5},{5,4},{6,7},{7,6},{8,9},{9,8},{10,11... | collective-permute-start | bytes 2949128 | tf_op jit(solution)/shard_map/mix/ppermute | solution.py:426
  87.8 21.1 %collective-permute-start.12 = (f32[10,2,16,640]{3,2,1,0:T(8,128)}, f32[10,2,16,640]{3,2,1,0:T(8,128)}, u32[]{:S(2)}, u32[]{:S(2)}) collective-permute-start(f32[10,2,16,640]{3,2,1,0:T(8,128)} %get-tuple-element.74), channel_id=1, source_target_pairs={{0,2},{2,4},{4,6},{6,8},{8,10},{10,12},{12,14},{14,16},{16,18},{18... | collective-permute-start | bytes 2457608 | tf_op jit(solution)/shard_map/edges/ppermute | solution.py:499
  87.8 25.5 %collective-permute-start.13 = (f32[10,2,16,640]{3,2,1,0:T(8,128)}, f32[10,2,16,640]{3,2,1,0:T(8,128)}, u32[]{:S(2)}, u32[]{:S(2)}) collective-permute-start(f32[10,2,16,640]{3,2,1,0:T(8,128)} %get-tuple-element.75), channel_id=1, source_target_pairs={{2,0},{4,2},{6,4},{8,6},{10,8},{12,10},{14,12},{16,14},{18,16},{20... | collective-permute-start | bytes 2457608 | tf_op jit(solution)/shard_map/edges/ppermute | solution.py:499
  108.9 38.0 %collective-permute-start.8 = (f32[24,8,640]{2,1,0:T(8,128)}, f32[24,8,640]{2,1,0:T(8,128)}, u32[]{:S(2)}, u32[]{:S(2)}) collective-permute-start(f32[24,8,640]{2,1,0:T(8,128)} %get-tuple-element.69), channel_id=1, source_target_pairs={{0,1},{1,0},{2,3},{3,2},{4,5},{5,4},{6,7},{7,6},{8,9},{9,8},{10,11... | collective-permute-start | bytes 1474568 | tf_op jit(solution)/shard_map/ppermute | solution.py:426
  108.9 25.5 %collective-permute-start.9 = (f32[10,2,16,640]{3,2,1,0:T(8,128)}, f32[10,2,16,640]{3,2,1,0:T(8,128)}, u32[]{:S(2)}, u32[]{:S(2)}) collective-permute-start(f32[10,2,16,640]{3,2,1,0:T(8,128)} %get-tuple-element.70), channel_id=1, source_target_pairs={{0,2},{2,4},{4,6},{6,8},{8,10},{10,12},{12,14},{14,16},{16,18},{18... | collective-permute-start | bytes 2457608 | tf_op jit(solution)/shard_map/edges/ppermute | solution.py:499
  108.9 25.4 %collective-permute-start.10 = (f32[10,2,16,640]{3,2,1,0:T(8,128)}, f32[10,2,16,640]{3,2,1,0:T(8,128)}, u32[]{:S(2)}, u32[]{:S(2)}) collective-permute-start(f32[10,2,16,640]{3,2,1,0:T(8,128)} %get-tuple-element.71), channel_id=1, source_target_pairs={{2,0},{4,2},{6,4},{8,6},{10,8},{12,10},{14,12},{16,14},{18,16},{20... | collective-permute-start | bytes 2457608 | tf_op jit(solution)/shard_map/edges/ppermute | solution.py:499
  129.9 23.7 %collective-permute-start.16 = (f32[10,2,16,640]{3,2,1,0:T(8,128)}, f32[10,2,16,640]{3,2,1,0:T(8,128)}, u32[]{:S(2)}, u32[]{:S(2)}) collective-permute-start(f32[10,2,16,640]{3,2,1,0:T(8,128)} %get-tuple-element.84), channel_id=1, source_target_pairs={{0,2},{2,4},{4,6},{6,8},{8,10},{10,12},{12,14},{14,16},{16,18},{18... | collective-permute-start | bytes 2457608 | tf_op jit(solution)/shard_map/edges/ppermute | solution.py:499
  129.9 23.7 %collective-permute-start.17 = (f32[10,2,16,640]{3,2,1,0:T(8,128)}, f32[10,2,16,640]{3,2,1,0:T(8,128)}, u32[]{:S(2)}, u32[]{:S(2)}) collective-permute-start(f32[10,2,16,640]{3,2,1,0:T(8,128)} %get-tuple-element.85), channel_id=1, source_target_pairs={{2,0},{4,2},{6,4},{8,6},{10,8},{12,10},{14,12},{16,14},{18,16},{20... | collective-permute-start | bytes 2457608 | tf_op jit(solution)/shard_map/edges/ppermute | solution.py:499
  149.2 17.0 %collective-permute-start.14 = (f32[10,2,8,640]{3,2,1,0:T(8,128)}, f32[10,2,8,640]{3,2,1,0:T(8,128)}, u32[]{:S(2)}, u32[]{:S(2)}) collective-permute-start(f32[10,2,8,640]{3,2,1,0:T(8,128)} %get-tuple-element.82), channel_id=1, source_target_pairs={{0,2},{2,4},{4,6},{6,8},{8,10},{10,12},{12,14},{14,16},{16,18},{18... | collective-permute-start | bytes 1228808 | tf_op jit(solution)/shard_map/edges/ppermute | solution.py:499
  149.2 17.0 %collective-permute-start.15 = (f32[10,2,8,640]{3,2,1,0:T(8,128)}, f32[10,2,8,640]{3,2,1,0:T(8,128)}, u32[]{:S(2)}, u32[]{:S(2)}) collective-permute-start(f32[10,2,8,640]{3,2,1,0:T(8,128)} %get-tuple-element.83), channel_id=1, source_target_pairs={{2,0},{4,2},{6,4},{8,6},{10,8},{12,10},{14,12},{16,14},{18,16},{20... | collective-permute-start | bytes 1228808 | tf_op jit(solution)/shard_map/edges/ppermute | solution.py:499

commit v2 on v1

--- a/solution.py
+++ b/solution.py
@@ -15,7 +15,6 @@
 COEF_GROUPS = 4
 PAIR = 2
 EXACT = lax.Precision.HIGHEST
-VMEM_LIMIT = 65200 * 1024
 
 
 def chunk_units(total):
@@ -319,8 +318,8 @@
     return pl.BlockSpec(block, lambda i: (0,) * len(block))
 
 
-def params():
-    return pltpu.CompilerParams(vmem_limit_bytes=VMEM_LIMIT)
+def params(mebibytes):
+    return pltpu.CompilerParams(vmem_limit_bytes=mebibytes * 1024 * 1024)
 
 
 def spent(microseconds):
@@ -376,7 +375,7 @@
                 pltpu.VMEM((lons, padded, lats), f32),
                 pltpu.SemaphoreType.DMA((2 * tiles + 3 * COEF_GROUPS,)),
             ],
-            compiler_params=params(),
+            compiler_params=params(53),
             cost_estimate=spent(10),
             name="coef",
         )(land_sea.reshape(own * lons, lats), roughness.reshape(own * lons, lats), order, rows)
@@ -409,7 +408,7 @@
                 pltpu.VMEM((tiles, own * 2 * lons, LANES), f32),
                 pltpu.SemaphoreType.DMA((tiles,)),
             ],
-            compiler_params=params(),
+            compiler_params=params(30),
             cost_estimate=spent(20),
             name="mix",
         )(
@@ -446,7 +445,7 @@
                 pltpu.VMEM((3 * padded, PAIR * lats), jnp.bfloat16),
             ],
             input_output_aliases={5 + tiles * (lev_count - 1) + c: c for c in range(len(chunks))},
-            compiler_params=params(),
+            compiler_params=params(16),
             cost_estimate=spent(6),
             name="raw",
         )(
@@ -492,7 +491,7 @@
                 + [token_spec]
                 + [hidden] * len(passed),
                 input_output_aliases={len(sums) + 4 + i: 3 + i for i in range(len(passed))},
-                compiler_params=params(),
+                compiler_params=params(12),
                 cost_estimate=spent(2),
                 name="edges",
             )(*sums, coef, coef_before, coef_after, token, *passed)
@@ -522,7 +521,7 @@
                     pltpu.VMEM((tiles * ROWS * 2 * lons, LANES), f32),
                 ],
                 input_output_aliases={} if c == 0 else {len(operands) - 1: 0},
-                compiler_params=params(),
+                compiler_params=params(18),
                 cost_estimate=spent(11),
                 name="diffusion",
             )(*operands)

time: 174 us -> 169 us (0.971)
  the two profiles are of different devices: /device:TPU:0 before, /device:TPU:25 now
where the time goes in v2:
time: 169 us
  Pallas kernels  89.2 us (53%)
  waiting for transfers between devices  40.5 us (24%)
  starting transfers between devices  28.9 us (17%)
  local copies, waits for them, and re-layouts  9.66 us (6%)
    pallas_call x5, Pallas kernels, diffusion(): pl.pallas_call(functools.partial(diffuse_kernel, lons, lats, len(sums)),...  52.8 us
    ppermute x5, waiting for transfers between devices, send(): lax.ppermute(array, 'lev', along(shift + 1))  29.6 us
    ppermute x5, starting transfers between devices, edges(): lax.ppermute(last, 'tile', up)  19.3 us
    pallas_call x1, Pallas kernels, on_device(): pl.pallas_call(functools.partial(mix_kernel, shape, offsets), grid=(half...  16.8 us
    pallas_call x1, Pallas kernels, on_device(): pl.pallas_call(functools.partial(coef_kernel, own, padded, lons, halo - 1...  8.81 us
    ppermute x5, waiting for transfers between devices, edges(): lax.ppermute(first, 'tile', down)  7.2 us
    unnamed x56, local copies, waits for them, and re-layouts  6.67 us
    pallas_call x5, Pallas kernels, edges(): pl.pallas_call(functools.partial(edge_kernel, lons, halo, len(sums), len(...  6.01 us
  transfers between devices with their start and end apart: 18, of which 8 were waited for; matrix products, arithmetic and copies ran while one was open for 0% of the time, Pallas kernels for 49%

profile of v2, /device:TPU:25, one launch (start us, length us, event | category | flops | bytes accessed | tf_op | source)
XLA Modules:
  0.0 168.7 jit_solution(785668478027688678)
XLA Ops:
  0.0 2.8 %slice_bitcast_fusion._ = f32[72,8,640]{2,1,0:T(8,128)} fusion(f32[72,2,16,640]{3,2,1,0:T(8,128)} %param.10), kind=kLoop, calls=%fused_computation | loop fusion | bytes 2949120 | tf_op jit(solution)/shard_map/raw/squeeze | solution.py:349
  2.8 1.2 collective-permute-start
  4.0 8.8 %coef.1 = (f32[16,72,640]{2,1,0:T(8,128)}, f32[9,72,640]{2,1,0:T(8,128)}, f32[9,72,640]{2,1,0:T(8,128)}) custom-call(s32[1152,640]{1,0:T(8,128)} %bitcast.17, f32[1152,640]{1,0:T(8,128)} %bitcast.18, bf16[640,640]{1,0:T(8,128)(2,1)S(1)} %copy-done.23, f32[72,8,640]{2,1,0:T(8,128)} %slice_bitcast_fusion._), custom_call_target="tpu_custom_call" | custom-call | flops 11530000384 | bytes 1024 | tf_op jit(solution)/shard_map/coef/coef/pallas_call | solution.py:362
  12.8 2.1 %collective-permute-start.2 = (f32[9,72,640]{2,1,0:T(8,128)}, f32[9,72,640]{2,1,0:T(8,128)}, u32[]{:S(2)}, u32[]{:S(2)}) collective-permute-start(f32[9,72,640]{2,1,0:T(8,128)} %get-tuple-element.57), channel_id=1, source_target_pairs={{0,2},{2,4},{4,6},{6,8},{8,10},{10,12},{12,14},{14,16},{16,18},{18... | collective-permute-start | bytes 4976648 | tf_op jit(solution)/shard_map/coef/ppermute | solution.py:382
  15.0 2.7 %copy-done.13 = f32[72,2,16,640]{3,2,1,0:T(8,128)S(1)} copy-done((f32[72,2,16,640]{3,2,1,0:T(8,128)S(1)}, f32[72,2,16,640]{3,2,1,0:T(8,128)}, u32[]{:S(2)}) %copy-start.13) | copy-done | bytes 5898264
  17.7 16.8 %mix.1 = (f32[2,8,2,16,640]{4,3,2,1,0:T(8,128)S(1)}, f32[2,8,2,16,640]{4,3,2,1,0:T(8,128)S(1)}, f32[2,8,2,16,640]{4,3,2,1,0:T(8,128)S(1)}, f32[2,8,2,16,640]{4,3...) custom-call(s32[2]{0:T(128)S(1)} %pad_add_fusion.at, ...), custom_call_target="tpu_custom_call" | custom-call | flops 23060000768 | bytes 1024 | tf_op jit(solution)/shard_map/mix/mix/pallas_call | solution.py:393
  34.8 1.2 collective-permute-start.7
  37.4 1.4 copy-done.15
  38.8 4.9 %raw.1 = (f32[2,8,2,16,640]{4,3,2,1,0:T(8,128)S(1)}, f32[2,8,2,16,640]{4,3,2,1,0:T(8,128)S(1)}, f32[2,8,2,16,640]{4,3,2,1,0:T(8,128)S(1)}, f32[2,8,2,16,640]{4,3,2,1,0:T(8,128)S(1)}, f32[2,8,2,8,640]{4,3,2,1,0:T(8,128)S(1)}) custom-call(s32[2]{0:T(128)S(1)} %pad_add_fusion.at, ...), custom_call_target="tpu_custom_call", output_to_operand_aliasing={{0}: (10, {}), {1}: (11, {}), {2}: (12, {}), {3}: (13, {}),... | custom-call | flops 6918000128 | bytes 1024 | tf_op jit(solution)/shard_map/raw/raw/pallas_call | solution.py:431
  43.7 12.7 %collective-permute-done.4.refs_1_ = f32[24,16,640]{2,1,0:T(8,128)S(1)} collective-permute-done((f32[24,16,640]{2,1,0:T(8,128)S(1)}, f32[24,16,640]{2,1,0:T(8,128)S(1)}, u32[]{:S(2)}, u32[]{:S(2)}) %collective-permute-start.4) | collective-permute-done | bytes 983072 | tf_op jit(solution)/shard_map/mix/ppermute | solution.py:425
  56.5 1.5 edges.5
  58.0 4.6 %collective-permute-start.5 = (f32[10,2,16,640]{3,2,1,0:T(8,128)}, f32[10,2,16,640]{3,2,1,0:T(8,128)}, u32[]{:S(2)}, u32[]{:S(2)}) collective-permute-start(f32[10,2,16,640]{3,2,1,0:T(8,128)} %get-tuple-element.61), channel_id=1, source_target_pairs={{0,2},{2,4},{4,6},{6,8},{8,10},{10,12},{12,14},{14,16},{16,18},{18... | collective-permute-start | bytes 2457608 | tf_op jit(solution)/shard_map/edges/ppermute | solution.py:498
  62.6 1.2 collective-permute-start.1
  64.3 13.3 %collective-permute-done.7.refs_1_ = f32[24,16,640]{2,1,0:T(8,128)} collective-permute-done((f32[24,16,640]{2,1,0:T(8,128)}, f32[24,16,640]{2,1,0:T(8,128)}, u32[]{:S(2)}, u32[]{:S(2)}) %collective-permute-start.7) | collective-permute-done | bytes 983072 | tf_op jit(solution)/shard_map/mix/ppermute | solution.py:425
  77.6 1.3 copy-done.5
  78.9 1.5 edges.6
  80.5 4.6 %collective-permute-start.12 = (f32[10,2,16,640]{3,2,1,0:T(8,128)S(1)}, f32[10,2,16,640]{3,2,1,0:T(8,128)S(1)}, u32[]{:S(2)}, u32[]{:S(2)}) collective-permute-start(f32[10,2,16,640]{3,2,1,0:T(8,128)S(1)} %get-tuple-element.74), channel_id=1, source_target_pairs={{0,2},{2,4},{4,6},{6,8},{8,10},{10,12},{12,14},{14,16},{16,18},{18... | collective-permute-start | bytes 2457608 | tf_op jit(solution)/shard_map/edges/ppermute | solution.py:498
  85.3 11.7 %diffusion.5 = (f32[2304,640]{1,0:T(8,128)}, f32[8,128]{1,0:T(8,128)S(1)}) custom-call(f32[2,8,2,16,640]{4,3,2,1,0:T(8,128)S(1)} %copy-done.3, f32[24,16,640]{2,1,0:T(8,128)S(1)} %copy-done.12, f32[16,72,640]{2,1,0:T(8,128)S(1)} %copy-done.1, f32[10,2,16,640]{3,2,1,0:T(8,128)} %collective-permute-done.5.refs_3_, ...), custom_call_target="tpu_custom_call" | custom-call | flops 12682999808 | bytes 1024 | tf_op jit(solution)/shard_map/diffusion/diffusion/pallas_call | solution.py:507
  97.0 1.7 %collective-permute-done.1.refs_1_ = f32[24,16,640]{2,1,0:T(8,128)} collective-permute-done((f32[24,16,640]{2,1,0:T(8,128)}, f32[24,16,640]{2,1,0:T(8,128)}, u32[]{:S(2)}, u32[]{:S(2)}) %collective-permute-start.1) | collective-permute-done | bytes 983072 | tf_op jit(solution)/shard_map/mix/ppermute | solution.py:425
  98.7 1.5 edges.7
  100.2 2.3 %collective-permute-start.8 = (f32[24,8,640]{2,1,0:T(8,128)S(1)}, f32[24,8,640]{2,1,0:T(8,128)S(1)}, u32[]{:S(2)}, u32[]{:S(2)}) collective-permute-start(f32[24,8,640]{2,1,0:T(8,128)S(1)} %get-tuple-element.69), channel_id=1, source_target_pairs={{0,1},{1,0},{2,3},{3,2},{4,5},{5,4},{6,7},{7,6},{8,9},{9,8},{10,11... | collective-permute-start | bytes 1474568 | tf_op jit(solution)/shard_map/ppermute | solution.py:425
  102.4 3.9 %collective-permute-start.9 = (f32[10,2,16,640]{3,2,1,0:T(8,128)S(1)}, f32[10,2,16,640]{3,2,1,0:T(8,128)S(1)}, u32[]{:S(2)}, u32[]{:S(2)}) collective-permute-start(f32[10,2,16,640]{3,2,1,0:T(8,128)S(1)} %get-tuple-element.70), channel_id=1, source_target_pairs={{0,2},{2,4},{4,6},{6,8},{8,10},{10,12},{12,14},{14,16},{16,18},{18... | collective-permute-start | bytes 2457608 | tf_op jit(solution)/shard_map/edges/ppermute | solution.py:498
  106.3 11.6 %diffusion.6 = (f32[2304,640]{1,0:T(8,128)}, f32[8,128]{1,0:T(8,128)S(1)}) custom-call(f32[2,8,2,16,640]{4,3,2,1,0:T(8,128)S(1)} %copy-done.6, f32[24,16,640]{2,1,0:T(8,128)} %collective-permute-done.7.refs_1_, f32[16,72,640]{2,1,0:T(8,128)S(1)} %copy-done.1, ...), custom_call_target="tpu_custom_call", output_to_operand_aliasing={{0}: (10, {})} | custom-call | flops 12682999808 | bytes 1024 | tf_op jit(solution)/shard_map/diffusion/diffusion/pallas_call | solution.py:507
  117.9 1.8 %collective-permute-done.11.refs_1_ = f32[24,16,640]{2,1,0:T(8,128)} collective-permute-done((f32[24,16,640]{2,1,0:T(8,128)}, f32[24,16,640]{2,1,0:T(8,128)}, u32[]{:S(2)}, u32[]{:S(2)}) %collective-permute-start.11) | collective-permute-done | bytes 983072 | tf_op jit(solution)/shard_map/mix/ppermute | solution.py:425
  119.7 1.4 edges.8
  121.1 4.6 %collective-permute-start.16 = (f32[10,2,16,640]{3,2,1,0:T(8,128)S(1)}, f32[10,2,16,640]{3,2,1,0:T(8,128)S(1)}, u32[]{:S(2)}, u32[]{:S(2)}) collective-permute-start(f32[10,2,16,640]{3,2,1,0:T(8,128)S(1)} %get-tuple-element.84), channel_id=1, source_target_pairs={{0,2},{2,4},{4,6},{6,8},{8,10},{10,12},{12,14},{14,16},{16,18},{18... | collective-permute-start | bytes 2457608 | tf_op jit(solution)/shard_map/edges/ppermute | solution.py:498
  126.1 11.5 %diffusion.7 = (f32[2304,640]{1,0:T(8,128)}, f32[8,128]{1,0:T(8,128)S(1)}) custom-call(f32[2,8,2,16,640]{4,3,2,1,0:T(8,128)S(1)} %copy-done.8, f32[24,16,640]{2,1,0:T(8,128)} %collective-permute-done.1.refs_1_, f32[16,72,640]{2,1,0:T(8,128)S(1)} %copy-done.1, ...), custom_call_target="tpu_custom_call", output_to_operand_aliasing={{0}: (10, {})} | custom-call | flops 12682999808 | bytes 1024 | tf_op jit(solution)/shard_map/diffusion/diffusion/pallas_call | solution.py:507
  137.7 1.5 collective-permute-start.14
  140.2 3.6 %collective-permute-done.16.refs_3_ = f32[10,2,16,640]{3,2,1,0:T(8,128)S(1)} collective-permute-done((f32[10,2,16,640]{3,2,1,0:T(8,128)S(1)}, f32[10,2,16,640]{3,2,1,0:T(8,128)S(1)}, u32[]{:S(2)}, u32[]{:S(2)}) %collective-permute-start.16) | collective-permute-done | bytes 819232 | tf_op jit(solution)/shard_map/edges/ppermute | solution.py:498
  143.8 6.9 %collective-permute-done.17.refs_4_ = f32[10,2,16,640]{3,2,1,0:T(8,128)S(1)} collective-permute-done((f32[10,2,16,640]{3,2,1,0:T(8,128)S(1)}, f32[10,2,16,640]{3,2,1,0:T(8,128)S(1)}, u32[]{:S(2)}, u32[]{:S(2)}) %collective-permute-start.17) | collective-permute-done | bytes 819232 | tf_op jit(solution)/shard_map/edges/ppermute | solution.py:498
  150.7 11.5 %diffusion.8 = (f32[2304,640]{1,0:T(8,128)}, f32[8,128]{1,0:T(8,128)S(1)}) custom-call(f32[2,8,2,16,640]{4,3,2,1,0:T(8,128)S(1)} %copy-done.10, f32[24,16,640]{2,1,0:T(8,128)} %collective-permute-done.11.refs_1_, f32[16,72,640]{2,1,0:T(8,128)S(1)} %copy-done.1, ...), custom_call_target="tpu_custom_call", output_to_operand_aliasing={{0}: (10, {})} | custom-call | flops 12682999808 | bytes 1024 | tf_op jit(solution)/shard_map/diffusion/diffusion/pallas_call | solution.py:507
  162.2 6.6 %diffusion.9 = (f32[2304,640]{1,0:T(8,128)}, f32[8,128]{1,0:T(8,128)}) custom-call(f32[2,8,2,8,640]{4,3,2,1,0:T(8,128)S(1)} %copy-done.26, f32[24,8,640]{2,1,0:T(8,128)S(1)} %collective-permute-done.8.refs_1_, f32[16,72,640]{2,1,0:T(8,128)S(1)} %copy-done.1, f32[10,2,8,640]{3,2,1,0:T(8,128)S(1)} %collective-permute-done.14.refs_3_, ...), custom_call_target="tpu_custom_call", output_to_operand_aliasing={{0}: (10, {})} | custom-call | flops 12682999808 | bytes 1024 | tf_op jit(solution)/shard_map/diffusion/diffusion/pallas_call | solution.py:507
  (79 shorter events, 3.8 us)
Async XLA Ops:
  0.0 64.1 %copy-start = (s32[10,144]{1,0:T(8,128)S(1)}, s32[10,144]{1,0:T(8,128)}, u32[]{:S(2)}) copy-start(s32[10,144]{1,0:T(8,128)} %param.13) | copy-start | bytes 17284
  2.8 33.4 %collective-permute-start = (f32[72,8,640]{2,1,0:T(8,128)}, f32[72,8,640]{2,1,0:T(8,128)S(1)}, u32[]{:S(2)}, u32[]{:S(2)}) collective-permute-start(f32[72,8,640]{2,1,0:T(8,128)} %slice_bitcast_fusion._), channel_id=1, source_target_pairs={{0,1},{1,0},{2,3},{3,2},{4,5},{5,4},{6,7},{7,6},{8,9},{9,8},{10,11... | collective-permute-start | bytes 4423688 | tf_op jit(solution)/shard_map/raw/ppermute | solution.py:350
  12.8 43.6 %collective-permute-start.2 = (f32[9,72,640]{2,1,0:T(8,128)}, f32[9,72,640]{2,1,0:T(8,128)}, u32[]{:S(2)}, u32[]{:S(2)}) collective-permute-start(f32[9,72,640]{2,1,0:T(8,128)} %get-tuple-element.57), channel_id=1, source_target_pairs={{0,2},{2,4},{4,6},{6,8},{8,10},{10,12},{12,14},{14,16},{16,18},{18... | collective-permute-start | bytes 4976648 | tf_op jit(solution)/shard_map/coef/ppermute | solution.py:382
  15.0 41.5 %collective-permute-start.3 = (f32[9,72,640]{2,1,0:T(8,128)}, f32[9,72,640]{2,1,0:T(8,128)}, u32[]{:S(2)}, u32[]{:S(2)}) collective-permute-start(f32[9,72,640]{2,1,0:T(8,128)} %get-tuple-element.58), channel_id=1, source_target_pairs={{2,0},{4,2},{6,4},{8,6},{10,8},{12,10},{14,12},{16,14},{18,16},{20... | collective-permute-start | bytes 4976648 | tf_op jit(solution)/shard_map/coef/ppermute | solution.py:383
  17.7 19.7 %copy-start.17 = (f32[144,144]{1,0:T(8,128)S(1)}, f32[144,144]{1,0:T(8,128)}, u32[]{:S(2)}) copy-start(f32[144,144]{1,0:T(8,128)} %refs_5_.1) | copy-start | bytes 248836
  17.7 19.7 %copy-start.19 = (f32[144,144]{1,0:T(8,128)S(1)}, f32[144,144]{1,0:T(8,128)}, u32[]{:S(2)}) copy-start(f32[144,144]{1,0:T(8,128)} %refs_6_.1) | copy-start | bytes 248836
  17.7 19.7 %copy-start.21 = (f32[144,144]{1,0:T(8,128)S(1)}, f32[144,144]{1,0:T(8,128)}, u32[]{:S(2)}) copy-start(f32[144,144]{1,0:T(8,128)} %refs_7_.1) | copy-start | bytes 248836
  17.7 19.7 %copy-start.24 = (bf16[640,640]{1,0:T(8,128)(2,1)S(1)}, bf16[640,640]{1,0:T(8,128)(2,1)}, u32[]{:S(2)}) copy-start(bf16[640,640]{1,0:T(8,128)(2,1)} %constant.26.clone.refs_4_.refs_8_.order) | copy-start | bytes 2457604
  34.5 21.9 %collective-permute-start.4 = (f32[24,16,640]{2,1,0:T(8,128)S(1)}, f32[24,16,640]{2,1,0:T(8,128)S(1)}, u32[]{:S(2)}, u32[]{:S(2)}) collective-permute-start(f32[24,16,640]{2,1,0:T(8,128)S(1)} %get-tuple-element.60), channel_id=1, source_target_pairs={{0,1},{1,0},{2,3},{3,2},{4,5},{5,4},{6,7},{7,6},{8,9},{9,8},{10,11... | collective-permute-start | bytes 2949128 | tf_op jit(solution)/shard_map/mix/ppermute | solution.py:425
  34.8 42.8 %collective-permute-start.7 = (f32[24,16,640]{2,1,0:T(8,128)}, f32[24,16,640]{2,1,0:T(8,128)}, u32[]{:S(2)}, u32[]{:S(2)}) collective-permute-start(f32[24,16,640]{2,1,0:T(8,128)} %get-tuple-element.64), channel_id=1, source_target_pairs={{0,1},{1,0},{2,3},{3,2},{4,5},{5,4},{6,7},{7,6},{8,9},{9,8},{10,11... | collective-permute-start | bytes 2949128 | tf_op jit(solution)/shard_map/mix/ppermute | solution.py:425
  38.8 17.7 %copy-start.1 = (f32[16,72,640]{2,1,0:T(8,128)S(1)}, f32[16,72,640]{2,1,0:T(8,128)}, u32[]{:S(2)}) copy-start(f32[16,72,640]{2,1,0:T(8,128)} %get-tuple-element.56.refs_2_) | copy-start | bytes 8847364
  43.6 14.3 %copy-start.2 = (f32[2,8,2,16,640]{4,3,2,1,0:T(8,128)}, f32[2,8,2,16,640]{4,3,2,1,0:T(8,128)S(1)}, u32[]{:S(2)}) copy-start(f32[2,8,2,16,640]{4,3,2,1,0:T(8,128)S(1)} %get-tuple-element.59.refs_0_) | copy-start | bytes 3932164
  43.7 14.3 %copy-start.4 = (f32[2,8,2,16,640]{4,3,2,1,0:T(8,128)}, f32[2,8,2,16,640]{4,3,2,1,0:T(8,128)S(1)}, u32[]{:S(2)}) copy-start(f32[2,8,2,16,640]{4,3,2,1,0:T(8,128)S(1)} %get-tuple-element.63.refs_0_) | copy-start | bytes 3932164
  43.7 14.3 %copy-start.7 = (f32[2,8,2,16,640]{4,3,2,1,0:T(8,128)}, f32[2,8,2,16,640]{4,3,2,1,0:T(8,128)S(1)}, u32[]{:S(2)}) copy-start(f32[2,8,2,16,640]{4,3,2,1,0:T(8,128)S(1)} %get-tuple-element.54.refs_0_) | copy-start | bytes 3932164
  43.7 14.3 %copy-start.9 = (f32[2,8,2,16,640]{4,3,2,1,0:T(8,128)}, f32[2,8,2,16,640]{4,3,2,1,0:T(8,128)S(1)}, u32[]{:S(2)}) copy-start(f32[2,8,2,16,640]{4,3,2,1,0:T(8,128)S(1)} %get-tuple-element.72.refs_0_) | copy-start | bytes 3932164
  43.7 14.3 %copy-start.25 = (f32[2,8,2,8,640]{4,3,2,1,0:T(8,128)}, f32[2,8,2,8,640]{4,3,2,1,0:T(8,128)S(1)}, u32[]{:S(2)}) copy-start(f32[2,8,2,8,640]{4,3,2,1,0:T(8,128)S(1)} %get-tuple-element.53.refs_0_) | copy-start | bytes 1966084
  58.0 27.1 %collective-permute-start.5 = (f32[10,2,16,640]{3,2,1,0:T(8,128)}, f32[10,2,16,640]{3,2,1,0:T(8,128)}, u32[]{:S(2)}, u32[]{:S(2)}) collective-permute-start(f32[10,2,16,640]{3,2,1,0:T(8,128)} %get-tuple-element.61), channel_id=1, source_target_pairs={{0,2},{2,4},{4,6},{6,8},{8,10},{10,12},{12,14},{14,16},{16,18},{18... | collective-permute-start | bytes 2457608 | tf_op jit(solution)/shard_map/edges/ppermute | solution.py:498
  62.6 22.5 %collective-permute-start.6 = (f32[10,2,16,640]{3,2,1,0:T(8,128)}, f32[10,2,16,640]{3,2,1,0:T(8,128)}, u32[]{:S(2)}, u32[]{:S(2)}) collective-permute-start(f32[10,2,16,640]{3,2,1,0:T(8,128)} %get-tuple-element.62), channel_id=1, source_target_pairs={{2,0},{4,2},{6,4},{8,6},{10,8},{12,10},{14,12},{16,14},{18,16},{20... | collective-permute-start | bytes 2457608 | tf_op jit(solution)/shard_map/edges/ppermute | solution.py:498
  62.6 36.0 %collective-permute-start.1 = (f32[24,16,640]{2,1,0:T(8,128)}, f32[24,16,640]{2,1,0:T(8,128)}, u32[]{:S(2)}, u32[]{:S(2)}) collective-permute-start(f32[24,16,640]{2,1,0:T(8,128)} %get-tuple-element.55), channel_id=1, source_target_pairs={{0,1},{1,0},{2,3},{3,2},{4,5},{5,4},{6,7},{7,6},{8,9},{9,8},{10,11... | collective-permute-start | bytes 2949128 | tf_op jit(solution)/shard_map/mix/ppermute | solution.py:425
  63.9 55.9 %collective-permute-start.11 = (f32[24,16,640]{2,1,0:T(8,128)}, f32[24,16,640]{2,1,0:T(8,128)}, u32[]{:S(2)}, u32[]{:S(2)}) collective-permute-start(f32[24,16,640]{2,1,0:T(8,128)} %get-tuple-element.73), channel_id=1, source_target_pairs={{0,1},{1,0},{2,3},{3,2},{4,5},{5,4},{6,7},{7,6},{8,9},{9,8},{10,11... | collective-permute-start | bytes 2949128 | tf_op jit(solution)/shard_map/mix/ppermute | solution.py:425
  80.5 25.9 %collective-permute-start.12 = (f32[10,2,16,640]{3,2,1,0:T(8,128)S(1)}, f32[10,2,16,640]{3,2,1,0:T(8,128)S(1)}, u32[]{:S(2)}, u32[]{:S(2)}) collective-permute-start(f32[10,2,16,640]{3,2,1,0:T(8,128)S(1)} %get-tuple-element.74), channel_id=1, source_target_pairs={{0,2},{2,4},{4,6},{6,8},{8,10},{10,12},{12,14},{14,16},{16,18},{18... | collective-permute-start | bytes 2457608 | tf_op jit(solution)/shard_map/edges/ppermute | solution.py:498
  85.1 21.2 %collective-permute-start.13 = (f32[10,2,16,640]{3,2,1,0:T(8,128)S(1)}, f32[10,2,16,640]{3,2,1,0:T(8,128)S(1)}, u32[]{:S(2)}, u32[]{:S(2)}) collective-permute-start(f32[10,2,16,640]{3,2,1,0:T(8,128)S(1)} %get-tuple-element.75), channel_id=1, source_target_pairs={{2,0},{4,2},{6,4},{8,6},{10,8},{12,10},{14,12},{16,14},{18,16},{20... | collective-permute-start | bytes 2457608 | tf_op jit(solution)/shard_map/edges/ppermute | solution.py:498
  85.3 13.4 %copy-start.8 = (f32[2,8,2,16,640]{4,3,2,1,0:T(8,128)S(1)}, f32[2,8,2,16,640]{4,3,2,1,0:T(8,128)}, u32[]{:S(2)}) copy-start(f32[2,8,2,16,640]{4,3,2,1,0:T(8,128)} %copy-done.7) | copy-start | bytes 3932164
  100.2 37.4 %collective-permute-start.8 = (f32[24,8,640]{2,1,0:T(8,128)S(1)}, f32[24,8,640]{2,1,0:T(8,128)S(1)}, u32[]{:S(2)}, u32[]{:S(2)}) collective-permute-start(f32[24,8,640]{2,1,0:T(8,128)S(1)} %get-tuple-element.69), channel_id=1, source_target_pairs={{0,1},{1,0},{2,3},{3,2},{4,5},{5,4},{6,7},{7,6},{8,9},{9,8},{10,11... | collective-permute-start | bytes 1474568 | tf_op jit(solution)/shard_map/ppermute | solution.py:425
  102.4 23.3 %collective-permute-start.9 = (f32[10,2,16,640]{3,2,1,0:T(8,128)S(1)}, f32[10,2,16,640]{3,2,1,0:T(8,128)S(1)}, u32[]{:S(2)}, u32[]{:S(2)}) collective-permute-start(f32[10,2,16,640]{3,2,1,0:T(8,128)S(1)} %get-tuple-element.70), channel_id=1, source_target_pairs={{0,2},{2,4},{4,6},{6,8},{8,10},{10,12},{12,14},{14,16},{16,18},{18... | collective-permute-start | bytes 2457608 | tf_op jit(solution)/shard_map/edges/ppermute | solution.py:498
  106.3 19.8 %collective-permute-start.10 = (f32[10,2,16,640]{3,2,1,0:T(8,128)S(1)}, f32[10,2,16,640]{3,2,1,0:T(8,128)S(1)}, u32[]{:S(2)}, u32[]{:S(2)}) collective-permute-start(f32[10,2,16,640]{3,2,1,0:T(8,128)S(1)} %get-tuple-element.71), channel_id=1, source_target_pairs={{2,0},{4,2},{6,4},{8,6},{10,8},{12,10},{14,12},{16,14},{18,16},{20... | collective-permute-start | bytes 2457608 | tf_op jit(solution)/shard_map/edges/ppermute | solution.py:498
  106.3 13.4 %copy-start.10 = (f32[2,8,2,16,640]{4,3,2,1,0:T(8,128)S(1)}, f32[2,8,2,16,640]{4,3,2,1,0:T(8,128)}, u32[]{:S(2)}) copy-start(f32[2,8,2,16,640]{4,3,2,1,0:T(8,128)} %copy-done.9) | copy-start | bytes 3932164
  121.1 22.7 %collective-permute-start.16 = (f32[10,2,16,640]{3,2,1,0:T(8,128)S(1)}, f32[10,2,16,640]{3,2,1,0:T(8,128)S(1)}, u32[]{:S(2)}, u32[]{:S(2)}) collective-permute-start(f32[10,2,16,640]{3,2,1,0:T(8,128)S(1)} %get-tuple-element.84), channel_id=1, source_target_pairs={{0,2},{2,4},{4,6},{6,8},{8,10},{10,12},{12,14},{14,16},{16,18},{18... | collective-permute-start | bytes 2457608 | tf_op jit(solution)/shard_map/edges/ppermute | solution.py:498
  125.8 24.9 %collective-permute-start.17 = (f32[10,2,16,640]{3,2,1,0:T(8,128)S(1)}, f32[10,2,16,640]{3,2,1,0:T(8,128)S(1)}, u32[]{:S(2)}, u32[]{:S(2)}) collective-permute-start(f32[10,2,16,640]{3,2,1,0:T(8,128)S(1)} %get-tuple-element.85), channel_id=1, source_target_pairs={{2,0},{4,2},{6,4},{8,6},{10,8},{12,10},{14,12},{16,14},{18,16},{20... | collective-permute-start | bytes 2457608 | tf_op jit(solution)/shard_map/edges/ppermute | solution.py:498
  126.1 11.5 %copy-start.26 = (f32[2,8,2,8,640]{4,3,2,1,0:T(8,128)S(1)}, f32[2,8,2,8,640]{4,3,2,1,0:T(8,128)}, u32[]{:S(2)}) copy-start(f32[2,8,2,8,640]{4,3,2,1,0:T(8,128)} %copy-done.25) | copy-start | bytes 1966084
  137.7 24.4 %collective-permute-start.14 = (f32[10,2,8,640]{3,2,1,0:T(8,128)S(1)}, f32[10,2,8,640]{3,2,1,0:T(8,128)S(1)}, u32[]{:S(2)}, u32[]{:S(2)}) collective-permute-start(f32[10,2,8,640]{3,2,1,0:T(8,128)S(1)} %get-tuple-element.82), channel_id=1, source_target_pairs={{0,2},{2,4},{4,6},{6,8},{8,10},{10,12},{12,14},{14,16},{16,18},{18... | collective-permute-start | bytes 1228808 | tf_op jit(solution)/shard_map/edges/ppermute | solution.py:498
  139.2 22.9 %collective-permute-start.15 = (f32[10,2,8,640]{3,2,1,0:T(8,128)S(1)}, f32[10,2,8,640]{3,2,1,0:T(8,128)S(1)}, u32[]{:S(2)}, u32[]{:S(2)}) collective-permute-start(f32[10,2,8,640]{3,2,1,0:T(8,128)S(1)} %get-tuple-element.83), channel_id=1, source_target_pairs={{2,0},{4,2},{6,4},{8,6},{10,8},{12,10},{14,12},{16,14},{18,16},{20... | collective-permute-start | bytes 1228808 | tf_op jit(solution)/shard_map/edges/ppermute | solution.py:498
  (14 other events, 79.7 us)

commit v3 on v2

--- a/solution.py
+++ b/solution.py
@@ -179,7 +179,14 @@
                 out[0, side, var] = more[0, side, var] + total[first : first + size, place]
 
 
-def coef_kernel(own, padded, lons, halo, tiles, sea, rough, order, _, coef, first, last, seas, roughs, lines, values, sems):
+def even_tile():
+    return lax.axis_index("tile") % 2 == 0
+
+
+def coef_kernel(own, padded, lons, halo, tiles, sea, rough, order, _, coef, near, far, *scratch):
+    seas, roughs, lines, values, sems = scratch
+    even = even_tile()
+    odd = jnp.logical_not(even)
     arriving = []
     for j in range(tiles):
         for source, held in ((sea, seas), (rough, roughs)):
@@ -192,10 +199,18 @@
     size = lons // COEF_GROUPS
     leaving = []
 
-    def leave(source, target):
-        copy = pltpu.make_async_copy(source, target, sems.at[len(arriving) + len(leaving)])
-        copy.start()
-        leaving.append(copy)
+    def leave(source, *targets):
+        sem = sems.at[len(arriving) + len(leaving)]
+        copies = [pltpu.make_async_copy(source, target, sem) for target in targets]
+        leaving.append(copies)
+        act(copies, "start")
+
+    def act(copies, what):
+        if len(copies) == 1:
+            getattr(copies[0], what)()
+        else:
+            pl.when(even)(getattr(copies[0], what))
+            pl.when(odd)(getattr(copies[1], what))
 
     for group in range(COEF_GROUPS):
         for at in range(size):
@@ -212,12 +227,13 @@
         leave(values.at[start:stop], coef.at[start:stop])
         if start < halo:
             until = min(stop, halo)
-            leave(values.at[start:until], first.at[start:until])
+            leave(values.at[start:until], far.at[start:until], near.at[start:until])
         if stop > lons - halo:
             since = max(start, lons - halo)
-            leave(values.at[since:stop], last.at[since - (lons - halo) : stop - (lons - halo)])
-    for copy in leaving:
-        copy.wait()
+            place = slice(since - (lons - halo), stop - (lons - halo))
+            leave(values.at[since:stop], near.at[place], far.at[place])
+    for copies in leaving:
+        act(copies, "wait")
 
 
 def mixed_at(lons, sums, lon, var):
@@ -230,15 +246,21 @@
 
 
 def edge_kernel(lons, halo, parts, passed, *refs):
-    sums, coef, (first, last, token) = refs[:parts], refs[parts], refs[parts + 4 + passed : parts + 7 + passed]
+    sums, coef, (near, far, token) = refs[:parts], refs[parts], refs[parts + 4 + passed : parts + 7 + passed]
     token[...] = jnp.zeros_like(token)
-    for lon in range(lons):
-        for var in range(2):
-            value = coef[lon] * mixed_at(lons, sums, lon, var)
-            if lon < halo:
-                first[lon, var] = value
-            if lon >= lons - halo:
-                last[lon - (lons - halo), var] = value
+
+    def give(first, last):
+        for lon in range(lons):
+            for var in range(2):
+                value = coef[lon] * mixed_at(lons, sums, lon, var)
+                if lon < halo:
+                    first[lon, var] = value
+                if lon >= lons - halo:
+                    last[lon - (lons - halo), var] = value
+
+    even = even_tile()
+    pl.when(even)(lambda: give(far, near))
+    pl.when(jnp.logical_not(even))(lambda: give(near, far))
 
 
 def neighbours(tiles, lane):
@@ -249,7 +271,7 @@
     return [line[j] + line[j + 2] for j in range(count)]
 
 
-def diffuse(lons, lats, sums, coef, before, after, coef_before, coef_after, rates, weighted, square):
+def diffuse(lons, lats, sums, coef, near, far, coef_near, coef_far, rates, weighted, square):
     halo = PASSES
     tiles = lats // LANES
     lane = lax.broadcasted_iota(jnp.int32, (ROWS, LANES), 1)
@@ -259,12 +281,18 @@
         square[halo + lon] = scale * scale
         for var in range(2):
             weighted[0][halo + lon, var] = scale * mixed_at(lons, sums, lon, var)
-    for lon in range(halo):
-        weighted[0][lon] = before[lon]
-        weighted[0][halo + lons + lon] = after[lon]
-    for lon in range(halo - 1):
-        square[1 + lon] = coef_before[lon] * coef_before[lon]
-        square[halo + lons + lon] = coef_after[lon] * coef_after[lon]
+
+    def sides(before, after, coef_before, coef_after):
+        for lon in range(halo):
+            weighted[0][lon] = before[lon]
+            weighted[0][halo + lons + lon] = after[lon]
+        for lon in range(halo - 1):
+            square[1 + lon] = coef_before[lon] * coef_before[lon]
+            square[halo + lons + lon] = coef_after[lon] * coef_after[lon]
+
+    even = even_tile()
+    pl.when(even)(lambda: sides(far, near, coef_far, coef_near))
+    pl.when(jnp.logical_not(even))(lambda: sides(near, far, coef_near, coef_far))
 
     for section in range(PASSES):
         source, target = weighted[section % 2], weighted[(section + 1) % 2]
@@ -292,11 +320,11 @@
 
 def diffuse_kernel(lons, lats, parts, *refs):
     sums, rest = refs[:parts], refs[parts:]
-    coef, before, after, coef_before, coef_after, rates, back, _, _, out, token, *rest = rest
+    coef, near, far, coef_near, coef_far, rates, back, _, _, out, token, *rest = rest
     *weighted, square, lines = rest
     tiles = lats // LANES
     token[...] = jnp.zeros_like(token)
-    diffuse(lons, lats, sums, coef, before, after, coef_before, coef_after, rates, weighted, square)
+    diffuse(lons, lats, sums, coef, near, far, coef_near, coef_far, rates, weighted, square)
 
     count = ROWS * 2 * lons
     for lon in range(lons):
@@ -356,10 +384,15 @@
     back = jnp.asarray(order.T, jnp.bfloat16)
     order = jnp.asarray(order, jnp.bfloat16)
 
-    up = [(i, (i + 1) % tile_count) for i in range(tile_count)]
-    down = [(j, i) for i, j in up]
+    def swaps(first):
+        pairs = [(i, (i + 1) % tile_count) for i in range(first, tile_count, 2)]
+        return pairs + [(j, i) for i, j in pairs]
+
+    def exchange(near, far):
+        return lax.ppermute(near, "tile", swaps(0)), lax.ppermute(far, "tile", swaps(1))
+
     with jax.named_scope("coef"):
-        coef, first, last = pl.pallas_call(
+        coef, near, far = pl.pallas_call(
             functools.partial(coef_kernel, own, padded, lons, halo - 1, tiles),
             out_shape=[
                 jax.ShapeDtypeStruct((lons, padded, lats), f32),
@@ -379,8 +412,7 @@
             cost_estimate=spent(10),
             name="coef",
         )(land_sea.reshape(own * lons, lats), roughness.reshape(own * lons, lats), order, rows)
-        coef_before = lax.ppermute(last, "tile", up)
-        coef_after = lax.ppermute(first, "tile", down)
+        coef_near, coef_far = exchange(near, far)
 
     half = lons // 2
     shape = (levels, own, padded, lons, tiles, lev_count)
@@ -480,7 +512,7 @@
         halo_shape = jax.ShapeDtypeStruct((halo, 2, count * ROWS, lats), f32)
         fixed = [jax.ShapeDtypeStruct(array.shape, array.dtype) for array in passed]
         with jax.named_scope("edges"):
-            first, last, token, *passed = pl.pallas_call(
+            near, far, token, *passed = pl.pallas_call(
                 functools.partial(edge_kernel, lons, halo, len(sums), len(passed)),
                 grid=(count,),
                 out_shape=[halo_shape, halo_shape, token_shape, *fixed],
@@ -494,15 +526,14 @@
                 compiler_params=params(12),
                 cost_estimate=spent(2),
                 name="edges",
-            )(*sums, coef, coef_before, coef_after, token, *passed)
-            return lax.ppermute(last, "tile", up), lax.ppermute(first, "tile", down), token, passed
-
-    def diffusion(c, before, after, result, token):
+            )(*sums, coef, coef_near, coef_far, token, *passed)
+            return *exchange(near, far), token, passed
+
+    def diffusion(c, near, far, result, token):
         sums = [kept[c]] + received[c]
         count, start = chunks[c], starts[c]
-        fixed = lambda i: (0, 0, i, 0)
         level = lambda i: (0, start + i, 0)
-        operands = [*sums, coef, before, after, coef_before, coef_after, rates, back, token, result]
+        operands = [*sums, coef, near, far, coef_near, coef_far, rates, back, token, result]
         with jax.named_scope("diffusion"):
             return pl.pallas_call(
                 functools.partial(diffuse_kernel, lons, lats, len(sums)),
@@ -510,7 +541,7 @@
                 out_shape=[jax.ShapeDtypeStruct((own * 2 * lons, lats), f32), token_shape],
                 in_specs=sum_specs(len(sums))
                 + [pl.BlockSpec((lons, ROWS, lats), level)]
-                + [pl.BlockSpec((halo, 2, ROWS, lats), fixed)] * 2
+                + [pl.BlockSpec((halo, 2, ROWS, lats), lambda i: (0, 0, i, 0))] * 2
                 + [pl.BlockSpec((halo - 1, ROWS, lats), level)] * 2
                 + [pl.BlockSpec((PASSES, ROWS, LANES), level), whole(lats, lats), hidden, hidden],
                 out_specs=[pl.BlockSpec((ROWS * 2 * lons, lats), lambda i: (start + i, 0)), token_spec],
@@ -528,12 +559,12 @@
 
     waiting = None
     for c in range(len(chunks)):
-        before, after, token, passed = edges(c, token, sent[final] if c == final - 2 else [])
+        near, far, token, passed = edges(c, token, sent[final] if c == final - 2 else [])
         if c == final - 2:
             received[final] = send(passed)
         if waiting is not None:
             result, token = diffusion(c - 1, *waiting, result, token)
-        waiting = (before, after)
+        waiting = (near, far)
     result, _ = diffusion(len(chunks) - 1, *waiting, result, token)
     return result.reshape(own, 2, lons, lats)
 

time: 169 us -> 172 us (1.018)
  the two profiles are of different devices: /device:TPU:25 before, /device:TPU:1 now
where the time goes in v3:
time: 172 us; the launch traced here: 171 us
  Pallas kernels  89.4 us (52%)
  starting transfers between devices  37.6 us (22%)
  waiting for transfers between devices  34.1 us (20%)
  local copies, waits for them, and re-layouts  9.66 us (6%)
    pallas_call x5, Pallas kernels, diffusion(): pl.pallas_call(functools.partial(diffuse_kernel, lons, lats, len(sums)),...  53.3 us
    ppermute x6, starting transfers between devices, exchange(): lax.ppermute(near, 'tile', swaps(0))  30.4 us
    ppermute x5, waiting for transfers between devices, send(): lax.ppermute(array, 'lev', along(shift + 1))  21.3 us
    pallas_call x1, Pallas kernels, on_device(): pl.pallas_call(functools.partial(mix_kernel, shape, offsets), grid=(half...  16.9 us
    ppermute x6, waiting for transfers between devices, exchange(): lax.ppermute(far, 'tile', swaps(1))  12.1 us
    pallas_call x1, Pallas kernels, on_device(): pl.pallas_call(functools.partial(coef_kernel, own, padded, lons, halo - 1...  8.16 us
    unnamed x56, local copies, waits for them, and re-layouts  6.67 us
    pallas_call x5, Pallas kernels, edges(): pl.pallas_call(functools.partial(edge_kernel, lons, halo, len(sums), len(...  6.16 us
  transfers between devices with their start and end apart: 18, of which 6 were waited for; matrix products, arithmetic and copies ran while one was open for 0% of the time, Pallas kernels for 48%

profile of v3, /device:TPU:1, one launch (start us, length us, event | category | flops | bytes accessed | tf_op | source)
XLA Modules:
  0.0 171.2 jit_solution(8261797447785932044)
XLA Ops:
  0.0 2.8 %slice_bitcast_fusion._ = f32[72,8,640]{2,1,0:T(8,128)} fusion(f32[72,2,16,640]{3,2,1,0:T(8,128)} %param.10), kind=kLoop, calls=%fused_computation | loop fusion | bytes 2949120 | tf_op jit(solution)/shard_map/raw/squeeze | solution.py:377
  2.8 2.1 %collective-permute-start = (f32[72,8,640]{2,1,0:T(8,128)}, f32[72,8,640]{2,1,0:T(8,128)S(1)}, u32[]{:S(2)}, u32[]{:S(2)}) collective-permute-start(f32[72,8,640]{2,1,0:T(8,128)} %slice_bitcast_fusion._), channel_id=1, source_target_pairs={{0,1},{1,0},{2,3},{3,2},{4,5},{5,4},{6,7},{7,6},{8,9},{9,8},{10,11... | collective-permute-start | bytes 4423688 | tf_op jit(solution)/shard_map/raw/ppermute | solution.py:378
  4.9 8.2 %coef.1 = (f32[16,72,640]{2,1,0:T(8,128)}, f32[9,72,640]{2,1,0:T(8,128)}, f32[9,72,640]{2,1,0:T(8,128)}) custom-call(s32[1152,640]{1,0:T(8,128)} %bitcast.17, f32[1152,640]{1,0:T(8,128)} %bitcast.18, bf16[640,640]{1,0:T(8,128)(2,1)S(1)} %copy-done.23, f32[72,8,640]{2,1,0:T(8,128)} %slice_bitcast_fusion._), custom_call_target="tpu_custom_call" | custom-call | flops 11530000384 | bytes 1024 | tf_op jit(solution)/shard_map/coef/coef/pallas_call | solution.py:395
  13.0 1.0 collective-permute-start.2
  14.0 1.2 collective-permute-start.3
  15.3 2.7 %copy-done.13 = f32[72,2,16,640]{3,2,1,0:T(8,128)S(1)} copy-done((f32[72,2,16,640]{3,2,1,0:T(8,128)S(1)}, f32[72,2,16,640]{3,2,1,0:T(8,128)}, u32[]{:S(2)}) %copy-start.13) | copy-done | bytes 5898264
  18.0 16.9 %mix.1 = (f32[2,8,2,16,640]{4,3,2,1,0:T(8,128)S(1)}, f32[2,8,2,16,640]{4,3,2,1,0:T(8,128)S(1)}, f32[2,8,2,16,640]{4,3,2,1,0:T(8,128)S(1)}, f32[2,8,2,16,640]{4,3...) custom-call(s32[2]{0:T(128)S(1)} %pad_add_fusion.at, ...), custom_call_target="tpu_custom_call" | custom-call | flops 23060000768 | bytes 1024 | tf_op jit(solution)/shard_map/mix/mix/pallas_call | solution.py:425
  35.2 1.2 collective-permute-start.7
  37.2 1.2 copy-done.14
  38.4 1.4 copy-done.15
  39.8 4.9 %raw.1 = (f32[2,8,2,16,640]{4,3,2,1,0:T(8,128)S(1)}, f32[2,8,2,16,640]{4,3,2,1,0:T(8,128)S(1)}, f32[2,8,2,16,640]{4,3,2,1,0:T(8,128)S(1)}, f32[2,8,2,16,640]{4,3,2,1,0:T(8,128)S(1)}, f32[2,8,2,8,640]{4,3,2,1,0:T(8,128)S(1)}) custom-call(s32[2]{0:T(128)S(1)} %pad_add_fusion.at, ...), custom_call_target="tpu_custom_call", output_to_operand_aliasing={{0}: (10, {}), {1}: (11, {}), {2}: (12, {}), {3}: (13, {}),... | custom-call | flops 6918000128 | bytes 1024 | tf_op jit(solution)/shard_map/raw/raw/pallas_call | solution.py:463
  44.7 10.9 %collective-permute-done.4.refs_1_ = f32[24,16,640]{2,1,0:T(8,128)S(1)} collective-permute-done((f32[24,16,640]{2,1,0:T(8,128)S(1)}, f32[24,16,640]{2,1,0:T(8,128)S(1)}, u32[]{:S(2)}, u32[]{:S(2)}) %collective-permute-start.4) | collective-permute-done | bytes 983072 | tf_op jit(solution)/shard_map/mix/ppermute | solution.py:457
  55.7 1.5 edges.5
  57.3 7.6 %collective-permute-start.5 = (f32[10,2,16,640]{3,2,1,0:T(8,128)}, f32[10,2,16,640]{3,2,1,0:T(8,128)}, u32[]{:S(2)}, u32[]{:S(2)}) collective-permute-start(f32[10,2,16,640]{3,2,1,0:T(8,128)} %get-tuple-element.61), channel_id=1, source_target_pairs={{0,2},{4,6},{8,10},{12,14},{16,18},{20,22},{24,26},{28,30},{2,0},{... | collective-permute-start | bytes 2457608 | tf_op jit(solution)/shard_map/edges/ppermute | solution.py:392
  65.1 1.2 collective-permute-start.11
  66.5 10.4 %collective-permute-done.7.refs_1_ = f32[24,16,640]{2,1,0:T(8,128)} collective-permute-done((f32[24,16,640]{2,1,0:T(8,128)}, f32[24,16,640]{2,1,0:T(8,128)}, u32[]{:S(2)}, u32[]{:S(2)}) %collective-permute-start.7) | collective-permute-done | bytes 983072 | tf_op jit(solution)/shard_map/mix/ppermute | solution.py:457
  76.8 1.3 copy-done.5
  78.2 1.6 edges.6
  79.7 7.6 %collective-permute-start.12 = (f32[10,2,16,640]{3,2,1,0:T(8,128)S(1)}, f32[10,2,16,640]{3,2,1,0:T(8,128)S(1)}, u32[]{:S(2)}, u32[]{:S(2)}) collective-permute-start(f32[10,2,16,640]{3,2,1,0:T(8,128)S(1)} %get-tuple-element.74), channel_id=1, source_target_pairs={{0,2},{4,6},{8,10},{12,14},{16,18},{20,22},{24,26},{28,30},{2,0},{... | collective-permute-start | bytes 2457608 | tf_op jit(solution)/shard_map/edges/ppermute | solution.py:392
  87.5 11.7 %diffusion.5 = (f32[2304,640]{1,0:T(8,128)}, f32[8,128]{1,0:T(8,128)S(1)}) custom-call(f32[2,8,2,16,640]{4,3,2,1,0:T(8,128)S(1)} %copy-done.3, f32[24,16,640]{2,1,0:T(8,128)S(1)} %copy-done.12, f32[16,72,640]{2,1,0:T(8,128)S(1)} %copy-done.1, f32[10,2,16,640]{3,2,1,0:T(8,128)} %collective-permute-done.5.refs_3_, ...), custom_call_target="tpu_custom_call" | custom-call | flops 12682999808 | bytes 1024 | tf_op jit(solution)/shard_map/diffusion/diffusion/pallas_call | solution.py:538
  99.2 1.5 edges.7
  100.7 1.0 collective-permute-start.8
  101.7 5.8 %collective-permute-start.9 = (f32[10,2,16,640]{3,2,1,0:T(8,128)S(1)}, f32[10,2,16,640]{3,2,1,0:T(8,128)S(1)}, u32[]{:S(2)}, u32[]{:S(2)}) collective-permute-start(f32[10,2,16,640]{3,2,1,0:T(8,128)S(1)} %get-tuple-element.70), channel_id=1, source_target_pairs={{0,2},{4,6},{8,10},{12,14},{16,18},{20,22},{24,26},{28,30},{2,0},{... | collective-permute-start | bytes 2457608 | tf_op jit(solution)/shard_map/edges/ppermute | solution.py:392
  107.5 0.7 collective-permute-done.13.refs_4_
  108.2 11.8 %diffusion.6 = (f32[2304,640]{1,0:T(8,128)}, f32[8,128]{1,0:T(8,128)S(1)}) custom-call(f32[2,8,2,16,640]{4,3,2,1,0:T(8,128)S(1)} %copy-done.6, f32[24,16,640]{2,1,0:T(8,128)} %collective-permute-done.7.refs_1_, f32[16,72,640]{2,1,0:T(8,128)S(1)} %copy-done.1, ...), custom_call_target="tpu_custom_call", output_to_operand_aliasing={{0}: (10, {})} | custom-call | flops 12682999808 | bytes 1024 | tf_op jit(solution)/shard_map/diffusion/diffusion/pallas_call | solution.py:538
  120.0 1.4 edges.8
  121.5 6.5 %collective-permute-start.16 = (f32[10,2,16,640]{3,2,1,0:T(8,128)S(1)}, f32[10,2,16,640]{3,2,1,0:T(8,128)S(1)}, u32[]{:S(2)}, u32[]{:S(2)}) collective-permute-start(f32[10,2,16,640]{3,2,1,0:T(8,128)S(1)} %get-tuple-element.84), channel_id=1, source_target_pairs={{0,2},{4,6},{8,10},{12,14},{16,18},{20,22},{24,26},{28,30},{2,0},{... | collective-permute-start | bytes 2457608 | tf_op jit(solution)/shard_map/edges/ppermute | solution.py:392
  128.3 11.5 %diffusion.7 = (f32[2304,640]{1,0:T(8,128)}, f32[8,128]{1,0:T(8,128)S(1)}) custom-call(f32[2,8,2,16,640]{4,3,2,1,0:T(8,128)S(1)} %copy-done.8, f32[24,16,640]{2,1,0:T(8,128)} %collective-permute-done.1.refs_1_, f32[16,72,640]{2,1,0:T(8,128)S(1)} %copy-done.1, ...), custom_call_target="tpu_custom_call", output_to_operand_aliasing={{0}: (10, {})} | custom-call | flops 12682999808 | bytes 1024 | tf_op jit(solution)/shard_map/diffusion/diffusion/pallas_call | solution.py:538
  140.0 1.9 %collective-permute-start.14 = (f32[10,2,8,640]{3,2,1,0:T(8,128)S(1)}, f32[10,2,8,640]{3,2,1,0:T(8,128)S(1)}, u32[]{:S(2)}, u32[]{:S(2)}) collective-permute-start(f32[10,2,8,640]{3,2,1,0:T(8,128)S(1)} %get-tuple-element.82), channel_id=1, source_target_pairs={{0,2},{4,6},{8,10},{12,14},{16,18},{20,22},{24,26},{28,30},{2,0},{... | collective-permute-start | bytes 1228808 | tf_op jit(solution)/shard_map/edges/ppermute | solution.py:392
  141.9 11.0 %collective-permute-done.17.refs_4_ = f32[10,2,16,640]{3,2,1,0:T(8,128)S(1)} collective-permute-done((f32[10,2,16,640]{3,2,1,0:T(8,128)S(1)}, f32[10,2,16,640]{3,2,1,0:T(8,128)S(1)}, u32[]{:S(2)}, u32[]{:S(2)}) %collective-permute-start.17) | collective-permute-done | bytes 819232 | tf_op jit(solution)/shard_map/edges/ppermute | solution.py:392
  152.9 11.5 %diffusion.8 = (f32[2304,640]{1,0:T(8,128)}, f32[8,128]{1,0:T(8,128)S(1)}) custom-call(f32[2,8,2,16,640]{4,3,2,1,0:T(8,128)S(1)} %copy-done.10, f32[24,16,640]{2,1,0:T(8,128)} %collective-permute-done.11.refs_1_, f32[16,72,640]{2,1,0:T(8,128)S(1)} %copy-done.1, ...), custom_call_target="tpu_custom_call", output_to_operand_aliasing={{0}: (10, {})} | custom-call | flops 12682999808 | bytes 1024 | tf_op jit(solution)/shard_map/diffusion/diffusion/pallas_call | solution.py:538
  164.4 6.9 %diffusion.9 = (f32[2304,640]{1,0:T(8,128)}, f32[8,128]{1,0:T(8,128)}) custom-call(f32[2,8,2,8,640]{4,3,2,1,0:T(8,128)S(1)} %copy-done.26, f32[24,8,640]{2,1,0:T(8,128)S(1)} %collective-permute-done.8.refs_1_, f32[16,72,640]{2,1,0:T(8,128)S(1)} %copy-done.1, f32[10,2,8,640]{3,2,1,0:T(8,128)S(1)} %collective-permute-done.14.refs_3_, ...), custom_call_target="tpu_custom_call", output_to_operand_aliasing={{0}: (10, {})} | custom-call | flops 12682999808 | bytes 1024 | tf_op jit(solution)/shard_map/diffusion/diffusion/pallas_call | solution.py:538
  (79 shorter events, 2.3 us)
Async XLA Ops:
  0.0 66.3 %copy-start = (s32[10,144]{1,0:T(8,128)S(1)}, s32[10,144]{1,0:T(8,128)}, u32[]{:S(2)}) copy-start(s32[10,144]{1,0:T(8,128)} %param.13) | copy-start | bytes 17284
  2.8 34.4 %collective-permute-start = (f32[72,8,640]{2,1,0:T(8,128)}, f32[72,8,640]{2,1,0:T(8,128)S(1)}, u32[]{:S(2)}, u32[]{:S(2)}) collective-permute-start(f32[72,8,640]{2,1,0:T(8,128)} %slice_bitcast_fusion._), channel_id=1, source_target_pairs={{0,1},{1,0},{2,3},{3,2},{4,5},{5,4},{6,7},{7,6},{8,9},{9,8},{10,11... | collective-permute-start | bytes 4423688 | tf_op jit(solution)/shard_map/raw/ppermute | solution.py:378
  13.0 42.6 %collective-permute-start.2 = (f32[9,72,640]{2,1,0:T(8,128)}, f32[9,72,640]{2,1,0:T(8,128)}, u32[]{:S(2)}, u32[]{:S(2)}) collective-permute-start(f32[9,72,640]{2,1,0:T(8,128)} %get-tuple-element.57), channel_id=1, source_target_pairs={{0,2},{4,6},{8,10},{12,14},{16,18},{20,22},{24,26},{28,30},{2,0},{... | collective-permute-start | bytes 4976648 | tf_op jit(solution)/shard_map/coef/ppermute | solution.py:392
  14.0 41.6 %collective-permute-start.3 = (f32[9,72,640]{2,1,0:T(8,128)}, f32[9,72,640]{2,1,0:T(8,128)}, u32[]{:S(2)}, u32[]{:S(2)}) collective-permute-start(f32[9,72,640]{2,1,0:T(8,128)} %get-tuple-element.58), channel_id=1, source_target_pairs={{2,4},{6,8},{10,12},{14,16},{18,20},{22,24},{26,28},{30,0},{4,2},{... | collective-permute-start | bytes 4976648 | tf_op jit(solution)/shard_map/coef/ppermute | solution.py:392
  18.0 20.4 %copy-start.17 = (f32[144,144]{1,0:T(8,128)S(1)}, f32[144,144]{1,0:T(8,128)}, u32[]{:S(2)}) copy-start(f32[144,144]{1,0:T(8,128)} %refs_5_.1) | copy-start | bytes 248836
  18.0 20.4 %copy-start.19 = (f32[144,144]{1,0:T(8,128)S(1)}, f32[144,144]{1,0:T(8,128)}, u32[]{:S(2)}) copy-start(f32[144,144]{1,0:T(8,128)} %refs_6_.1) | copy-start | bytes 248836
  18.0 20.4 %copy-start.21 = (f32[144,144]{1,0:T(8,128)S(1)}, f32[144,144]{1,0:T(8,128)}, u32[]{:S(2)}) copy-start(f32[144,144]{1,0:T(8,128)} %refs_7_.1) | copy-start | bytes 248836
  18.0 20.4 %copy-start.24 = (bf16[640,640]{1,0:T(8,128)(2,1)S(1)}, bf16[640,640]{1,0:T(8,128)(2,1)}, u32[]{:S(2)}) copy-start(bf16[640,640]{1,0:T(8,128)(2,1)} %constant.26.clone.refs_4_.refs_8_.order) | copy-start | bytes 2457604
  34.9 20.7 %collective-permute-start.4 = (f32[24,16,640]{2,1,0:T(8,128)S(1)}, f32[24,16,640]{2,1,0:T(8,128)S(1)}, u32[]{:S(2)}, u32[]{:S(2)}) collective-permute-start(f32[24,16,640]{2,1,0:T(8,128)S(1)} %get-tuple-element.60), channel_id=1, source_target_pairs={{0,1},{1,0},{2,3},{3,2},{4,5},{5,4},{6,7},{7,6},{8,9},{9,8},{10,11... | collective-permute-start | bytes 2949128 | tf_op jit(solution)/shard_map/mix/ppermute | solution.py:457
  35.2 41.6 %collective-permute-start.7 = (f32[24,16,640]{2,1,0:T(8,128)}, f32[24,16,640]{2,1,0:T(8,128)}, u32[]{:S(2)}, u32[]{:S(2)}) collective-permute-start(f32[24,16,640]{2,1,0:T(8,128)} %get-tuple-element.64), channel_id=1, source_target_pairs={{0,1},{1,0},{2,3},{3,2},{4,5},{5,4},{6,7},{7,6},{8,9},{9,8},{10,11... | collective-permute-start | bytes 2949128 | tf_op jit(solution)/shard_map/mix/ppermute | solution.py:457
  39.8 15.9 %copy-start.1 = (f32[16,72,640]{2,1,0:T(8,128)S(1)}, f32[16,72,640]{2,1,0:T(8,128)}, u32[]{:S(2)}) copy-start(f32[16,72,640]{2,1,0:T(8,128)} %get-tuple-element.56.refs_2_) | copy-start | bytes 8847364
  44.7 12.5 %copy-start.2 = (f32[2,8,2,16,640]{4,3,2,1,0:T(8,128)}, f32[2,8,2,16,640]{4,3,2,1,0:T(8,128)S(1)}, u32[]{:S(2)}) copy-start(f32[2,8,2,16,640]{4,3,2,1,0:T(8,128)S(1)} %get-tuple-element.59.refs_0_) | copy-start | bytes 3932164
  44.7 12.5 %copy-start.4 = (f32[2,8,2,16,640]{4,3,2,1,0:T(8,128)}, f32[2,8,2,16,640]{4,3,2,1,0:T(8,128)S(1)}, u32[]{:S(2)}) copy-start(f32[2,8,2,16,640]{4,3,2,1,0:T(8,128)S(1)} %get-tuple-element.63.refs_0_) | copy-start | bytes 3932164
  44.7 12.5 %copy-start.7 = (f32[2,8,2,16,640]{4,3,2,1,0:T(8,128)}, f32[2,8,2,16,640]{4,3,2,1,0:T(8,128)S(1)}, u32[]{:S(2)}) copy-start(f32[2,8,2,16,640]{4,3,2,1,0:T(8,128)S(1)} %get-tuple-element.54.refs_0_) | copy-start | bytes 3932164
  44.7 12.5 %copy-start.9 = (f32[2,8,2,16,640]{4,3,2,1,0:T(8,128)}, f32[2,8,2,16,640]{4,3,2,1,0:T(8,128)S(1)}, u32[]{:S(2)}) copy-start(f32[2,8,2,16,640]{4,3,2,1,0:T(8,128)S(1)} %get-tuple-element.72.refs_0_) | copy-start | bytes 3932164
  44.7 12.5 %copy-start.25 = (f32[2,8,2,8,640]{4,3,2,1,0:T(8,128)}, f32[2,8,2,8,640]{4,3,2,1,0:T(8,128)S(1)}, u32[]{:S(2)}) copy-start(f32[2,8,2,8,640]{4,3,2,1,0:T(8,128)S(1)} %get-tuple-element.53.refs_0_) | copy-start | bytes 1966084
  57.3 30.0 %collective-permute-start.5 = (f32[10,2,16,640]{3,2,1,0:T(8,128)}, f32[10,2,16,640]{3,2,1,0:T(8,128)}, u32[]{:S(2)}, u32[]{:S(2)}) collective-permute-start(f32[10,2,16,640]{3,2,1,0:T(8,128)} %get-tuple-element.61), channel_id=1, source_target_pairs={{0,2},{4,6},{8,10},{12,14},{16,18},{20,22},{24,26},{28,30},{2,0},{... | collective-permute-start | bytes 2457608 | tf_op jit(solution)/shard_map/edges/ppermute | solution.py:392
  64.8 22.5 %collective-permute-start.6 = (f32[10,2,16,640]{3,2,1,0:T(8,128)}, f32[10,2,16,640]{3,2,1,0:T(8,128)}, u32[]{:S(2)}, u32[]{:S(2)}) collective-permute-start(f32[10,2,16,640]{3,2,1,0:T(8,128)} %get-tuple-element.62), channel_id=1, source_target_pairs={{2,4},{6,8},{10,12},{14,16},{18,20},{22,24},{26,28},{30,0},{4,2},{... | collective-permute-start | bytes 2457608 | tf_op jit(solution)/shard_map/edges/ppermute | solution.py:392
  64.8 34.3 %collective-permute-start.1 = (f32[24,16,640]{2,1,0:T(8,128)}, f32[24,16,640]{2,1,0:T(8,128)}, u32[]{:S(2)}, u32[]{:S(2)}) collective-permute-start(f32[24,16,640]{2,1,0:T(8,128)} %get-tuple-element.55), channel_id=1, source_target_pairs={{0,1},{1,0},{2,3},{3,2},{4,5},{5,4},{6,7},{7,6},{8,9},{9,8},{10,11... | collective-permute-start | bytes 2949128 | tf_op jit(solution)/shard_map/mix/ppermute | solution.py:457
  65.1 55.0 %collective-permute-start.11 = (f32[24,16,640]{2,1,0:T(8,128)}, f32[24,16,640]{2,1,0:T(8,128)}, u32[]{:S(2)}, u32[]{:S(2)}) collective-permute-start(f32[24,16,640]{2,1,0:T(8,128)} %get-tuple-element.73), channel_id=1, source_target_pairs={{0,1},{1,0},{2,3},{3,2},{4,5},{5,4},{6,7},{7,6},{8,9},{9,8},{10,11... | collective-permute-start | bytes 2949128 | tf_op jit(solution)/shard_map/mix/ppermute | solution.py:457
  79.7 27.8 %collective-permute-start.12 = (f32[10,2,16,640]{3,2,1,0:T(8,128)S(1)}, f32[10,2,16,640]{3,2,1,0:T(8,128)S(1)}, u32[]{:S(2)}, u32[]{:S(2)}) collective-permute-start(f32[10,2,16,640]{3,2,1,0:T(8,128)S(1)} %get-tuple-element.74), channel_id=1, source_target_pairs={{0,2},{4,6},{8,10},{12,14},{16,18},{20,22},{24,26},{28,30},{2,0},{... | collective-permute-start | bytes 2457608 | tf_op jit(solution)/shard_map/edges/ppermute | solution.py:392
  87.3 20.9 %collective-permute-start.13 = (f32[10,2,16,640]{3,2,1,0:T(8,128)S(1)}, f32[10,2,16,640]{3,2,1,0:T(8,128)S(1)}, u32[]{:S(2)}, u32[]{:S(2)}) collective-permute-start(f32[10,2,16,640]{3,2,1,0:T(8,128)S(1)} %get-tuple-element.75), channel_id=1, source_target_pairs={{2,4},{6,8},{10,12},{14,16},{18,20},{22,24},{26,28},{30,0},{4,2},{... | collective-permute-start | bytes 2457608 | tf_op jit(solution)/shard_map/edges/ppermute | solution.py:392
  87.5 11.7 %copy-start.8 = (f32[2,8,2,16,640]{4,3,2,1,0:T(8,128)S(1)}, f32[2,8,2,16,640]{4,3,2,1,0:T(8,128)}, u32[]{:S(2)}) copy-start(f32[2,8,2,16,640]{4,3,2,1,0:T(8,128)} %copy-done.7) | copy-start | bytes 3932164
  100.7 39.1 %collective-permute-start.8 = (f32[24,8,640]{2,1,0:T(8,128)S(1)}, f32[24,8,640]{2,1,0:T(8,128)S(1)}, u32[]{:S(2)}, u32[]{:S(2)}) collective-permute-start(f32[24,8,640]{2,1,0:T(8,128)S(1)} %get-tuple-element.69), channel_id=1, source_target_pairs={{0,1},{1,0},{2,3},{3,2},{4,5},{5,4},{6,7},{7,6},{8,9},{9,8},{10,11... | collective-permute-start | bytes 1474568 | tf_op jit(solution)/shard_map/ppermute | solution.py:457
  101.7 26.3 %collective-permute-start.9 = (f32[10,2,16,640]{3,2,1,0:T(8,128)S(1)}, f32[10,2,16,640]{3,2,1,0:T(8,128)S(1)}, u32[]{:S(2)}, u32[]{:S(2)}) collective-permute-start(f32[10,2,16,640]{3,2,1,0:T(8,128)S(1)} %get-tuple-element.70), channel_id=1, source_target_pairs={{0,2},{4,6},{8,10},{12,14},{16,18},{20,22},{24,26},{28,30},{2,0},{... | collective-permute-start | bytes 2457608 | tf_op jit(solution)/shard_map/edges/ppermute | solution.py:392
  107.5 20.8 %collective-permute-start.10 = (f32[10,2,16,640]{3,2,1,0:T(8,128)S(1)}, f32[10,2,16,640]{3,2,1,0:T(8,128)S(1)}, u32[]{:S(2)}, u32[]{:S(2)}) collective-permute-start(f32[10,2,16,640]{3,2,1,0:T(8,128)S(1)} %get-tuple-element.71), channel_id=1, source_target_pairs={{2,4},{6,8},{10,12},{14,16},{18,20},{22,24},{26,28},{30,0},{4,2},{... | collective-permute-start | bytes 2457608 | tf_op jit(solution)/shard_map/edges/ppermute | solution.py:392
  108.2 11.8 %copy-start.10 = (f32[2,8,2,16,640]{4,3,2,1,0:T(8,128)S(1)}, f32[2,8,2,16,640]{4,3,2,1,0:T(8,128)}, u32[]{:S(2)}) copy-start(f32[2,8,2,16,640]{4,3,2,1,0:T(8,128)} %copy-done.9) | copy-start | bytes 3932164
  121.5 20.4 %collective-permute-start.16 = (f32[10,2,16,640]{3,2,1,0:T(8,128)S(1)}, f32[10,2,16,640]{3,2,1,0:T(8,128)S(1)}, u32[]{:S(2)}, u32[]{:S(2)}) collective-permute-start(f32[10,2,16,640]{3,2,1,0:T(8,128)S(1)} %get-tuple-element.84), channel_id=1, source_target_pairs={{0,2},{4,6},{8,10},{12,14},{16,18},{20,22},{24,26},{28,30},{2,0},{... | collective-permute-start | bytes 2457608 | tf_op jit(solution)/shard_map/edges/ppermute | solution.py:392
  128.0 24.9 %collective-permute-start.17 = (f32[10,2,16,640]{3,2,1,0:T(8,128)S(1)}, f32[10,2,16,640]{3,2,1,0:T(8,128)S(1)}, u32[]{:S(2)}, u32[]{:S(2)}) collective-permute-start(f32[10,2,16,640]{3,2,1,0:T(8,128)S(1)} %get-tuple-element.85), channel_id=1, source_target_pairs={{2,4},{6,8},{10,12},{14,16},{18,20},{22,24},{26,28},{30,0},{4,2},{... | collective-permute-start | bytes 2457608 | tf_op jit(solution)/shard_map/edges/ppermute | solution.py:392
  128.3 11.5 %copy-start.26 = (f32[2,8,2,8,640]{4,3,2,1,0:T(8,128)S(1)}, f32[2,8,2,8,640]{4,3,2,1,0:T(8,128)}, u32[]{:S(2)}) copy-start(f32[2,8,2,8,640]{4,3,2,1,0:T(8,128)} %copy-done.25) | copy-start | bytes 1966084
  140.0 24.4 %collective-permute-start.14 = (f32[10,2,8,640]{3,2,1,0:T(8,128)S(1)}, f32[10,2,8,640]{3,2,1,0:T(8,128)S(1)}, u32[]{:S(2)}, u32[]{:S(2)}) collective-permute-start(f32[10,2,8,640]{3,2,1,0:T(8,128)S(1)} %get-tuple-element.82), channel_id=1, source_target_pairs={{0,2},{4,6},{8,10},{12,14},{16,18},{20,22},{24,26},{28,30},{2,0},{... | collective-permute-start | bytes 1228808 | tf_op jit(solution)/shard_map/edges/ppermute | solution.py:392
  141.9 22.4 %collective-permute-start.15 = (f32[10,2,8,640]{3,2,1,0:T(8,128)S(1)}, f32[10,2,8,640]{3,2,1,0:T(8,128)S(1)}, u32[]{:S(2)}, u32[]{:S(2)}) collective-permute-start(f32[10,2,8,640]{3,2,1,0:T(8,128)S(1)} %get-tuple-element.83), channel_id=1, source_target_pairs={{2,4},{6,8},{10,12},{14,16},{18,20},{22,24},{26,28},{30,0},{4,2},{... | collective-permute-start | bytes 1228808 | tf_op jit(solution)/shard_map/edges/ppermute | solution.py:392
  (14 other events, 92.1 us)

commit v4 on v2

--- a/solution.py
+++ b/solution.py
@@ -375,7 +375,7 @@
                 pltpu.VMEM((lons, padded, lats), f32),
                 pltpu.SemaphoreType.DMA((2 * tiles + 3 * COEF_GROUPS,)),
             ],
-            compiler_params=params(53),
+            compiler_params=params(20),
             cost_estimate=spent(10),
             name="coef",
         )(land_sea.reshape(own * lons, lats), roughness.reshape(own * lons, lats), order, rows)

time: 169 us -> 175 us (1.036)
  local copies, waits for them, and re-layouts: 9.66 us -> 13.9 us
  waiting for transfers between devices: 40.5 us -> 42.7 us
    unnamed x56 -> x48, local copies, waits for them, and re-layouts: 6.67 us -> 10.9 us
    ppermute x5, starting transfers between devices: 5.26 us -> 3.29 us  [send(): lax.ppermute(array, 'lev', along(shift + 1))]
  transfers between devices with their start and end apart: 18 -> 18, of which waited for: 8 -> 8; matrix products, arithmetic and copies ran while one was open for 0% -> 0% of each run, Pallas kernels for 49% -> 47%
where the time goes in v4:
time: 175 us
  Pallas kernels  89.2 us (51%)
  waiting for transfers between devices  42.7 us (24%)
  starting transfers between devices  28.5 us (16%)
  local copies, waits for them, and re-layouts  13.9 us (8%)
    pallas_call x5, Pallas kernels, diffusion(): pl.pallas_call(functools.partial(diffuse_kernel, lons, lats, len(sums)),...  52.8 us
    ppermute x5, waiting for transfers between devices, send(): lax.ppermute(array, 'lev', along(shift + 1))  31.1 us
    ppermute x5, starting transfers between devices, edges(): lax.ppermute(last, 'tile', up)  20.8 us
    pallas_call x1, Pallas kernels, on_device(): pl.pallas_call(functools.partial(mix_kernel, shape, offsets), grid=(half...  16.8 us
    unnamed x48, local copies, waits for them, and re-layouts  10.9 us
    ppermute x5, waiting for transfers between devices, edges(): lax.ppermute(first, 'tile', down)  7.98 us
    pallas_call x1, Pallas kernels, on_device(): pl.pallas_call(functools.partial(coef_kernel, own, padded, lons, halo - 1...  7.92 us
    pallas_call x5, Pallas kernels, edges(): pl.pallas_call(functools.partial(edge_kernel, lons, halo, len(sums), len(...  6.07 us
  transfers between devices with their start and end apart: 18, of which 8 were waited for; matrix products, arithmetic and copies ran while one was open for 0% of the time, Pallas kernels for 47%

profile of v4, /device:TPU:25, one launch (start us, length us, event | category | flops | bytes accessed | tf_op | source)
XLA Modules:
  0.0 174.7 jit_solution(11009489233096985255)
XLA Ops:
  0.0 2.8 %slice_bitcast_fusion._ = f32[72,8,640]{2,1,0:T(8,128)} fusion(f32[72,2,16,640]{3,2,1,0:T(8,128)} %param.10), kind=kLoop, calls=%fused_computation | loop fusion | bytes 2949120 | tf_op jit(solution)/shard_map/raw/squeeze | solution.py:349
  2.8 1.2 collective-permute-start
  4.0 1.8 %copy-done.14 = f32[72,16,640]{2,1,0:T(8,128)S(1)} copy-done((f32[72,16,640]{2,1,0:T(8,128)S(1)}, f32[72,16,640]{2,1,0:T(8,128)}, u32[]{:S(2)}) %copy-start.14) | copy-done | bytes 2949144
  5.9 1.1 copy-done.19
  7.0 7.9 %coef.1 = (f32[16,72,640]{2,1,0:T(8,128)S(1)}, f32[9,72,640]{2,1,0:T(8,128)}, f32[9,72,640]{2,1,0:T(8,128)}) custom-call(s32[1152,640]{1,0:T(8,128)S(1)} %bitcast.12, f32[1152,640]{1,0:T(8,128)S(1)} %bitcast.13, bf16[640,640]{1,0:T(8,128)(2,1)S(1)} %copy-done.19, f32[72,8,640]{2,1,0:T(8,128)} %slice_bitcast_fusion._), custom_call_target="tpu_custom_call" | custom-call | flops 11530000384 | bytes 1024 | tf_op jit(solution)/shard_map/coef/coef/pallas_call | solution.py:362
  14.9 2.1 %collective-permute-start.2 = (f32[9,72,640]{2,1,0:T(8,128)}, f32[9,72,640]{2,1,0:T(8,128)}, u32[]{:S(2)}, u32[]{:S(2)}) collective-permute-start(f32[9,72,640]{2,1,0:T(8,128)} %get-tuple-element.57), channel_id=1, source_target_pairs={{0,2},{2,4},{4,6},{6,8},{8,10},{10,12},{12,14},{14,16},{16,18},{18... | collective-permute-start | bytes 4976648 | tf_op jit(solution)/shard_map/coef/ppermute | solution.py:382
  17.1 2.7 %copy-done.12 = f32[72,2,16,640]{3,2,1,0:T(8,128)S(1)} copy-done((f32[72,2,16,640]{3,2,1,0:T(8,128)S(1)}, f32[72,2,16,640]{3,2,1,0:T(8,128)}, u32[]{:S(2)}) %copy-start.12) | copy-done | bytes 5898264
  23.7 16.8 %mix.1 = (f32[2,8,2,16,640]{4,3,2,1,0:T(8,128)S(1)}, f32[2,8,2,16,640]{4,3,2,1,0:T(8,128)S(1)}, f32[2,8,2,16,640]{4,3,2,1,0:T(8,128)S(1)}, f32[2,8,2,16,640]{4,3...) custom-call(s32[2]{0:T(128)S(1)} %pad_add_fusion.at, ...), custom_call_target="tpu_custom_call" | custom-call | flops 23060000768 | bytes 1024 | tf_op jit(solution)/shard_map/mix/mix/pallas_call | solution.py:393
  40.8 1.2 collective-permute-start.7
  42.0 5.7 %raw.1 = (f32[2,8,2,16,640]{4,3,2,1,0:T(8,128)S(1)}, f32[2,8,2,16,640]{4,3,2,1,0:T(8,128)S(1)}, f32[2,8,2,16,640]{4,3,2,1,0:T(8,128)S(1)}, f32[2,8,2,16,640]{4,3,2,1,0:T(8,128)S(1)}, f32[2,8,2,8,640]{4,3,2,1,0:T(8,128)S(1)}) custom-call(s32[2]{0:T(128)S(1)} %pad_add_fusion.at, ...), custom_call_target="tpu_custom_call", output_to_operand_aliasing={{0}: (10, {}), {1}: (11, {}), {2}: (12, {}), {3}: (13, {}),... | custom-call | flops 6918000128 | bytes 1024 | tf_op jit(solution)/shard_map/raw/raw/pallas_call | solution.py:431
  47.8 14.5 %collective-permute-done.4.refs_1_ = f32[24,16,640]{2,1,0:T(8,128)S(1)} collective-permute-done((f32[24,16,640]{2,1,0:T(8,128)S(1)}, f32[24,16,640]{2,1,0:T(8,128)S(1)}, u32[]{:S(2)}, u32[]{:S(2)}) %collective-permute-start.4) | collective-permute-done | bytes 983072 | tf_op jit(solution)/shard_map/mix/ppermute | solution.py:425
  62.3 1.6 edges.5
  63.9 4.8 %collective-permute-start.5 = (f32[10,2,16,640]{3,2,1,0:T(8,128)}, f32[10,2,16,640]{3,2,1,0:T(8,128)}, u32[]{:S(2)}, u32[]{:S(2)}) collective-permute-start(f32[10,2,16,640]{3,2,1,0:T(8,128)} %get-tuple-element.61), channel_id=1, source_target_pairs={{0,2},{2,4},{4,6},{6,8},{8,10},{10,12},{12,14},{14,16},{16,18},{18... | collective-permute-start | bytes 2457608 | tf_op jit(solution)/shard_map/edges/ppermute | solution.py:498
  68.9 1.2 collective-permute-start.11
  70.3 13.1 %collective-permute-done.7.refs_1_ = f32[24,16,640]{2,1,0:T(8,128)} collective-permute-done((f32[24,16,640]{2,1,0:T(8,128)}, f32[24,16,640]{2,1,0:T(8,128)}, u32[]{:S(2)}, u32[]{:S(2)}) %collective-permute-start.7) | collective-permute-done | bytes 983072 | tf_op jit(solution)/shard_map/mix/ppermute | solution.py:425
  83.4 1.3 copy-done.4
  84.7 1.5 edges.6
  86.3 4.8 %collective-permute-start.12 = (f32[10,2,16,640]{3,2,1,0:T(8,128)S(1)}, f32[10,2,16,640]{3,2,1,0:T(8,128)S(1)}, u32[]{:S(2)}, u32[]{:S(2)}) collective-permute-start(f32[10,2,16,640]{3,2,1,0:T(8,128)S(1)} %get-tuple-element.74), channel_id=1, source_target_pairs={{0,2},{2,4},{4,6},{6,8},{8,10},{10,12},{12,14},{14,16},{16,18},{18... | collective-permute-start | bytes 2457608 | tf_op jit(solution)/shard_map/edges/ppermute | solution.py:498
  91.3 11.7 %diffusion.5 = (f32[2304,640]{1,0:T(8,128)}, f32[8,128]{1,0:T(8,128)S(1)}) custom-call(f32[2,8,2,16,640]{4,3,2,1,0:T(8,128)S(1)} %copy-done.2, f32[24,16,640]{2,1,0:T(8,128)S(1)} %copy-done.11, f32[16,72,640]{2,1,0:T(8,128)S(1)} %get-tuple-element.56.refs_2_, f32[10,2,16,640]{3,2,1,0:T(8,128)} %collective-permute-done.5.refs_3_, ...), custom_call_target="tpu_custom_call" | custom-call | flops 12682999808 | bytes 1024 | tf_op jit(solution)/shard_map/diffusion/diffusion/pallas_call | solution.py:507
  102.9 1.5 collective-permute-done.1.refs_1_
  104.5 1.5 edges.7
  106.3 5.0 %collective-permute-start.9 = (f32[10,2,16,640]{3,2,1,0:T(8,128)S(1)}, f32[10,2,16,640]{3,2,1,0:T(8,128)S(1)}, u32[]{:S(2)}, u32[]{:S(2)}) collective-permute-start(f32[10,2,16,640]{3,2,1,0:T(8,128)S(1)} %get-tuple-element.70), channel_id=1, source_target_pairs={{0,2},{2,4},{4,6},{6,8},{8,10},{10,12},{12,14},{14,16},{16,18},{18... | collective-permute-start | bytes 2457608 | tf_op jit(solution)/shard_map/edges/ppermute | solution.py:498
  112.0 11.5 %diffusion.6 = (f32[2304,640]{1,0:T(8,128)}, f32[8,128]{1,0:T(8,128)S(1)}) custom-call(f32[2,8,2,16,640]{4,3,2,1,0:T(8,128)S(1)} %copy-done.5, f32[24,16,640]{2,1,0:T(8,128)} %collective-permute-done.7.refs_1_, f32[16,72,640]{2,1,0:T(8,128)S(1)} %get-tuple-element.56.refs_2_, ...), custom_call_target="tpu_custom_call", output_to_operand_aliasing={{0}: (10, {})} | custom-call | flops 12682999808 | bytes 1024 | tf_op jit(solution)/shard_map/diffusion/diffusion/pallas_call | solution.py:507
  123.6 2.0 %collective-permute-done.11.refs_1_ = f32[24,16,640]{2,1,0:T(8,128)} collective-permute-done((f32[24,16,640]{2,1,0:T(8,128)}, f32[24,16,640]{2,1,0:T(8,128)}, u32[]{:S(2)}, u32[]{:S(2)}) %collective-permute-start.11) | collective-permute-done | bytes 983072 | tf_op jit(solution)/shard_map/mix/ppermute | solution.py:425
  125.6 1.4 edges.8
  127.0 4.8 %collective-permute-start.16 = (f32[10,2,16,640]{3,2,1,0:T(8,128)S(1)}, f32[10,2,16,640]{3,2,1,0:T(8,128)S(1)}, u32[]{:S(2)}, u32[]{:S(2)}) collective-permute-start(f32[10,2,16,640]{3,2,1,0:T(8,128)S(1)} %get-tuple-element.84), channel_id=1, source_target_pairs={{0,2},{2,4},{4,6},{6,8},{8,10},{10,12},{12,14},{14,16},{16,18},{18... | collective-permute-start | bytes 2457608 | tf_op jit(solution)/shard_map/edges/ppermute | solution.py:498
  132.1 11.5 %diffusion.7 = (f32[2304,640]{1,0:T(8,128)}, f32[8,128]{1,0:T(8,128)S(1)}) custom-call(f32[2,8,2,16,640]{4,3,2,1,0:T(8,128)S(1)} %copy-done.7, f32[24,16,640]{2,1,0:T(8,128)} %collective-permute-done.1.refs_1_, f32[16,72,640]{2,1,0:T(8,128)S(1)} %get-tuple-element.56.refs_2_, ...), custom_call_target="tpu_custom_call", output_to_operand_aliasing={{0}: (10, {})} | custom-call | flops 12682999808 | bytes 1024 | tf_op jit(solution)/shard_map/diffusion/diffusion/pallas_call | solution.py:507
  143.7 1.5 collective-permute-start.14
  146.2 3.6 %collective-permute-done.16.refs_3_ = f32[10,2,16,640]{3,2,1,0:T(8,128)S(1)} collective-permute-done((f32[10,2,16,640]{3,2,1,0:T(8,128)S(1)}, f32[10,2,16,640]{3,2,1,0:T(8,128)S(1)}, u32[]{:S(2)}, u32[]{:S(2)}) %collective-permute-start.16) | collective-permute-done | bytes 819232 | tf_op jit(solution)/shard_map/edges/ppermute | solution.py:498
  149.8 6.9 %collective-permute-done.17.refs_4_ = f32[10,2,16,640]{3,2,1,0:T(8,128)S(1)} collective-permute-done((f32[10,2,16,640]{3,2,1,0:T(8,128)S(1)}, f32[10,2,16,640]{3,2,1,0:T(8,128)S(1)}, u32[]{:S(2)}, u32[]{:S(2)}) %collective-permute-start.17) | collective-permute-done | bytes 819232 | tf_op jit(solution)/shard_map/edges/ppermute | solution.py:498
  156.7 11.5 %diffusion.8 = (f32[2304,640]{1,0:T(8,128)}, f32[8,128]{1,0:T(8,128)S(1)}) custom-call(f32[2,8,2,16,640]{4,3,2,1,0:T(8,128)S(1)} %copy-done.9, f32[24,16,640]{2,1,0:T(8,128)} %collective-permute-done.11.refs_1_, f32[16,72,640]{2,1,0:T(8,128)S(1)} %get-tuple-element.56.refs_2_, ...), custom_call_target="tpu_custom_call", output_to_operand_aliasing={{0}: (10, {})} | custom-call | flops 12682999808 | bytes 1024 | tf_op jit(solution)/shard_map/diffusion/diffusion/pallas_call | solution.py:507
  168.1 6.6 %diffusion.9 = (f32[2304,640]{1,0:T(8,128)}, f32[8,128]{1,0:T(8,128)}) custom-call(f32[2,8,2,8,640]{4,3,2,1,0:T(8,128)S(1)} %copy-done.22, f32[24,8,640]{2,1,0:T(8,128)S(1)} %collective-permute-done.8.refs_1_, f32[16,72,640]{2,1,0:T(8,128)S(1)} %get-tuple-element.56.refs_2_, ...), custom_call_target="tpu_custom_call", output_to_operand_aliasing={{0}: (10, {})} | custom-call | flops 12682999808 | bytes 1024 | tf_op jit(solution)/shard_map/diffusion/diffusion/pallas_call | solution.py:507
  (71 shorter events, 7.4 us)
Async XLA Ops:
  0.0 70.1 %copy-start = (s32[10,144]{1,0:T(8,128)S(1)}, s32[10,144]{1,0:T(8,128)}, u32[]{:S(2)}) copy-start(s32[10,144]{1,0:T(8,128)} %param.13) | copy-start | bytes 17284
  2.8 39.2 %collective-permute-start = (f32[72,8,640]{2,1,0:T(8,128)}, f32[72,8,640]{2,1,0:T(8,128)}, u32[]{:S(2)}, u32[]{:S(2)}) collective-permute-start(f32[72,8,640]{2,1,0:T(8,128)} %slice_bitcast_fusion._), channel_id=1, source_target_pairs={{0,1},{1,0},{2,3},{3,2},{4,5},{5,4},{6,7},{7,6},{8,9},{9,8},{10,11... | collective-permute-start | bytes 4423688 | tf_op jit(solution)/shard_map/raw/ppermute | solution.py:350
  14.9 47.3 %collective-permute-start.2 = (f32[9,72,640]{2,1,0:T(8,128)}, f32[9,72,640]{2,1,0:T(8,128)}, u32[]{:S(2)}, u32[]{:S(2)}) collective-permute-start(f32[9,72,640]{2,1,0:T(8,128)} %get-tuple-element.57), channel_id=1, source_target_pairs={{0,2},{2,4},{4,6},{6,8},{8,10},{10,12},{12,14},{14,16},{16,18},{18... | collective-permute-start | bytes 4976648 | tf_op jit(solution)/shard_map/coef/ppermute | solution.py:382
  17.0 45.2 %collective-permute-start.3 = (f32[9,72,640]{2,1,0:T(8,128)}, f32[9,72,640]{2,1,0:T(8,128)}, u32[]{:S(2)}, u32[]{:S(2)}) collective-permute-start(f32[9,72,640]{2,1,0:T(8,128)} %get-tuple-element.58), channel_id=1, source_target_pairs={{2,0},{4,2},{6,4},{8,6},{10,8},{12,10},{14,12},{16,14},{18,16},{20... | collective-permute-start | bytes 4976648 | tf_op jit(solution)/shard_map/coef/ppermute | solution.py:383
  40.5 21.8 %collective-permute-start.4 = (f32[24,16,640]{2,1,0:T(8,128)S(1)}, f32[24,16,640]{2,1,0:T(8,128)S(1)}, u32[]{:S(2)}, u32[]{:S(2)}) collective-permute-start(f32[24,16,640]{2,1,0:T(8,128)S(1)} %get-tuple-element.60), channel_id=1, source_target_pairs={{0,1},{1,0},{2,3},{3,2},{4,5},{5,4},{6,7},{7,6},{8,9},{9,8},{10,11... | collective-permute-start | bytes 2949128 | tf_op jit(solution)/shard_map/mix/ppermute | solution.py:425
  40.8 42.6 %collective-permute-start.7 = (f32[24,16,640]{2,1,0:T(8,128)}, f32[24,16,640]{2,1,0:T(8,128)}, u32[]{:S(2)}, u32[]{:S(2)}) collective-permute-start(f32[24,16,640]{2,1,0:T(8,128)} %get-tuple-element.64), channel_id=1, source_target_pairs={{0,1},{1,0},{2,3},{3,2},{4,5},{5,4},{6,7},{7,6},{8,9},{9,8},{10,11... | collective-permute-start | bytes 2949128 | tf_op jit(solution)/shard_map/mix/ppermute | solution.py:425
  47.7 16.1 %copy-start.1 = (f32[2,8,2,16,640]{4,3,2,1,0:T(8,128)}, f32[2,8,2,16,640]{4,3,2,1,0:T(8,128)S(1)}, u32[]{:S(2)}) copy-start(f32[2,8,2,16,640]{4,3,2,1,0:T(8,128)S(1)} %get-tuple-element.59.refs_0_) | copy-start | bytes 3932164
  47.7 16.1 %copy-start.3 = (f32[2,8,2,16,640]{4,3,2,1,0:T(8,128)}, f32[2,8,2,16,640]{4,3,2,1,0:T(8,128)S(1)}, u32[]{:S(2)}) copy-start(f32[2,8,2,16,640]{4,3,2,1,0:T(8,128)S(1)} %get-tuple-element.63.refs_0_) | copy-start | bytes 3932164
  47.7 16.1 %copy-start.6 = (f32[2,8,2,16,640]{4,3,2,1,0:T(8,128)}, f32[2,8,2,16,640]{4,3,2,1,0:T(8,128)S(1)}, u32[]{:S(2)}) copy-start(f32[2,8,2,16,640]{4,3,2,1,0:T(8,128)S(1)} %get-tuple-element.54.refs_0_) | copy-start | bytes 3932164
  47.7 16.1 %copy-start.8 = (f32[2,8,2,16,640]{4,3,2,1,0:T(8,128)}, f32[2,8,2,16,640]{4,3,2,1,0:T(8,128)S(1)}, u32[]{:S(2)}) copy-start(f32[2,8,2,16,640]{4,3,2,1,0:T(8,128)S(1)} %get-tuple-element.72.refs_0_) | copy-start | bytes 3932164
  47.7 16.1 %copy-start.21 = (f32[2,8,2,8,640]{4,3,2,1,0:T(8,128)}, f32[2,8,2,8,640]{4,3,2,1,0:T(8,128)S(1)}, u32[]{:S(2)}) copy-start(f32[2,8,2,8,640]{4,3,2,1,0:T(8,128)S(1)} %get-tuple-element.53.refs_0_) | copy-start | bytes 1966084
  62.3 7.9 %copy-start.23 = (f32[8]{0:T(128)S(1)}, f32[8]{0:T(128)}, u32[]{:S(2)}) copy-start(f32[8]{0:T(128)} %param.14) | copy-start | bytes 100
  63.9 27.2 %collective-permute-start.5 = (f32[10,2,16,640]{3,2,1,0:T(8,128)}, f32[10,2,16,640]{3,2,1,0:T(8,128)}, u32[]{:S(2)}, u32[]{:S(2)}) collective-permute-start(f32[10,2,16,640]{3,2,1,0:T(8,128)} %get-tuple-element.61), channel_id=1, source_target_pairs={{0,2},{2,4},{4,6},{6,8},{8,10},{10,12},{12,14},{14,16},{16,18},{18... | collective-permute-start | bytes 2457608 | tf_op jit(solution)/shard_map/edges/ppermute | solution.py:498
  68.7 22.4 %collective-permute-start.6 = (f32[10,2,16,640]{3,2,1,0:T(8,128)}, f32[10,2,16,640]{3,2,1,0:T(8,128)}, u32[]{:S(2)}, u32[]{:S(2)}) collective-permute-start(f32[10,2,16,640]{3,2,1,0:T(8,128)} %get-tuple-element.62), channel_id=1, source_target_pairs={{2,0},{4,2},{6,4},{8,6},{10,8},{12,10},{14,12},{16,14},{18,16},{20... | collective-permute-start | bytes 2457608 | tf_op jit(solution)/shard_map/edges/ppermute | solution.py:498
  68.7 35.8 %collective-permute-start.1 = (f32[24,16,640]{2,1,0:T(8,128)}, f32[24,16,640]{2,1,0:T(8,128)}, u32[]{:S(2)}, u32[]{:S(2)}) collective-permute-start(f32[24,16,640]{2,1,0:T(8,128)} %get-tuple-element.55), channel_id=1, source_target_pairs={{0,1},{1,0},{2,3},{3,2},{4,5},{5,4},{6,7},{7,6},{8,9},{9,8},{10,11... | collective-permute-start | bytes 2949128 | tf_op jit(solution)/shard_map/mix/ppermute | solution.py:425
  68.9 56.7 %collective-permute-start.11 = (f32[24,16,640]{2,1,0:T(8,128)}, f32[24,16,640]{2,1,0:T(8,128)}, u32[]{:S(2)}, u32[]{:S(2)}) collective-permute-start(f32[24,16,640]{2,1,0:T(8,128)} %get-tuple-element.73), channel_id=1, source_target_pairs={{0,1},{1,0},{2,3},{3,2},{4,5},{5,4},{6,7},{7,6},{8,9},{9,8},{10,11... | collective-permute-start | bytes 2949128 | tf_op jit(solution)/shard_map/mix/ppermute | solution.py:425
  84.7 6.5 %copy-start.2 = (f32[2,8,2,16,640]{4,3,2,1,0:T(8,128)S(1)}, f32[2,8,2,16,640]{4,3,2,1,0:T(8,128)}, u32[]{:S(2)}) copy-start(f32[2,8,2,16,640]{4,3,2,1,0:T(8,128)} %copy-done.1) | copy-start | bytes 3932164
  84.7 6.5 %copy-start.11 = (f32[24,16,640]{2,1,0:T(8,128)S(1)}, f32[24,16,640]{2,1,0:T(8,128)}, u32[]{:S(2)}) copy-start(f32[24,16,640]{2,1,0:T(8,128)} %copy-done.10) | copy-start | bytes 2949124
  84.7 6.5 %copy-start.18 = (bf16[640,640]{1,0:T(8,128)(2,1)S(1)}, bf16[640,640]{1,0:T(8,128)(2,1)}, u32[]{:S(2)}) copy-start(bf16[640,640]{1,0:T(8,128)(2,1)} %constant.25.clone.refs_8_) | copy-start | bytes 2457604
  86.3 25.0 %collective-permute-start.12 = (f32[10,2,16,640]{3,2,1,0:T(8,128)S(1)}, f32[10,2,16,640]{3,2,1,0:T(8,128)S(1)}, u32[]{:S(2)}, u32[]{:S(2)}) collective-permute-start(f32[10,2,16,640]{3,2,1,0:T(8,128)S(1)} %get-tuple-element.74), channel_id=1, source_target_pairs={{0,2},{2,4},{4,6},{6,8},{8,10},{10,12},{12,14},{14,16},{16,18},{18... | collective-permute-start | bytes 2457608 | tf_op jit(solution)/shard_map/edges/ppermute | solution.py:498
  91.1 20.9 %collective-permute-start.13 = (f32[10,2,16,640]{3,2,1,0:T(8,128)S(1)}, f32[10,2,16,640]{3,2,1,0:T(8,128)S(1)}, u32[]{:S(2)}, u32[]{:S(2)}) collective-permute-start(f32[10,2,16,640]{3,2,1,0:T(8,128)S(1)} %get-tuple-element.75), channel_id=1, source_target_pairs={{2,0},{4,2},{6,4},{8,6},{10,8},{12,10},{14,12},{16,14},{18,16},{20... | collective-permute-start | bytes 2457608 | tf_op jit(solution)/shard_map/edges/ppermute | solution.py:498
  91.3 13.2 %copy-start.7 = (f32[2,8,2,16,640]{4,3,2,1,0:T(8,128)S(1)}, f32[2,8,2,16,640]{4,3,2,1,0:T(8,128)}, u32[]{:S(2)}) copy-start(f32[2,8,2,16,640]{4,3,2,1,0:T(8,128)} %copy-done.6) | copy-start | bytes 3932164
  104.5 7.5 %copy-start.5 = (f32[2,8,2,16,640]{4,3,2,1,0:T(8,128)S(1)}, f32[2,8,2,16,640]{4,3,2,1,0:T(8,128)}, u32[]{:S(2)}) copy-start(f32[2,8,2,16,640]{4,3,2,1,0:T(8,128)} %copy-done.3) | copy-start | bytes 3932164
  106.0 37.7 %collective-permute-start.8 = (f32[24,8,640]{2,1,0:T(8,128)S(1)}, f32[24,8,640]{2,1,0:T(8,128)S(1)}, u32[]{:S(2)}, u32[]{:S(2)}) collective-permute-start(f32[24,8,640]{2,1,0:T(8,128)S(1)} %get-tuple-element.69), channel_id=1, source_target_pairs={{0,1},{1,0},{2,3},{3,2},{4,5},{5,4},{6,7},{7,6},{8,9},{9,8},{10,11... | collective-permute-start | bytes 1474568 | tf_op jit(solution)/shard_map/ppermute | solution.py:425
  106.3 25.5 %collective-permute-start.9 = (f32[10,2,16,640]{3,2,1,0:T(8,128)S(1)}, f32[10,2,16,640]{3,2,1,0:T(8,128)S(1)}, u32[]{:S(2)}, u32[]{:S(2)}) collective-permute-start(f32[10,2,16,640]{3,2,1,0:T(8,128)S(1)} %get-tuple-element.70), channel_id=1, source_target_pairs={{0,2},{2,4},{4,6},{6,8},{8,10},{10,12},{12,14},{14,16},{16,18},{18... | collective-permute-start | bytes 2457608 | tf_op jit(solution)/shard_map/edges/ppermute | solution.py:498
  111.3 20.8 %collective-permute-start.10 = (f32[10,2,16,640]{3,2,1,0:T(8,128)S(1)}, f32[10,2,16,640]{3,2,1,0:T(8,128)S(1)}, u32[]{:S(2)}, u32[]{:S(2)}) collective-permute-start(f32[10,2,16,640]{3,2,1,0:T(8,128)S(1)} %get-tuple-element.71), channel_id=1, source_target_pairs={{2,0},{4,2},{6,4},{8,6},{10,8},{12,10},{14,12},{16,14},{18,16},{20... | collective-permute-start | bytes 2457608 | tf_op jit(solution)/shard_map/edges/ppermute | solution.py:498
  112.0 13.5 %copy-start.9 = (f32[2,8,2,16,640]{4,3,2,1,0:T(8,128)S(1)}, f32[2,8,2,16,640]{4,3,2,1,0:T(8,128)}, u32[]{:S(2)}) copy-start(f32[2,8,2,16,640]{4,3,2,1,0:T(8,128)} %copy-done.8) | copy-start | bytes 3932164
  127.0 22.8 %collective-permute-start.16 = (f32[10,2,16,640]{3,2,1,0:T(8,128)S(1)}, f32[10,2,16,640]{3,2,1,0:T(8,128)S(1)}, u32[]{:S(2)}, u32[]{:S(2)}) collective-permute-start(f32[10,2,16,640]{3,2,1,0:T(8,128)S(1)} %get-tuple-element.84), channel_id=1, source_target_pairs={{0,2},{2,4},{4,6},{6,8},{8,10},{10,12},{12,14},{14,16},{16,18},{18... | collective-permute-start | bytes 2457608 | tf_op jit(solution)/shard_map/edges/ppermute | solution.py:498
  131.7 24.9 %collective-permute-start.17 = (f32[10,2,16,640]{3,2,1,0:T(8,128)S(1)}, f32[10,2,16,640]{3,2,1,0:T(8,128)S(1)}, u32[]{:S(2)}, u32[]{:S(2)}) collective-permute-start(f32[10,2,16,640]{3,2,1,0:T(8,128)S(1)} %get-tuple-element.85), channel_id=1, source_target_pairs={{2,0},{4,2},{6,4},{8,6},{10,8},{12,10},{14,12},{16,14},{18,16},{20... | collective-permute-start | bytes 2457608 | tf_op jit(solution)/shard_map/edges/ppermute | solution.py:498
  132.1 11.5 %copy-start.22 = (f32[2,8,2,8,640]{4,3,2,1,0:T(8,128)S(1)}, f32[2,8,2,8,640]{4,3,2,1,0:T(8,128)}, u32[]{:S(2)}) copy-start(f32[2,8,2,8,640]{4,3,2,1,0:T(8,128)} %copy-done.21) | copy-start | bytes 1966084
  143.7 24.4 %collective-permute-start.14 = (f32[10,2,8,640]{3,2,1,0:T(8,128)S(1)}, f32[10,2,8,640]{3,2,1,0:T(8,128)S(1)}, u32[]{:S(2)}, u32[]{:S(2)}) collective-permute-start(f32[10,2,8,640]{3,2,1,0:T(8,128)S(1)} %get-tuple-element.82), channel_id=1, source_target_pairs={{0,2},{2,4},{4,6},{6,8},{8,10},{10,12},{12,14},{14,16},{16,18},{18... | collective-permute-start | bytes 1228808 | tf_op jit(solution)/shard_map/edges/ppermute | solution.py:498
  145.2 22.9 %collective-permute-start.15 = (f32[10,2,8,640]{3,2,1,0:T(8,128)S(1)}, f32[10,2,8,640]{3,2,1,0:T(8,128)S(1)}, u32[]{:S(2)}, u32[]{:S(2)}) collective-permute-start(f32[10,2,8,640]{3,2,1,0:T(8,128)S(1)} %get-tuple-element.83), channel_id=1, source_target_pairs={{2,0},{4,2},{6,4},{8,6},{10,8},{12,10},{14,12},{16,14},{18,16},{20... | collective-permute-start | bytes 1228808 | tf_op jit(solution)/shard_map/edges/ppermute | solution.py:498
  (10 other events, 16.5 us)

commit v5 on v2

--- a/solution.py
+++ b/solution.py
@@ -408,7 +408,7 @@
                 pltpu.VMEM((tiles, own * 2 * lons, LANES), f32),
                 pltpu.SemaphoreType.DMA((tiles,)),
             ],
-            compiler_params=params(30),
+            compiler_params=params(50),
             cost_estimate=spent(20),
             name="mix",
         )(

time: 169 us -> 169 us (level)
  local copies, waits for them, and re-layouts: 9.66 us -> 18.1 us
  waiting for transfers between devices: 40.5 us -> 34.7 us
  starting transfers between devices: 28.9 us -> 24.6 us
    unnamed x56 -> x64, local copies, waits for them, and re-layouts: 6.67 us -> 15.2 us
    ppermute x5, waiting for transfers between devices: 29.6 us -> 21.6 us  [send(): lax.ppermute(array, 'lev', along(shift + 1))]
    ppermute x5, starting transfers between devices: 19.3 us -> 16.9 us  [edges(): lax.ppermute(last, 'tile', up)]
    ppermute x1, waiting for transfers between devices: 0.12 us -> 2.04 us  [on_device(): lax.ppermute(rows, 'lev', along(shift))]
  transfers between devices with their start and end apart: 18 -> 18, of which waited for: 8 -> 8; matrix products, arithmetic and copies ran while one was open for 0% -> 0% of each run, Pallas kernels for 49% -> 50%
where the time goes in v5:
time: 169 us; the launch traced here: 168 us
  Pallas kernels  90 us (53%)
  waiting for transfers between devices  34.7 us (21%)
  starting transfers between devices  24.6 us (15%)
  local copies, waits for them, and re-layouts  18.1 us (11%)
    pallas_call x5, Pallas kernels, diffusion(): pl.pallas_call(functools.partial(diffuse_kernel, lons, lats, len(sums)),...  52.8 us
    ppermute x5, waiting for transfers between devices, send(): lax.ppermute(array, 'lev', along(shift + 1))  21.6 us
    pallas_call x1, Pallas kernels, on_device(): pl.pallas_call(functools.partial(mix_kernel, shape, offsets), grid=(half...  17.4 us
    ppermute x5, starting transfers between devices, edges(): lax.ppermute(last, 'tile', up)  16.9 us
    unnamed x64, local copies, waits for them, and re-layouts  15.2 us
    pallas_call x1, Pallas kernels, on_device(): pl.pallas_call(functools.partial(coef_kernel, own, padded, lons, halo - 1...  8.89 us
    ppermute x5, waiting for transfers between devices, edges(): lax.ppermute(first, 'tile', down)  6.49 us
    pallas_call x5, Pallas kernels, edges(): pl.pallas_call(functools.partial(edge_kernel, lons, halo, len(sums), len(...  6.03 us
  transfers between devices with their start and end apart: 18, of which 8 were waited for; matrix products, arithmetic and copies ran while one was open for 0% of the time, Pallas kernels for 50%

profile of v5, /device:TPU:25, one launch (start us, length us, event | category | flops | bytes accessed | tf_op | source)
XLA Modules:
  0.0 167.8 jit_solution(3263047265969381425)
XLA Ops:
  0.0 2.7 %slice_bitcast_fusion._ = f32[72,8,640]{2,1,0:T(8,128)} fusion(f32[72,2,16,640]{3,2,1,0:T(8,128)} %param.10), kind=kLoop, calls=%fused_computation | loop fusion | bytes 2949120 | tf_op jit(solution)/shard_map/raw/squeeze | solution.py:349
  4.0 8.9 %coef.1 = (f32[16,72,640]{2,1,0:T(8,128)}, f32[9,72,640]{2,1,0:T(8,128)}, f32[9,72,640]{2,1,0:T(8,128)}) custom-call(s32[1152,640]{1,0:T(8,128)} %bitcast.17, f32[1152,640]{1,0:T(8,128)} %bitcast.18, bf16[640,640]{1,0:T(8,128)(2,1)S(1)} %copy-done.27, f32[72,8,640]{2,1,0:T(8,128)} %slice_bitcast_fusion._), custom_call_target="tpu_custom_call" | custom-call | flops 11530000384 | bytes 1024 | tf_op jit(solution)/shard_map/coef/coef/pallas_call | solution.py:362
  12.9 2.1 %collective-permute-start.2 = (f32[9,72,640]{2,1,0:T(8,128)}, f32[9,72,640]{2,1,0:T(8,128)}, u32[]{:S(2)}, u32[]{:S(2)}) collective-permute-start(f32[9,72,640]{2,1,0:T(8,128)} %get-tuple-element.57), channel_id=1, source_target_pairs={{0,2},{2,4},{4,6},{6,8},{8,10},{10,12},{12,14},{14,16},{16,18},{18... | collective-permute-start | bytes 4976648 | tf_op jit(solution)/shard_map/coef/ppermute | solution.py:382
  15.1 17.4 %mix.1 = (f32[2,8,2,16,640]{4,3,2,1,0:T(8,128)}, f32[2,8,2,16,640]{4,3,2,1,0:T(8,128)}, f32[2,8,2,16,640]{4,3,2,1,0:T(8,128)}, f32[2,8,2,16,640]{4,3,2,1,0:T(8,1...) custom-call(s32[2]{0:T(128)S(1)} %pad_add_fusion.at, ...), custom_call_target="tpu_custom_call" | custom-call | flops 23060000768 | bytes 1024 | tf_op jit(solution)/shard_map/mix/mix/pallas_call | solution.py:393
  34.0 2.0 %collective-permute-done = f32[72,8,640]{2,1,0:T(8,128)S(1)} collective-permute-done((f32[72,8,640]{2,1,0:T(8,128)}, f32[72,8,640]{2,1,0:T(8,128)S(1)}, u32[]{:S(2)}, u32[]{:S(2)}) %collective-permute-start) | collective-permute-done | bytes 1474592 | tf_op jit(solution)/shard_map/raw/ppermute | solution.py:350
  38.6 1.3 copy-done.6
  39.9 1.3 copy-done.10
  41.2 1.3 copy-done.13
  42.5 1.4 copy-done.19
  43.9 4.9 %raw.1 = (f32[2,8,2,16,640]{4,3,2,1,0:T(8,128)S(1)}, f32[2,8,2,16,640]{4,3,2,1,0:T(8,128)S(1)}, f32[2,8,2,16,640]{4,3,2,1,0:T(8,128)S(1)}, f32[2,8,2,16,640]{4,3,2,1,0:T(8,128)S(1)}, f32[2,8,2,8,640]{4,3,2,1,0:T(8,128)S(1)}) custom-call(s32[2]{0:T(128)S(1)} %pad_add_fusion.at, ...), custom_call_target="tpu_custom_call", output_to_operand_aliasing={{0}: (10, {}), {1}: (11, {}), {2}: (12, {}), {3}: (13, {}),... | custom-call | flops 6918000128 | bytes 1024 | tf_op jit(solution)/shard_map/raw/raw/pallas_call | solution.py:431
  53.1 4.0 %collective-permute-done.4.refs_1_ = f32[24,16,640]{2,1,0:T(8,128)S(1)} collective-permute-done((f32[24,16,640]{2,1,0:T(8,128)S(1)}, f32[24,16,640]{2,1,0:T(8,128)S(1)}, u32[]{:S(2)}, u32[]{:S(2)}) %collective-permute-start.4) | collective-permute-done | bytes 983072 | tf_op jit(solution)/shard_map/mix/ppermute | solution.py:425
  57.2 1.7 copy-done.4
  58.8 1.5 edges.5
  60.3 3.8 %collective-permute-start.5 = (f32[10,2,16,640]{3,2,1,0:T(8,128)}, f32[10,2,16,640]{3,2,1,0:T(8,128)}, u32[]{:S(2)}, u32[]{:S(2)}) collective-permute-start(f32[10,2,16,640]{3,2,1,0:T(8,128)} %get-tuple-element.61), channel_id=1, source_target_pairs={{0,2},{2,4},{4,6},{6,8},{8,10},{10,12},{12,14},{14,16},{16,18},{18... | collective-permute-start | bytes 2457608 | tf_op jit(solution)/shard_map/edges/ppermute | solution.py:498
  65.8 12.5 %collective-permute-done.7.refs_1_ = f32[24,16,640]{2,1,0:T(8,128)} collective-permute-done((f32[24,16,640]{2,1,0:T(8,128)}, f32[24,16,640]{2,1,0:T(8,128)}, u32[]{:S(2)}, u32[]{:S(2)}) %collective-permute-start.7) | collective-permute-done | bytes 983072 | tf_op jit(solution)/shard_map/mix/ppermute | solution.py:425
  78.3 1.3 copy-done.8
  79.6 1.5 edges.6
  81.2 3.8 %collective-permute-start.12 = (f32[10,2,16,640]{3,2,1,0:T(8,128)S(1)}, f32[10,2,16,640]{3,2,1,0:T(8,128)S(1)}, u32[]{:S(2)}, u32[]{:S(2)}) collective-permute-start(f32[10,2,16,640]{3,2,1,0:T(8,128)S(1)} %get-tuple-element.74), channel_id=1, source_target_pairs={{0,2},{2,4},{4,6},{6,8},{8,10},{10,12},{12,14},{14,16},{16,18},{18... | collective-permute-start | bytes 2457608 | tf_op jit(solution)/shard_map/edges/ppermute | solution.py:498
  85.2 11.7 %diffusion.5 = (f32[2304,640]{1,0:T(8,128)}, f32[8,128]{1,0:T(8,128)S(1)}) custom-call(f32[2,8,2,16,640]{4,3,2,1,0:T(8,128)S(1)} %copy-done.5, f32[24,16,640]{2,1,0:T(8,128)S(1)} %copy-done.17, f32[16,72,640]{2,1,0:T(8,128)S(1)} %copy-done.1, f32[10,2,16,640]{3,2,1,0:T(8,128)} %collective-permute-done.5.refs_3_, ...), custom_call_target="tpu_custom_call" | custom-call | flops 12682999808 | bytes 1024 | tf_op jit(solution)/shard_map/diffusion/diffusion/pallas_call | solution.py:507
  96.9 2.5 %collective-permute-done.1.refs_1_ = f32[24,16,640]{2,1,0:T(8,128)} collective-permute-done((f32[24,16,640]{2,1,0:T(8,128)}, f32[24,16,640]{2,1,0:T(8,128)}, u32[]{:S(2)}, u32[]{:S(2)}) %collective-permute-start.1) | collective-permute-done | bytes 983072 | tf_op jit(solution)/shard_map/mix/ppermute | solution.py:425
  99.4 1.5 edges.7
  102.2 4.1 %collective-permute-start.9 = (f32[10,2,16,640]{3,2,1,0:T(8,128)S(1)}, f32[10,2,16,640]{3,2,1,0:T(8,128)S(1)}, u32[]{:S(2)}, u32[]{:S(2)}) collective-permute-start(f32[10,2,16,640]{3,2,1,0:T(8,128)S(1)} %get-tuple-element.70), channel_id=1, source_target_pairs={{0,2},{2,4},{4,6},{6,8},{8,10},{10,12},{12,14},{14,16},{16,18},{18... | collective-permute-start | bytes 2457608 | tf_op jit(solution)/shard_map/edges/ppermute | solution.py:498
  106.3 11.6 %diffusion.6 = (f32[2304,640]{1,0:T(8,128)}, f32[8,128]{1,0:T(8,128)S(1)}) custom-call(f32[2,8,2,16,640]{4,3,2,1,0:T(8,128)S(1)} %copy-done.9, f32[24,16,640]{2,1,0:T(8,128)} %collective-permute-done.7.refs_1_, f32[16,72,640]{2,1,0:T(8,128)S(1)} %copy-done.1, ...), custom_call_target="tpu_custom_call", output_to_operand_aliasing={{0}: (10, {})} | custom-call | flops 12682999808 | bytes 1024 | tf_op jit(solution)/shard_map/diffusion/diffusion/pallas_call | solution.py:507
  117.8 2.6 %collective-permute-done.11.refs_1_ = f32[24,16,640]{2,1,0:T(8,128)} collective-permute-done((f32[24,16,640]{2,1,0:T(8,128)}, f32[24,16,640]{2,1,0:T(8,128)}, u32[]{:S(2)}, u32[]{:S(2)}) %collective-permute-start.11) | collective-permute-done | bytes 983072 | tf_op jit(solution)/shard_map/mix/ppermute | solution.py:425
  120.4 1.4 edges.8
  121.9 3.8 %collective-permute-start.16 = (f32[10,2,16,640]{3,2,1,0:T(8,128)S(1)}, f32[10,2,16,640]{3,2,1,0:T(8,128)S(1)}, u32[]{:S(2)}, u32[]{:S(2)}) collective-permute-start(f32[10,2,16,640]{3,2,1,0:T(8,128)S(1)} %get-tuple-element.84), channel_id=1, source_target_pairs={{0,2},{2,4},{4,6},{6,8},{8,10},{10,12},{12,14},{14,16},{16,18},{18... | collective-permute-start | bytes 2457608 | tf_op jit(solution)/shard_map/edges/ppermute | solution.py:498
  126.2 11.5 %diffusion.7 = (f32[2304,640]{1,0:T(8,128)}, f32[8,128]{1,0:T(8,128)S(1)}) custom-call(f32[2,8,2,16,640]{4,3,2,1,0:T(8,128)S(1)} %copy-done.12, f32[24,16,640]{2,1,0:T(8,128)} %collective-permute-done.1.refs_1_, f32[16,72,640]{2,1,0:T(8,128)S(1)} %copy-done.1, ...), custom_call_target="tpu_custom_call", output_to_operand_aliasing={{0}: (10, {})} | custom-call | flops 12682999808 | bytes 1024 | tf_op jit(solution)/shard_map/diffusion/diffusion/pallas_call | solution.py:507
  137.8 1.3 collective-permute-start.14
  139.2 4.5 %collective-permute-done.16.refs_3_ = f32[10,2,16,640]{3,2,1,0:T(8,128)S(1)} collective-permute-done((f32[10,2,16,640]{3,2,1,0:T(8,128)S(1)}, f32[10,2,16,640]{3,2,1,0:T(8,128)S(1)}, u32[]{:S(2)}, u32[]{:S(2)}) %collective-permute-start.16) | collective-permute-done | bytes 819232 | tf_op jit(solution)/shard_map/edges/ppermute | solution.py:498
  143.8 6.0 %collective-permute-done.17.refs_4_ = f32[10,2,16,640]{3,2,1,0:T(8,128)S(1)} collective-permute-done((f32[10,2,16,640]{3,2,1,0:T(8,128)S(1)}, f32[10,2,16,640]{3,2,1,0:T(8,128)S(1)}, u32[]{:S(2)}, u32[]{:S(2)}) %collective-permute-start.17) | collective-permute-done | bytes 819232 | tf_op jit(solution)/shard_map/edges/ppermute | solution.py:498
  149.7 11.5 %diffusion.8 = (f32[2304,640]{1,0:T(8,128)}, f32[8,128]{1,0:T(8,128)S(1)}) custom-call(f32[2,8,2,16,640]{4,3,2,1,0:T(8,128)S(1)} %copy-done.15, f32[24,16,640]{2,1,0:T(8,128)} %collective-permute-done.11.refs_1_, f32[16,72,640]{2,1,0:T(8,128)S(1)} %copy-done.1, ...), custom_call_target="tpu_custom_call", output_to_operand_aliasing={{0}: (10, {})} | custom-call | flops 12682999808 | bytes 1024 | tf_op jit(solution)/shard_map/diffusion/diffusion/pallas_call | solution.py:507
  161.2 6.6 %diffusion.9 = (f32[2304,640]{1,0:T(8,128)}, f32[8,128]{1,0:T(8,128)}) custom-call(f32[2,8,2,8,640]{4,3,2,1,0:T(8,128)S(1)} %copy-done.30, f32[24,8,640]{2,1,0:T(8,128)S(1)} %collective-permute-done.8.refs_1_, f32[16,72,640]{2,1,0:T(8,128)S(1)} %copy-done.1, f32[10,2,8,640]{3,2,1,0:T(8,128)S(1)} %collective-permute-done.14.refs_3_, ...), custom_call_target="tpu_custom_call", output_to_operand_aliasing={{0}: (10, {})} | custom-call | flops 12682999808 | bytes 1024 | tf_op jit(solution)/shard_map/diffusion/diffusion/pallas_call | solution.py:507
  (87 shorter events, 13.5 us)
Async XLA Ops:
  0.0 65.6 %copy-start = (s32[10,144]{1,0:T(8,128)S(1)}, s32[10,144]{1,0:T(8,128)}, u32[]{:S(2)}) copy-start(s32[10,144]{1,0:T(8,128)} %param.13) | copy-start | bytes 17284
  2.7 33.4 %collective-permute-start = (f32[72,8,640]{2,1,0:T(8,128)}, f32[72,8,640]{2,1,0:T(8,128)S(1)}, u32[]{:S(2)}, u32[]{:S(2)}) collective-permute-start(f32[72,8,640]{2,1,0:T(8,128)} %slice_bitcast_fusion._), channel_id=1, source_target_pairs={{0,1},{1,0},{2,3},{3,2},{4,5},{5,4},{6,7},{7,6},{8,9},{9,8},{10,11... | collective-permute-start | bytes 4423688 | tf_op jit(solution)/shard_map/raw/ppermute | solution.py:350
  4.0 11.1 %copy-start.20 = (f32[144,144]{1,0:T(8,128)S(1)}, f32[144,144]{1,0:T(8,128)}, u32[]{:S(2)}) copy-start(f32[144,144]{1,0:T(8,128)} %refs_5_.1) | copy-start | bytes 248836
  4.0 11.1 %copy-start.22 = (f32[144,144]{1,0:T(8,128)S(1)}, f32[144,144]{1,0:T(8,128)}, u32[]{:S(2)}) copy-start(f32[144,144]{1,0:T(8,128)} %refs_6_.1) | copy-start | bytes 248836
  4.0 11.1 %copy-start.24 = (f32[144,144]{1,0:T(8,128)S(1)}, f32[144,144]{1,0:T(8,128)}, u32[]{:S(2)}) copy-start(f32[144,144]{1,0:T(8,128)} %refs_7_.1) | copy-start | bytes 248836
  12.9 44.3 %collective-permute-start.2 = (f32[9,72,640]{2,1,0:T(8,128)}, f32[9,72,640]{2,1,0:T(8,128)}, u32[]{:S(2)}, u32[]{:S(2)}) collective-permute-start(f32[9,72,640]{2,1,0:T(8,128)} %get-tuple-element.57), channel_id=1, source_target_pairs={{0,2},{2,4},{4,6},{6,8},{8,10},{10,12},{12,14},{14,16},{16,18},{18... | collective-permute-start | bytes 4976648 | tf_op jit(solution)/shard_map/coef/ppermute | solution.py:382
  15.0 42.2 %collective-permute-start.3 = (f32[9,72,640]{2,1,0:T(8,128)}, f32[9,72,640]{2,1,0:T(8,128)}, u32[]{:S(2)}, u32[]{:S(2)}) collective-permute-start(f32[9,72,640]{2,1,0:T(8,128)} %get-tuple-element.58), channel_id=1, source_target_pairs={{2,0},{4,2},{6,4},{8,6},{10,8},{12,10},{14,12},{16,14},{18,16},{20... | collective-permute-start | bytes 4976648 | tf_op jit(solution)/shard_map/coef/ppermute | solution.py:383
  15.0 22.2 %copy-start.21 = (f32[144,144]{1,0:T(8,128)S(1)}, f32[144,144]{1,0:T(8,128)}, u32[]{:S(2)}) copy-start(f32[144,144]{1,0:T(8,128)} %refs_5_.1) | copy-start | bytes 248836
  15.0 22.2 %copy-start.23 = (f32[144,144]{1,0:T(8,128)S(1)}, f32[144,144]{1,0:T(8,128)}, u32[]{:S(2)}) copy-start(f32[144,144]{1,0:T(8,128)} %refs_6_.1) | copy-start | bytes 248836
  15.1 22.2 %copy-start.25 = (f32[144,144]{1,0:T(8,128)S(1)}, f32[144,144]{1,0:T(8,128)}, u32[]{:S(2)}) copy-start(f32[144,144]{1,0:T(8,128)} %refs_7_.1) | copy-start | bytes 248836
  15.1 22.2 %copy-start.28 = (bf16[640,640]{1,0:T(8,128)(2,1)S(1)}, bf16[640,640]{1,0:T(8,128)(2,1)}, u32[]{:S(2)}) copy-start(bf16[640,640]{1,0:T(8,128)(2,1)} %constant.26.clone.refs_4_.refs_8_.order) | copy-start | bytes 2457604
  32.5 24.6 %collective-permute-start.4 = (f32[24,16,640]{2,1,0:T(8,128)S(1)}, f32[24,16,640]{2,1,0:T(8,128)S(1)}, u32[]{:S(2)}, u32[]{:S(2)}) collective-permute-start(f32[24,16,640]{2,1,0:T(8,128)S(1)} %get-tuple-element.60), channel_id=1, source_target_pairs={{0,1},{1,0},{2,3},{3,2},{4,5},{5,4},{6,7},{7,6},{8,9},{9,8},{10,11... | collective-permute-start | bytes 2949128 | tf_op jit(solution)/shard_map/mix/ppermute | solution.py:425
  32.8 45.5 %collective-permute-start.7 = (f32[24,16,640]{2,1,0:T(8,128)}, f32[24,16,640]{2,1,0:T(8,128)}, u32[]{:S(2)}, u32[]{:S(2)}) collective-permute-start(f32[24,16,640]{2,1,0:T(8,128)} %get-tuple-element.64), channel_id=1, source_target_pairs={{0,1},{1,0},{2,3},{3,2},{4,5},{5,4},{6,7},{7,6},{8,9},{9,8},{10,11... | collective-permute-start | bytes 2949128 | tf_op jit(solution)/shard_map/mix/ppermute | solution.py:425
  43.9 13.3 %copy-start.1 = (f32[16,72,640]{2,1,0:T(8,128)S(1)}, f32[16,72,640]{2,1,0:T(8,128)}, u32[]{:S(2)}) copy-start(f32[16,72,640]{2,1,0:T(8,128)} %get-tuple-element.56.refs_2_) | copy-start | bytes 8847364
  53.1 7.2 %copy-start.29 = (f32[2,8,2,8,640]{4,3,2,1,0:T(8,128)}, f32[2,8,2,8,640]{4,3,2,1,0:T(8,128)S(1)}, u32[]{:S(2)}) copy-start(f32[2,8,2,8,640]{4,3,2,1,0:T(8,128)S(1)} %get-tuple-element.53.refs_0_) | copy-start | bytes 1966084
  60.3 24.7 %collective-permute-start.5 = (f32[10,2,16,640]{3,2,1,0:T(8,128)}, f32[10,2,16,640]{3,2,1,0:T(8,128)}, u32[]{:S(2)}, u32[]{:S(2)}) collective-permute-start(f32[10,2,16,640]{3,2,1,0:T(8,128)} %get-tuple-element.61), channel_id=1, source_target_pairs={{0,2},{2,4},{4,6},{6,8},{8,10},{10,12},{12,14},{14,16},{16,18},{18... | collective-permute-start | bytes 2457608 | tf_op jit(solution)/shard_map/edges/ppermute | solution.py:498
  64.1 20.9 %collective-permute-start.6 = (f32[10,2,16,640]{3,2,1,0:T(8,128)}, f32[10,2,16,640]{3,2,1,0:T(8,128)}, u32[]{:S(2)}, u32[]{:S(2)}) collective-permute-start(f32[10,2,16,640]{3,2,1,0:T(8,128)} %get-tuple-element.62), channel_id=1, source_target_pairs={{2,0},{4,2},{6,4},{8,6},{10,8},{12,10},{14,12},{16,14},{18,16},{20... | collective-permute-start | bytes 2457608 | tf_op jit(solution)/shard_map/edges/ppermute | solution.py:498
  64.1 35.2 %collective-permute-start.1 = (f32[24,16,640]{2,1,0:T(8,128)}, f32[24,16,640]{2,1,0:T(8,128)}, u32[]{:S(2)}, u32[]{:S(2)}) collective-permute-start(f32[24,16,640]{2,1,0:T(8,128)} %get-tuple-element.55), channel_id=1, source_target_pairs={{0,1},{1,0},{2,3},{3,2},{4,5},{5,4},{6,7},{7,6},{8,9},{9,8},{10,11... | collective-permute-start | bytes 2949128 | tf_op jit(solution)/shard_map/mix/ppermute | solution.py:425
  65.4 55.1 %collective-permute-start.11 = (f32[24,16,640]{2,1,0:T(8,128)}, f32[24,16,640]{2,1,0:T(8,128)}, u32[]{:S(2)}, u32[]{:S(2)}) collective-permute-start(f32[24,16,640]{2,1,0:T(8,128)} %get-tuple-element.73), channel_id=1, source_target_pairs={{0,1},{1,0},{2,3},{3,2},{4,5},{5,4},{6,7},{7,6},{8,9},{9,8},{10,11... | collective-permute-start | bytes 2949128 | tf_op jit(solution)/shard_map/mix/ppermute | solution.py:425
  81.2 25.1 %collective-permute-start.12 = (f32[10,2,16,640]{3,2,1,0:T(8,128)S(1)}, f32[10,2,16,640]{3,2,1,0:T(8,128)S(1)}, u32[]{:S(2)}, u32[]{:S(2)}) collective-permute-start(f32[10,2,16,640]{3,2,1,0:T(8,128)S(1)} %get-tuple-element.74), channel_id=1, source_target_pairs={{0,2},{2,4},{4,6},{6,8},{8,10},{10,12},{12,14},{14,16},{16,18},{18... | collective-permute-start | bytes 2457608 | tf_op jit(solution)/shard_map/edges/ppermute | solution.py:498
  85.0 21.2 %collective-permute-start.13 = (f32[10,2,16,640]{3,2,1,0:T(8,128)S(1)}, f32[10,2,16,640]{3,2,1,0:T(8,128)S(1)}, u32[]{:S(2)}, u32[]{:S(2)}) collective-permute-start(f32[10,2,16,640]{3,2,1,0:T(8,128)S(1)} %get-tuple-element.75), channel_id=1, source_target_pairs={{2,0},{4,2},{6,4},{8,6},{10,8},{12,10},{14,12},{16,14},{18,16},{20... | collective-permute-start | bytes 2457608 | tf_op jit(solution)/shard_map/edges/ppermute | solution.py:498
  85.2 14.2 %copy-start.12 = (f32[2,8,2,16,640]{4,3,2,1,0:T(8,128)S(1)}, f32[2,8,2,16,640]{4,3,2,1,0:T(8,128)}, u32[]{:S(2)}) copy-start(f32[2,8,2,16,640]{4,3,2,1,0:T(8,128)} %copy-done.11) | copy-start | bytes 3932164
  99.4 6.9 %copy-start.9 = (f32[2,8,2,16,640]{4,3,2,1,0:T(8,128)S(1)}, f32[2,8,2,16,640]{4,3,2,1,0:T(8,128)}, u32[]{:S(2)}) copy-start(f32[2,8,2,16,640]{4,3,2,1,0:T(8,128)} %copy-done.7) | copy-start | bytes 3932164
  100.9 36.8 %collective-permute-start.8 = (f32[24,8,640]{2,1,0:T(8,128)S(1)}, f32[24,8,640]{2,1,0:T(8,128)S(1)}, u32[]{:S(2)}, u32[]{:S(2)}) collective-permute-start(f32[24,8,640]{2,1,0:T(8,128)S(1)} %get-tuple-element.69), channel_id=1, source_target_pairs={{0,1},{1,0},{2,3},{3,2},{4,5},{5,4},{6,7},{7,6},{8,9},{9,8},{10,11... | collective-permute-start | bytes 1474568 | tf_op jit(solution)/shard_map/ppermute | solution.py:425
  102.2 23.5 %collective-permute-start.9 = (f32[10,2,16,640]{3,2,1,0:T(8,128)S(1)}, f32[10,2,16,640]{3,2,1,0:T(8,128)S(1)}, u32[]{:S(2)}, u32[]{:S(2)}) collective-permute-start(f32[10,2,16,640]{3,2,1,0:T(8,128)S(1)} %get-tuple-element.70), channel_id=1, source_target_pairs={{0,2},{2,4},{4,6},{6,8},{8,10},{10,12},{12,14},{14,16},{16,18},{18... | collective-permute-start | bytes 2457608 | tf_op jit(solution)/shard_map/edges/ppermute | solution.py:498
  106.3 19.9 %collective-permute-start.10 = (f32[10,2,16,640]{3,2,1,0:T(8,128)S(1)}, f32[10,2,16,640]{3,2,1,0:T(8,128)S(1)}, u32[]{:S(2)}, u32[]{:S(2)}) collective-permute-start(f32[10,2,16,640]{3,2,1,0:T(8,128)S(1)} %get-tuple-element.71), channel_id=1, source_target_pairs={{2,0},{4,2},{6,4},{8,6},{10,8},{12,10},{14,12},{16,14},{18,16},{20... | collective-permute-start | bytes 2457608 | tf_op jit(solution)/shard_map/edges/ppermute | solution.py:498
  106.3 14.2 %copy-start.15 = (f32[2,8,2,16,640]{4,3,2,1,0:T(8,128)S(1)}, f32[2,8,2,16,640]{4,3,2,1,0:T(8,128)}, u32[]{:S(2)}) copy-start(f32[2,8,2,16,640]{4,3,2,1,0:T(8,128)} %copy-done.14) | copy-start | bytes 3932164
  121.9 21.9 %collective-permute-start.16 = (f32[10,2,16,640]{3,2,1,0:T(8,128)S(1)}, f32[10,2,16,640]{3,2,1,0:T(8,128)S(1)}, u32[]{:S(2)}, u32[]{:S(2)}) collective-permute-start(f32[10,2,16,640]{3,2,1,0:T(8,128)S(1)} %get-tuple-element.84), channel_id=1, source_target_pairs={{0,2},{2,4},{4,6},{6,8},{8,10},{10,12},{12,14},{14,16},{16,18},{18... | collective-permute-start | bytes 2457608 | tf_op jit(solution)/shard_map/edges/ppermute | solution.py:498
  125.7 24.0 %collective-permute-start.17 = (f32[10,2,16,640]{3,2,1,0:T(8,128)S(1)}, f32[10,2,16,640]{3,2,1,0:T(8,128)S(1)}, u32[]{:S(2)}, u32[]{:S(2)}) collective-permute-start(f32[10,2,16,640]{3,2,1,0:T(8,128)S(1)} %get-tuple-element.85), channel_id=1, source_target_pairs={{2,0},{4,2},{6,4},{8,6},{10,8},{12,10},{14,12},{16,14},{18,16},{20... | collective-permute-start | bytes 2457608 | tf_op jit(solution)/shard_map/edges/ppermute | solution.py:498
  126.2 11.5 %copy-start.30 = (f32[2,8,2,8,640]{4,3,2,1,0:T(8,128)S(1)}, f32[2,8,2,8,640]{4,3,2,1,0:T(8,128)}, u32[]{:S(2)}) copy-start(f32[2,8,2,8,640]{4,3,2,1,0:T(8,128)} %copy-done.29) | copy-start | bytes 1966084
  137.8 23.4 %collective-permute-start.14 = (f32[10,2,8,640]{3,2,1,0:T(8,128)S(1)}, f32[10,2,8,640]{3,2,1,0:T(8,128)S(1)}, u32[]{:S(2)}, u32[]{:S(2)}) collective-permute-start(f32[10,2,8,640]{3,2,1,0:T(8,128)S(1)} %get-tuple-element.82), channel_id=1, source_target_pairs={{0,2},{2,4},{4,6},{6,8},{8,10},{10,12},{12,14},{14,16},{16,18},{18... | collective-permute-start | bytes 1228808 | tf_op jit(solution)/shard_map/edges/ppermute | solution.py:498
  139.2 22.1 %collective-permute-start.15 = (f32[10,2,8,640]{3,2,1,0:T(8,128)S(1)}, f32[10,2,8,640]{3,2,1,0:T(8,128)S(1)}, u32[]{:S(2)}, u32[]{:S(2)}) collective-permute-start(f32[10,2,8,640]{3,2,1,0:T(8,128)S(1)} %get-tuple-element.83), channel_id=1, source_target_pairs={{2,0},{4,2},{6,4},{8,6},{10,8},{12,10},{14,12},{16,14},{18,16},{20... | collective-permute-start | bytes 1228808 | tf_op jit(solution)/shard_map/edges/ppermute | solution.py:498
  (18 other events, 45.8 us)
